TPU v7x, 32 devices: a whole 2x2x4 slice. The times are simulated.
32 devices in a mesh: row: 4 (over y, core), col: 8 (over z, x).
Axes of the slice: x: 2, y: 2, z: 4, core: 2. Of those that a mesh axis runs over, the one named last changes fastest.
Arguments:
- matrix: float32 [4, 4, 256, 2, 8, 256], P(None, 'row', None, None, 'col'), as said below
- vectors: float32 [4, 4, 256, 256], P(None, 'row'), may hold values from -0.09375 to 0.09375
- t_factor: float32 [256, 256], replicated, as said below
Outputs:
- updated: float32 [4, 4, 256, 2, 8, 256], P(None, 'row', None, None, 'col')
Inputs may be any that keep to these rules, and one draw needn't show every extreme that they name: matrix is exactly symmetric as an 4096 x 4096 matrix: entry (i, j) equals entry (j, i). t_factor is upper triangular with its diagonal between 0.5 and 1.5.
All inputs are finite; a program needn't handle non-finite values.
Results may differ from a plain program's by a relative error of at most 0.000068.
Values sent between devices are 32-bit elements; how exact they have to be, the bound alone decides.
No kernel may reach another device: no remote copies, remote signals or barrier semaphores. Data moves between devices by JAX's collectives and lax.ppermute only.
A program may use at most 64 MiB of HBM per device.

v0:
```python
import jax
import jax.numpy as jnp
from jax import lax
from jax.sharding import PartitionSpec as P


def spread(value, axis, root):
    mine = lax.axis_index(axis) == root
    return lax.psum(jnp.where(mine, value, jnp.zeros_like(value)), axis)


def product(left, right):
    return jnp.dot(left, right, precision=lax.Precision.HIGHEST, preferred_element_type=jnp.float32)


def per_device(matrix, vectors, t_factor):
    block_rows = vectors.shape[0]
    block_size = vectors.shape[2]
    block_cols = matrix.shape[3]
    row_devs = lax.axis_size("row")
    col_devs = lax.axis_size("col")
    col_ratio = col_devs // row_devs
    row_pos = lax.axis_index("row")
    col_pos = lax.axis_index("col")
    top_block = vectors[0, 0]
    unit_top = jnp.tril(top_block, -1) + jnp.eye(block_size, dtype=jnp.float32)
    first_block = jnp.where(row_pos == 0, unit_top, top_block)
    blocks = jnp.concatenate([first_block[None], vectors[1:, 0]], axis=0)
    chosen_ids = col_ratio * jnp.arange(block_cols, dtype=jnp.int32) + col_pos // row_devs
    source_row = col_pos % row_devs
    chosen = jnp.take(blocks, chosen_ids, axis=0)
    col_vecs = spread(chosen, "row", source_row).reshape(block_cols * block_size, block_size)
    row_vecs = blocks.reshape(block_rows * block_size, block_size)
    local_tile = matrix.reshape(block_rows * block_size, block_cols * block_size)
    summed = lax.psum(product(local_tile, col_vecs), "col")
    applied = product(summed, t_factor)
    inner = lax.psum(product(row_vecs.T, applied), "row")
    middle = product(t_factor.T, inner)
    coupled_rows = applied - 0.5 * product(row_vecs, middle)
    mirrored = lax.psum(product(local_tile.T, row_vecs), "row")
    coupled_cols = product(mirrored, t_factor) - 0.5 * product(col_vecs, middle)
    result = local_tile - product(row_vecs, coupled_cols.T) - product(coupled_rows, col_vecs.T)
    return result.reshape(matrix.shape)


def solution(mesh):
    in_specs = (P(None, "row", None, None, "col", None), P(None, "row", None, None), P())
    out_specs = P(None, "row", None, None, "col", None)
    return jax.shard_map(
        per_device, mesh=mesh, in_specs=in_specs, out_specs=out_specs, check_vma=False
    )
```

profile of v0, /device:TPU:0, one launch (start us, length us, event | category | flops | bytes accessed | tf_op | source)
XLA Modules:
  0.0 195.0 jit_solution(11677775799956465152)
XLA Ops:
  6.5 0.0 copy-start
  6.5 0.0 all-reduce.5.cloned.1.call-start
  6.6 1.2 slice_bitcast_fusion
  7.8 1.1 bitcast_select_fusion
  8.9 0.0 copy-start.4
  8.9 0.1 pad_maximum_fusion
  9.0 1.4 gather_fusion
  10.4 2.0 %select_select_fusion = f32[2,256,256]{2,1,0:T(8,128)} fusion(f32[2,256,256]{2,1,0:T(8,128)} %gather_fusion, pred[2]{0:T(512)(128)(4,1)S(1)} %compare_and_fusion, pred[]{:T(512)S(6)} %eq.20), kind=kLoop, calls=%fused_computation.10 | loop fusion | flops 262144 | bytes 1048579 | tf_op jit(solution)/shard_map/jit(_where)/select_n | solution.py:9
  12.3 0.0 all-reduce.5.cloned.1.call-update
  12.3 0.0 all-reduce.7.cloned.1.call-start
  12.4 0.0 copy-done.4
  12.4 8.1 %reduce = f32[4,256,2,256]{3,2,1,0:T(2,128)} reduce(f32[4,1,256,2,1,256]{5,4,3,2,1,0:T(1,128)S(1)} %copy-done.4, f32[]{:T(128)} %constant.60), dimensions={1,4}, to_apply=%param.3.reduce_sub_computation | reduce | bytes 4194308 | tf_op args[0]
  20.5 1.8 copy.5
  22.2 26.2 %all-reduce.5.cloned.1.call-done = f32[512,256]{1,0:T(8,128)} async-done(((f32[512,256]{1,0:T(8,128)}), f32[512,256]{1,0:T(8,128)}) %all-reduce.5.cloned.1.call-update) | async-done | bytes 524304 | tf_op jit(solution)/shard_map/psum | solution.py:9
  48.4 5.5 %convolution_bitcast_fusion = f32[1024,256]{0,1:T(8,128)} fusion(f32[512,256]{1,0:T(8,128)} %all-reduce.5.cloned.1.call-done, f32[1024,512]{1,0:T(8,128)S(1)} %bitcast.40), kind=kOutput, calls=%fused_computation.2 | convolution fusion | flops 1610612736 | bytes 3670016 | tf_op jit(solution)/shard_map/dot_general | solution.py:13
  53.9 0.0 all-reduce.7.cloned.1.call-update
  53.9 0.2 all-reduce.9.cloned.1.call-start
  54.2 2.7 %convolution_bitcast_fusion.1 = f32[512,256]{0,1:T(8,128)} fusion(f32[1024,256]{1,0:T(8,128)S(1)} %bitcast.43, f32[1024,512]{1,0:T(8,128)S(1)} %bitcast.41), kind=kOutput, calls=%fused_computation.5 | convolution fusion | flops 1610612736 | bytes 3670016 | tf_op jit(solution)/shard_map/dot_general | solution.py:13
  56.9 75.2 %all-reduce.7.cloned.1.call-done = f32[1024,256]{0,1:T(8,128)} async-done(((f32[1024,256]{0,1:T(8,128)}), f32[1024,256]{0,1:T(8,128)}) %all-reduce.7.cloned.1.call-update) | async-done | bytes 1048592 | tf_op jit(solution)/shard_map/psum | solution.py:35
  132.1 0.0 copy-done
  132.1 3.0 %fusion.5 = f32[1024,256]{1,0:T(8,128)S(1)} fusion(f32[1024,256]{0,1:T(8,128)} %all-reduce.7.cloned.1.call-done, f32[256,256]{1,0:T(8,128)S(1)} %copy-done), kind=kOutput, calls=%fused_computation.23 | convolution fusion | flops 805306368 | bytes 2359296 | tf_op jit(solution)/shard_map/dot_general | solution.py:13
  135.1 0.0 copy-start.1
  135.1 1.0 copy-done.1
  136.1 2.5 %fusion.6 = f32[256,256]{1,0:T(8,128)} fusion(f32[1024,256]{1,0:T(8,128)S(1)} %bitcast.44, f32[1024,256]{1,0:T(8,128)S(1)} %fusion.5), kind=kOutput, calls=%fused_computation.24 | convolution fusion | flops 805306368 | bytes 2359296 | tf_op jit(solution)/shard_map/dot_general | solution.py:13
  138.6 0.0 all-reduce.9.cloned.1.call-update
  138.6 34.4 %all-reduce.9.cloned.1.call-done = (f32[512,256]{0,1:T(8,128)}, f32[256,256]{1,0:T(8,128)}) async-done(((f32[512,256]{0,1:T(8,128)}, f32[256,256]{1,0:T(8,128)}), (f32[512,256]{0,1:T(8,128)}, f32[256,256]{1,0:T(8,128)})) %all-reduce.9.cloned.1.call-update) | async-done | bytes 786448 | tf_op jit(solution)/shard_map/psum | solution.py:40
  173.0 0.0 copy-start.2
  173.0 2.1 %fusion.4 = f32[512,256]{1,0:T(8,128)S(1)} fusion(f32[512,256]{0,1:T(8,128)} %get-tuple-element.5, f32[256,256]{1,0:T(8,128)S(1)} %copy-done), kind=kOutput, calls=%fused_computation.22 | convolution fusion | flops 402653184 | bytes 1310720 | tf_op jit(solution)/shard_map/dot_general | solution.py:13
  175.2 0.0 copy-start.3
  175.2 1.6 fusion.7
  176.8 0.0 copy-done.2
  176.8 1.0 fusion
  177.8 0.0 copy-done.3
  177.9 0.6 fusion.1
  178.5 1.9 fusion.8
  180.3 3.4 %subtract_subtract_fusion = f32[1024,512]{1,0:T(8,128)} fusion(f32[1024,512]{1,0:T(8,128)S(1)} %bitcast.42, f32[1024,512]{1,0:T(8,128)S(1)} %fusion.8, f32[1024,256]{1,0:T(8,128)S(1)} %fusion, f32[512,256]{1,0:T(8,128)S(1)} %copy-done.3), kind=kOutput, calls=%fused_computation.1 | convolution fusion | flops 1611661312 | bytes 7864320 | tf_op jit(solution)/shard_map/dot_general | solution.py:13
  183.7 4.7 %reshape.108 = f32[4,1,256,2,1,256]{5,4,3,2,1,0:T(1,128)} reshape(f32[1024,512]{1,0:T(8,128)} %subtract_subtract_fusion) | data formatting | bytes 4194304 | tf_op jit(solution)/shard_map/reshape | solution.py:43
  (4 shorter events, 0.0 us)
Async XLA Ops:
  6.5 125.5 %copy-start = (f32[256,256]{1,0:T(8,128)S(1)}, f32[256,256]{1,0:T(8,128)}, u32[]{:S(2)}) copy-start(f32[256,256]{1,0:T(8,128)} %param.5) | copy-start | bytes 786436
  6.5 41.9 %all-reduce.5.cloned.1.call-start = ((), (), s32[]{:S(2)}) async-start(), calls=%async_computation | async-start | bytes 1048576 | tf_op jit(solution)/shard_map/psum | solution.py:9
  8.9 3.5 %copy-start.4 = (f32[4,1,256,2,1,256]{5,4,3,2,1,0:T(1,128)S(1)}, f32[4,1,256,2,1,256]{5,4,3,2,1,0:T(1,128)}, u32[]{:S(2)}) copy-start(f32[4,1,256,2,1,256]{5,4,3,2,1,0:T(1,128)} %param.3) | copy-start | bytes 6291460
  12.3 119.7 %all-reduce.7.cloned.1.call-start = ((), (), s32[]{:S(2)}) async-start(), calls=%async_computation.1 | async-start | bytes 2097152 | tf_op jit(solution)/shard_map/psum | solution.py:35
  53.9 119.1 %all-reduce.9.cloned.1.call-start = ((), (), s32[]{:S(2)}) async-start(), calls=%async_computation.2 | async-start | bytes 1572864 | tf_op jit(solution)/shard_map/psum | solution.py:40
  135.1 1.0 copy-start.1
  173.0 3.8 %copy-start.2 = (f32[1024,256]{1,0:T(8,128)S(1)}, f32[1024,256]{1,0:T(8,128)}, u32[]{:S(2)}) copy-start(f32[1024,256]{1,0:T(8,128)} %copy-done.1) | copy-start | bytes 3145732
  175.2 2.7 %copy-start.3 = (f32[512,256]{1,0:T(8,128)S(1)}, f32[512,256]{1,0:T(8,128)}, u32[]{:S(2)}) copy-start(f32[512,256]{1,0:T(8,128)} %all-reduce.5.cloned.1.call-done) | copy-start | bytes 1572868
Sparse Core Ops, SparseCore 0:
  12.5 35.8 all-reduce.4
  54.1 77.9 all-reduce.6
  138.8 34.2 all-reduce.8
where the time goes:
time: 195 us
  waiting for transfers between devices  136 us (70%)
  matrix products  24.4 us (13%)
  between operations  13.3 us (7%)
  other arithmetic  11.2 us (6%)
  local copies, waits for them, and re-layouts  10.1 us (5%)
    psum x1, waiting for transfers between devices, per_device(): summed = lax.psum(product(local_tile, col_vecs), 'col')  75.2 us
    psum x1, waiting for transfers between devices, per_device(): mirrored = lax.psum(product(local_tile.T, row_vecs), 'row')  34.4 us
    psum x1, waiting for transfers between devices, spread(): return lax.psum(jnp.where(mine, value, jnp.zeros_like(value)), axis)  26.2 us
    dot_general x10, matrix products, product(): jnp.dot(left, right, precision=lax.Precision.HIGHEST, preferred_element_t...  24.4 us
    unnamed x1, other arithmetic  8.06 us
    reshape x1, local copies, waits for them, and re-layouts, per_device(): return result.reshape(matrix.shape)  4.7 us
  transfers between devices with their start and end apart: 3, of which 3 were waited for; matrix products, arithmetic and copies ran while one was open for 6% of the time, Pallas kernels for 0%

commit v1 on v0

v1 whole, which is shorter than its diff:
```python
import functools

import jax
import jax.numpy as jnp
from jax import lax
from jax.experimental import pallas as pl
from jax.experimental.pallas import tpu as pltpu
from jax.sharding import PartitionSpec as P

AXES = ("row", "col")
F32, BF16 = jnp.float32, jnp.bfloat16
NN, NT, TN = ((1,), (0,)), ((1,), (1,)), ((0,), (0,))
LANES = 128
VMEM = pl.BlockSpec(memory_space=pltpu.VMEM)
HBM = pl.BlockSpec(memory_space=pltpu.HBM)


def split(value):
    high = value.astype(BF16)
    return high, (value - high.astype(F32)).astype(BF16)


def product(left, right, dims):
    def one(a, b):
        return lax.dot_general(a, b, (dims, ((), ())), preferred_element_type=F32)

    (lh, ll), (rh, rl) = left, right
    return one(lh, rh) + (one(lh, rl) + one(ll, rh))


def sds(*shape, dtype=F32):
    return jax.ShapeDtypeStruct(shape, dtype)


def call(kernel, outs, *args, specs=None, scratch=(), limit=32, flops=0):
    return pl.pallas_call(
        kernel,
        out_shape=outs,
        in_specs=specs or [VMEM] * len(args),
        out_specs=jax.tree.map(lambda _: VMEM, outs),
        scratch_shapes=list(scratch),
        compiler_params=pltpu.CompilerParams(vmem_limit_bytes=limit << 20),
        cost_estimate=pl.CostEstimate(flops=flops, bytes_accessed=1 << 20, transcendentals=0),
    )(*args)


def send(value, rows, cols, target):
    pairs = []
    for row in range(rows):
        for col in range(cols):
            to = target(row, col)
            if to is not None:
                pairs.append((row * cols + col, to[0] * cols + to[1]))
    return lax.ppermute(value, AXES, pairs)


def with_unit_top(block):
    size = block.shape[0]
    i = lax.broadcasted_iota(jnp.int32, (size, size), 0)
    j = lax.broadcasted_iota(jnp.int32, (size, size), 1)
    unit = jnp.where(i > j, block, jnp.where(i == j, 1.0, 0.0))
    return jnp.where(lax.axis_index("row") == 0, unit, block)


def tile_rows(ref, start, count, width, first, lanes):
    step = width // LANES
    return jnp.concatenate(
        [ref[pl.ds(start * step + first + k, count, stride=step), :] for k in range(lanes // LANES)], axis=1
    )


def sums_kernel(rows, cols, width, a_hbm, v_hbm, keep, give, own, a_buf, v_buf, a_sem, v_sem):
    nb = v_buf.shape[1]
    count, step, ratio = v_buf.shape[0], width // LANES, cols // rows
    core = lax.axis_index("row") % 2
    hi = lax.axis_index("col") // rows
    copies = []
    for b in range(count):
        v_copy = pltpu.make_async_copy(v_hbm.at[pl.ds(b * nb, nb)], v_buf.at[b], v_sem.at[b])
        a_copy = pltpu.make_async_copy(a_hbm.at[pl.ds(b * nb * step, nb * step)], a_buf.at[b], a_sem.at[b])
        v_copy.start()
        a_copy.start()
        copies.append((v_copy, a_copy))
    for b in range(count):
        copies[b][0].wait()
        block = v_buf[b]
        if b == 0:
            block = with_unit_top(block)

        @pl.when(hi == b % ratio)
        def _():
            own[pl.ds(b // ratio * nb, nb), :] = block

        right = split(block)
        copies[b][1].wait()
        for out, half in ((give, 1 - core), (keep, core)):
            left = split(tile_rows(a_buf.at[b], 0, nb, width, half * (nb // LANES), nb))
            value = product(left, right, TN)
            out[...] = value if b == 0 else out[...] + value


def chip_kernel(keep, came, chip, *parts):
    y = lax.axis_index("row") // 2
    chip[...] = keep[...] + came[...]
    piece = parts[0].shape[0]
    for s, part in enumerate(parts):
        part[...] = chip[pl.ds((y ^ s) * piece, piece), :]


def cols_kernel(near, over, t_ref, vecs, high, low):
    same = lax.axis_index("row") % 2 == lax.axis_index("col") % 2

    @pl.when(same)
    def _():
        vecs[...] = near[...]

    @pl.when(jnp.logical_not(same))
    def _():
        vecs[...] = over[...]

    high[...], low[...] = split(product(split(vecs[...]), split(t_ref[...]), NT))


def rows_kernel(v_ref, t_ref, high, low):
    nb = t_ref.shape[0]
    right = split(t_ref[...])
    for b in range(v_ref.shape[0] // nb):
        at = pl.ds(b * nb, nb)
        block = v_ref[at, :]
        if b == 0:
            block = with_unit_top(block)
        high[at, :], low[at, :] = split(product(split(block), right, NT))


def inner_kernel(mine, other, vecs, out, whole):
    half, count = mine.shape[0], out.shape[0]
    row = lax.axis_index("row")
    core = row % 2
    whole[...] = product(split(vecs[pl.ds(core * half, half), :]), split(mine[...]), TN) + product(
        split(vecs[pl.ds((1 - core) * half, half), :]), split(other[...]), TN
    )
    out[...] = whole[pl.ds(row * count, count), :]


def first_kernel(flip, pieces, nb, a_ref, u_high, u_low, *refs):
    *arrays, out, p_high, p_low = refs
    col = lax.axis_index("col")
    z, h = col // 2, (col % 2) ^ flip
    width, count = out.shape[1], out.shape[0]
    for array, at, s, piece in pieces:
        to = pl.ds((z ^ s) * piece, piece)
        p_high[to, :], p_low[to, :] = split(arrays[array][pl.ds(at, piece), :])
    right = u_high[...], u_low[...]
    for b in range(count // nb):
        at = pl.ds(b * nb, nb)
        value = product((p_high[at, :], p_low[at, :]), right, NT)
        out[at, :] = tile_rows(a_ref, h * count + b * nb, nb, width, 0, width) - value


def last_kernel(ys, nb, one, two, v_high, v_low, u_high, u_low, p_mine, p_other, *refs):
    *inners, out, inner, mixed, buf, sem = refs
    row, x = lax.axis_index("row"), lax.axis_index("col") % 2
    y, core = row // 2, row % 2
    count = inners[0].shape[0]
    for s in range(ys):
        inner[pl.ds(((y ^ s) * 2 + core) * count, count), :] = inners[s][...]
        inner[pl.ds(((y ^ s) * 2 + 1 - core) * count, count), :] = inners[ys][pl.ds(s * count, count), :]
    mixed[...] = product((u_high[...], u_low[...]), split(inner[...]), NT)
    half = p_mine.shape[0]
    for ref, c in ((p_mine, core), (p_other, 1 - core)):
        at = pl.ds(c * half, half)
        mixed[at, :] = mixed[at, :] - ref[...]
    right = split(mixed[...])
    width = one.shape[1]
    step = width // LANES
    blocks = one.shape[0] // nb
    copies = []
    for u, base in enumerate((one, two)):
        for b in range(blocks):
            at = (x ^ u) * blocks + b
            rows = pl.ds(at * nb, nb)
            value = base[pl.ds(b * nb, nb), :] + product((v_high[rows, :], v_low[rows, :]), right, NT)
            slot = u * blocks + b
            for k in range(step):
                buf[slot, pl.ds(k, nb, stride=step), :] = value[:, k * LANES : (k + 1) * LANES]
            copy = pltpu.make_async_copy(buf.at[slot], out.at[pl.ds(at * nb * step, nb * step)], sem.at[slot])
            copy.start()
            copies.append(copy)
    for copy in copies:
        copy.wait()


def per_device(matrix, vectors, t_factor):
    block_rows, _, nb, _ = vectors.shape
    width = matrix.shape[3] * nb
    rows, cols = lax.axis_size("row"), lax.axis_size("col")
    ratio, ys, zs = cols // rows, rows // 2, cols // 2
    row, col = lax.axis_index("row"), lax.axis_index("col")
    height, half, piece, share = block_rows * nb, width // 2, width // rows, nb // rows
    assert half == nb and block_rows == 2 * ratio
    step = width // LANES
    linear = matrix.reshape(height * step, LANES)
    vecs = vectors.reshape(height, nb)

    def move(value, target):
        return send(value, rows, cols, target)

    def other_core(r, c):
        return r ^ 1, c

    keep, give, own = call(
        functools.partial(sums_kernel, rows, cols, width),
        (sds(half, nb), sds(half, nb), sds(width, nb)),
        linear,
        vecs,
        specs=[HBM, HBM],
        scratch=[
            pltpu.VMEM((block_rows, nb * step, LANES), F32),
            pltpu.VMEM((block_rows, nb, nb), F32),
            pltpu.SemaphoreType.DMA((block_rows,)),
            pltpu.SemaphoreType.DMA((block_rows,)),
        ],
        limit=60,
    )
    chip, *parts = call(
        chip_kernel, [sds(half, nb)] + [sds(piece, nb)] * ys, keep, move(give, other_core)
    )

    shard = sum(
        move(part, lambda r, c, s=s: (c % rows, (c // rows) * rows + ((r // 2) ^ s) * 2 + r % 2))
        for s, part in enumerate(parts)
    )

    came = sum(move(own, lambda r, c, s=s: (r ^ (2 * s), c) if r == c % rows else None) for s in range(1, ys))
    near = jnp.where(row == col % rows, own, came)
    over = move(near, lambda r, c: other_core(r, c) if r % 2 == c % 2 else None)
    col_vecs, u_high, u_low = call(
        cols_kernel,
        (sds(width, nb), sds(width, nb, dtype=BF16), sds(width, nb, dtype=BF16)),
        near,
        over,
        t_factor,
    )
    v_high, v_low = call(
        rows_kernel, (sds(height, nb, dtype=BF16), sds(height, nb, dtype=BF16)), vecs, t_factor
    )

    mine = chip + sum(move(chip, lambda r, c, s=s: (r ^ (2 * s), c)) for s in range(1, ys))
    other = move(mine, other_core)

    inner = call(inner_kernel, sds(share, nb), mine, other, col_vecs, scratch=[pltpu.VMEM((nb, nb), F32)])
    inner = inner + sum(move(inner, lambda r, c, s=s: (r, c ^ (2 * s))) for s in range(1, zs))
    inner = inner + move(inner, lambda r, c: (r, c ^ 1))
    inners = [inner] + [move(inner, lambda r, c, s=s: (r ^ (2 * s), c)) for s in range(1, ys)]
    inners.append(move(jnp.concatenate(inners, axis=0), other_core))

    along = [shard] + [move(shard, lambda r, c, s=s: (r, c ^ (2 * s))) for s in range(1, zs)]
    early = move(jnp.concatenate(along[: zs // 2], axis=0), lambda r, c: (r, c ^ 1))
    late = move(jnp.concatenate(along[zs // 2 :], axis=0), lambda r, c: (r, c ^ 1))

    def first(flip, pieces, arrays):
        return call(
            functools.partial(first_kernel, flip, pieces, nb),
            sds(height // 2, width),
            linear,
            u_high,
            u_low,
            *arrays,
            scratch=[pltpu.VMEM((height // 2, nb), BF16)] * 2,
        )

    one = first(0, [(s, 0, s, piece) for s in range(zs)], along)
    two = first(1, [(2 * s // zs, s % (zs // 2) * piece, s, piece) for s in range(zs)], [early, late])

    result = pl.pallas_call(
        functools.partial(last_kernel, ys, nb),
        out_shape=sds(height * step, LANES),
        in_specs=[VMEM] * (8 + ys + 1),
        out_specs=HBM,
        scratch_shapes=[
            pltpu.VMEM((nb, nb), F32),
            pltpu.VMEM((width, nb), F32),
            pltpu.VMEM((block_rows, nb * step, LANES), F32),
            pltpu.SemaphoreType.DMA((block_rows,)),
        ],
        compiler_params=pltpu.CompilerParams(vmem_limit_bytes=32 << 20),
    )(one, two, v_high, v_low, u_high, u_low, mine, other, *inners)
    return result.reshape(matrix.shape)


def solution(mesh):
    in_specs = (P(None, "row", None, None, "col", None), P(None, "row", None, None), P())
    out_specs = P(None, "row", None, None, "col", None)
    return jax.shard_map(
        per_device, mesh=mesh, in_specs=in_specs, out_specs=out_specs, check_vma=False
    )
```

time: 195 us -> 71.3 us (0.37)
  waiting for transfers between devices: 136 us -> 29.7 us
  starting transfers between devices: 0.27 us -> 29.5 us
  matrix products: 24.4 us -> 0 us
  between operations: 13.3 us -> 0.23 us
  other arithmetic: 11.2 us -> 1.23 us
  Pallas kernels: 0 us -> 9.41 us
  local copies, waits for them, and re-layouts: 10.1 us -> 0.97 us
    psum x3 -> x0, waiting for transfers between devices: 136 us -> none  [the longest x1 75.2 us: per_device(): summed = lax.psum(product(local_tile, col_vecs), 'col')]
    ppermute x0 -> x18, waiting for transfers between devices: none -> 29.7 us  [send(): return lax.ppermute(value, AXES, pairs)]
    ppermute x0 -> x18, starting transfers between devices: none -> 29.5 us  [send(): return lax.ppermute(value, AXES, pairs)]
    dot_general x10 -> x0, matrix products: 24.4 us -> none  [product(): jnp.dot(left, right, precision=lax.Precision.HIGHEST, preferred_element_t...]
    pallas_call x0 -> x8, Pallas kernels: none -> 9.41 us  [the longest x7 6.51 us: call(): pl.pallas_call(kernel, out_shape=outs, in_specs=specs or [VMEM] * len(arg...]
    unnamed x1 -> x0, other arithmetic: 8.06 us -> none
    reshape x1 -> x0, local copies, waits for them, and re-layouts: 4.7 us -> none  [per_device(): return result.reshape(matrix.shape)]
  transfers between devices with their start and end apart: 3 -> 18, of which waited for: 3 -> 8; matrix products, arithmetic and copies ran while one was open for 6% -> 0% of each run, Pallas kernels for 0% -> 4%
where the time goes in v1:
time: 71.3 us; the launch traced here: 71 us
  waiting for transfers between devices  29.7 us (42%)
  starting transfers between devices  29.5 us (41%)
  Pallas kernels  9.41 us (13%)
  other arithmetic  1.23 us (2%)
  local copies, waits for them, and re-layouts  0.97 us (1%)
    ppermute x18, waiting for transfers between devices, send(): return lax.ppermute(value, AXES, pairs)  29.7 us
    ppermute x18, starting transfers between devices, send(): return lax.ppermute(value, AXES, pairs)  29.5 us
    pallas_call x7, Pallas kernels, call(): pl.pallas_call(kernel, out_shape=outs, in_specs=specs or [VMEM] * len(arg...  6.51 us
    pallas_call x1, Pallas kernels, per_device(): pl.pallas_call(functools.partial(last_kernel, ys, nb), out_shape=sds(heig...  2.89 us
  transfers between devices with their start and end apart: 18, of which 8 were waited for; matrix products, arithmetic and copies ran while one was open for 0% of the time, Pallas kernels for 4%

profile of v1, /device:TPU:0, one launch (start us, length us, event | category | flops | bytes accessed | tf_op | source)
XLA Modules:
  0.0 71.0 jit_solution(5892869933435913184)
XLA Ops:
  0.0 3.6 %shard_map.37 = (f32[256,256]{1,0:T(8,128)}, f32[256,256]{1,0:T(8,128)}, f32[512,256]{1,0:T(8,128)}) custom-call(f32[4096,128]{1,0:T(8,128)} %bitcast.3, f32[1024,256]{1,0:T(8,128)} %bitcast.6), custom_call_target="tpu_custom_call" | custom-call | bytes 1048576 | tf_op jit(solution)/shard_map/pallas_call | solution.py:36
  3.7 0.0 copy-start.2
  3.7 5.0 %collective-permute-start = (f32[512,256]{1,0:T(8,128)}, f32[512,256]{1,0:T(8,128)S(1)}, u32[]{:S(2)}, u32[]{:S(2)}) collective-permute-start(f32[512,256]{1,0:T(8,128)} %get-tuple-element.16), channel_id=1, source_target_pairs={{0,16},{4,20},{9,25},{13,29},{18,2},{22,6},{27,11},{31,15}} | collective-permute-start | bytes 1572872 | tf_op jit(solution)/shard_map/ppermute | solution.py:54
  8.7 0.1 collective-permute-start.2
  8.8 1.7 %collective-permute-done.2.came = f32[256,256]{1,0:T(8,128)S(1)} collective-permute-done((f32[256,256]{1,0:T(8,128)}, f32[256,256]{1,0:T(8,128)S(1)}, u32[]{:S(2)}, u32[]{:S(2)}) %collective-permute-start.2) | collective-permute-done | bytes 262176 | tf_op jit(solution)/shard_map/ppermute | solution.py:54
  10.5 0.9 %copy-done.3 = f32[256,256]{1,0:T(8,128)S(1)} copy-done((f32[256,256]{1,0:T(8,128)S(1)}, f32[256,256]{1,0:T(8,128)}, u32[]{:S(2)}) %copy-start.3) | copy-done | bytes 262168
  11.5 6.1 %collective-permute-done = f32[512,256]{1,0:T(8,128)S(1)} collective-permute-done((f32[512,256]{1,0:T(8,128)}, f32[512,256]{1,0:T(8,128)S(1)}, u32[]{:S(2)}, u32[]{:S(2)}) %collective-permute-start) | collective-permute-done | bytes 524320 | tf_op jit(solution)/shard_map/ppermute | solution.py:54
  17.7 1.1 %broadcast_select_fusion.near = f32[512,256]{1,0:T(8,128)S(1)} fusion(f32[512,256]{1,0:T(8,128)} %get-tuple-element.16, f32[512,256]{1,0:T(8,128)S(1)} %collective-permute-done, pred[]{:T(512)S(6)} %eq.5), kind=kLoop, calls=%fused_computation.2 | loop fusion | flops 131072 | bytes 1572865 | tf_op jit(solution)/shard_map/jit(_where)/select_n | solution.py:235
  18.8 1.3 %collective-permute-start.1 = (f32[512,256]{1,0:T(8,128)S(1)}, f32[512,256]{1,0:T(8,128)S(1)}, u32[]{:S(2)}, u32[]{:S(2)}) collective-permute-start(f32[512,256]{1,0:T(8,128)S(1)} %broadcast_select_fusion.near), channel_id=1, source_target_pairs={{0,8},{2,10},{4,12},{6,14},{9,1},{11,3},{13,5},{15,7},{16,24},{18,... | collective-permute-start | bytes 1572872 | tf_op jit(solution)/shard_map/ppermute | solution.py:54
  20.1 1.4 %collective-permute-start.10 = (f32[256,256]{1,0:T(8,128)S(1)}, f32[256,256]{1,0:T(8,128)S(1)}, u32[]{:S(2)}, u32[]{:S(2)}) collective-permute-start(f32[256,256]{1,0:T(8,128)S(1)} %get-tuple-element.25), channel_id=1, source_target_pairs={{0,16},{1,17},{2,18},{3,19},{4,20},{5,21},{6,22},{7,23},{8,24},{9,... | collective-permute-start | bytes 786440 | tf_op jit(solution)/shard_map/ppermute | solution.py:54
  21.5 5.0 %collective-permute-done.10 = f32[256,256]{1,0:T(8,128)S(1)} collective-permute-done((f32[256,256]{1,0:T(8,128)S(1)}, f32[256,256]{1,0:T(8,128)S(1)}, u32[]{:S(2)}, u32[]{:S(2)}) %collective-permute-start.10) | collective-permute-done | bytes 262176 | tf_op jit(solution)/shard_map/ppermute | solution.py:54
  26.6 0.1 collective-permute-start.11
  26.7 0.7 collective-permute-start.3
  27.3 0.0 copy-start.1
  27.3 4.1 %collective-permute-start.4 = (f32[128,256]{1,0:T(8,128)S(1)}, f32[128,256]{1,0:T(8,128)S(1)}, u32[]{:S(2)}, u32[]{:S(2)}) collective-permute-start(f32[128,256]{1,0:T(8,128)S(1)} %get-tuple-element.22), channel_id=1, source_target_pairs={{0,2},{1,10},{2,18},{3,26},{4,6},{5,14},{6,22},{7,30},{8,3},{9,11}... | collective-permute-start | bytes 393224 | tf_op jit(solution)/shard_map/ppermute | solution.py:54
  31.4 0.0 collective-permute-done.1.over
  31.4 0.5 shard_map.38
  31.9 0.0 collective-permute-done.11.other.p_other
  31.9 0.0 copy-start
  31.9 0.5 shard_map.43
  32.4 2.1 %collective-permute-start.14 = (f32[64,256]{1,0:T(8,128)S(1)}, f32[64,256]{1,0:T(8,128)S(1)}, u32[]{:S(2)}, u32[]{:S(2)}) collective-permute-start(f32[64,256]{1,0:T(8,128)S(1)} %shard_map.43), channel_id=1, source_target_pairs={{0,6},{1,7},{2,4},{3,5},{4,2},{5,3},{6,0},{7,1},{8,14},{9,15},{10,... | collective-permute-start | bytes 196616 | tf_op jit(solution)/shard_map/ppermute | solution.py:54
  34.5 0.6 collective-permute-start.13
  35.1 1.7 %collective-permute-start.12 = (f32[64,256]{1,0:T(8,128)S(1)}, f32[64,256]{1,0:T(8,128)S(1)}, u32[]{:S(2)}, u32[]{:S(2)}) collective-permute-start(f32[64,256]{1,0:T(8,128)S(1)} %shard_map.43), channel_id=1, source_target_pairs={{0,2},{1,3},{2,0},{3,1},{4,6},{5,7},{6,4},{7,5},{8,10},{9,11},{10,... | collective-permute-start | bytes 196616 | tf_op jit(solution)/shard_map/ppermute | solution.py:54
  36.8 0.0 collective-permute-done.3
  36.8 0.0 collective-permute-done.4
  36.9 2.7 %collective-permute-start.7 = (f32[128,256]{1,0:T(8,128)S(1)}, f32[128,256]{1,0:T(8,128)S(1)}, u32[]{:S(2)}, u32[]{:S(2)}) collective-permute-start(f32[128,256]{1,0:T(8,128)S(1)} %add.23.refs_0_), channel_id=1, source_target_pairs={{0,6},{1,7},{2,4},{3,5},{4,2},{5,3},{6,0},{7,1},{8,14},{9,15},{10,... | collective-permute-start | bytes 393224 | tf_op jit(solution)/shard_map/ppermute | solution.py:54
  39.6 0.0 collective-permute-start.6
  39.6 0.0 collective-permute-done.14
  39.6 1.7 %collective-permute-start.5 = (f32[128,256]{1,0:T(8,128)S(1)}, f32[128,256]{1,0:T(8,128)S(1)}, u32[]{:S(2)}, u32[]{:S(2)}) collective-permute-start(f32[128,256]{1,0:T(8,128)S(1)} %add.23.refs_0_), channel_id=1, source_target_pairs={{0,2},{1,3},{2,0},{3,1},{4,6},{5,7},{6,4},{7,5},{8,10},{9,11},{10,... | collective-permute-start | bytes 393224 | tf_op jit(solution)/shard_map/ppermute | solution.py:54
  41.3 1.0 %collective-permute-done.13 = f32[64,256]{1,0:T(8,128)S(1)} collective-permute-done((f32[64,256]{1,0:T(8,128)S(1)}, f32[64,256]{1,0:T(8,128)S(1)}, u32[]{:S(2)}, u32[]{:S(2)}) %collective-permute-start.13) | collective-permute-done | bytes 65568 | tf_op jit(solution)/shard_map/ppermute | solution.py:54
  42.3 0.0 collective-permute-done.12
  42.4 3.8 %collective-permute-start.15 = (f32[64,256]{1,0:T(8,128)S(1)}, f32[64,256]{1,0:T(8,128)S(1)}, u32[]{:S(2)}, u32[]{:S(2)}) collective-permute-start(f32[64,256]{1,0:T(8,128)S(1)} %add_add_fusion), channel_id=1, source_target_pairs={{0,1},{1,0},{2,3},{3,2},{4,5},{5,4},{6,7},{7,6},{8,9},{9,8},{10,11... | collective-permute-start | bytes 196616 | tf_op jit(solution)/shard_map/ppermute | solution.py:54
  46.1 0.0 collective-permute-done.7.refs_3_
  46.1 7.3 %collective-permute-done.6.refs_2_ = f32[128,256]{1,0:T(8,128)S(1)} collective-permute-done((f32[128,256]{1,0:T(8,128)S(1)}, f32[128,256]{1,0:T(8,128)S(1)}, u32[]{:S(2)}, u32[]{:S(2)}) %collective-permute-start.6) | collective-permute-done | bytes 131104 | tf_op jit(solution)/shard_map/ppermute | solution.py:54
  53.4 0.1 collective-permute-start.9
  53.5 0.0 collective-permute-done.15
  53.5 2.0 %collective-permute-start.16 = (f32[64,256]{1,0:T(8,128)S(1)}, f32[64,256]{1,0:T(8,128)S(1)}, u32[]{:S(2)}, u32[]{:S(2)}) collective-permute-start(f32[64,256]{1,0:T(8,128)S(1)} %add.28.refs_0_), channel_id=1, source_target_pairs={{0,16},{1,17},{2,18},{3,19},{4,20},{5,21},{6,22},{7,23},{8,24},{9,... | collective-permute-start | bytes 196616 | tf_op jit(solution)/shard_map/ppermute | solution.py:54
  55.5 0.0 collective-permute-done.5.refs_1_
  55.6 2.1 %collective-permute-start.8 = (f32[256,256]{1,0:T(8,128)S(1)}, f32[256,256]{1,0:T(8,128)S(1)}, u32[]{:S(2)}, u32[]{:S(2)}) collective-permute-start(f32[256,256]{1,0:T(8,128)S(1)} %pad_maximum_fusion), channel_id=1, source_target_pairs={{0,1},{1,0},{2,3},{3,2},{4,5},{5,4},{6,7},{7,6},{8,9},{9,8},{10,11... | collective-permute-start | bytes 786440 | tf_op jit(solution)/shard_map/ppermute | solution.py:54
  57.6 0.3 collective-permute-done.16.refs_1_
  57.9 0.1 collective-permute-start.17
  58.0 0.6 shard_map.42
  58.6 0.6 shard_map.40.one
  59.3 3.4 %collective-permute-done.9.refs_1_ = f32[256,256]{1,0:T(8,128)S(1)} collective-permute-done((f32[256,256]{1,0:T(8,128)S(1)}, f32[256,256]{1,0:T(8,128)S(1)}, u32[]{:S(2)}, u32[]{:S(2)}) %collective-permute-start.9) | collective-permute-done | bytes 262176 | tf_op jit(solution)/shard_map/ppermute | solution.py:54
  62.7 4.8 %collective-permute-done.8.refs_0_ = f32[256,256]{1,0:T(8,128)S(1)} collective-permute-done((f32[256,256]{1,0:T(8,128)S(1)}, f32[256,256]{1,0:T(8,128)S(1)}, u32[]{:S(2)}, u32[]{:S(2)}) %collective-permute-start.8) | collective-permute-done | bytes 262176 | tf_op jit(solution)/shard_map/ppermute | solution.py:54
  67.5 0.6 shard_map.41.two
  68.1 0.0 collective-permute-done.17.refs_2_
  68.1 2.9 %shard_map.44 = f32[4096,128]{1,0:T(8,128)} custom-call(f32[512,512]{1,0:T(8,128)S(1)} %shard_map.40.one, f32[512,512]{1,0:T(8,128)S(1)} %shard_map.41.two, bf16[1024,256]{1,0:T(8,128)(2,1)S(1)} %get-tuple-element.23.v_high, bf16[1024,256]{1,0:T(8,128)(2,1)S(1)} %get-tuple-element.24.v_low, bf16[512,256]{1,0:T(8,128)(2,1)S(1)} %get-tuple-element.17.u_high, ...), custom_call_target="tpu_custom_call" | custom-call | tf_op jit(solution)/shard_map/pallas_call | solution.py:275
  (12 shorter events, 0.2 us)
Async XLA Ops:
  3.7 27.8 %copy-start.2 = (f32[256,256]{1,0:T(8,128)S(1)}, f32[256,256]{1,0:T(8,128)}, u32[]{:S(2)}) copy-start(f32[256,256]{1,0:T(8,128)} %t_ref.3) | copy-start | bytes 786436
  3.7 14.0 %collective-permute-start = (f32[512,256]{1,0:T(8,128)}, f32[512,256]{1,0:T(8,128)S(1)}, u32[]{:S(2)}, u32[]{:S(2)}) collective-permute-start(f32[512,256]{1,0:T(8,128)} %get-tuple-element.16), channel_id=1, source_target_pairs={{0,16},{4,20},{9,25},{13,29},{18,2},{22,6},{27,11},{31,15}} | collective-permute-start | bytes 1572872 | tf_op jit(solution)/shard_map/ppermute | solution.py:54
  8.7 1.8 %collective-permute-start.2 = (f32[256,256]{1,0:T(8,128)}, f32[256,256]{1,0:T(8,128)S(1)}, u32[]{:S(2)}, u32[]{:S(2)}) collective-permute-start(f32[256,256]{1,0:T(8,128)} %get-tuple-element.20), channel_id=1, source_target_pairs={{0,8},{1,9},{2,10},{3,11},{4,12},{5,13},{6,14},{7,15},{8,0},{9,1},... | collective-permute-start | bytes 786440 | tf_op jit(solution)/shard_map/ppermute | solution.py:54
  10.5 1.0 %copy-start.3 = (f32[256,256]{1,0:T(8,128)S(1)}, f32[256,256]{1,0:T(8,128)}, u32[]{:S(2)}) copy-start(f32[256,256]{1,0:T(8,128)} %get-tuple-element.19.keep) | copy-start | bytes 786436
  18.8 12.7 %collective-permute-start.1 = (f32[512,256]{1,0:T(8,128)S(1)}, f32[512,256]{1,0:T(8,128)S(1)}, u32[]{:S(2)}, u32[]{:S(2)}) collective-permute-start(f32[512,256]{1,0:T(8,128)S(1)} %broadcast_select_fusion.near), channel_id=1, source_target_pairs={{0,8},{2,10},{4,12},{6,14},{9,1},{11,3},{13,5},{15,7},{16,24},{18,... | collective-permute-start | bytes 1572872 | tf_op jit(solution)/shard_map/ppermute | solution.py:54
  20.1 6.4 %collective-permute-start.10 = (f32[256,256]{1,0:T(8,128)S(1)}, f32[256,256]{1,0:T(8,128)S(1)}, u32[]{:S(2)}, u32[]{:S(2)}) collective-permute-start(f32[256,256]{1,0:T(8,128)S(1)} %get-tuple-element.25), channel_id=1, source_target_pairs={{0,16},{1,17},{2,18},{3,19},{4,20},{5,21},{6,22},{7,23},{8,24},{9,... | collective-permute-start | bytes 786440 | tf_op jit(solution)/shard_map/ppermute | solution.py:54
  26.6 5.3 %collective-permute-start.11 = (f32[256,256]{1,0:T(8,128)S(1)}, f32[256,256]{1,0:T(8,128)S(1)}, u32[]{:S(2)}, u32[]{:S(2)}) collective-permute-start(f32[256,256]{1,0:T(8,128)S(1)} %add.24.mine.p_mine), channel_id=1, source_target_pairs={{0,8},{1,9},{2,10},{3,11},{4,12},{5,13},{6,14},{7,15},{8,0},{9,1},... | collective-permute-start | bytes 786440 | tf_op jit(solution)/shard_map/ppermute | solution.py:54
  26.7 10.2 %collective-permute-start.3 = (f32[128,256]{1,0:T(8,128)S(1)}, f32[128,256]{1,0:T(8,128)S(1)}, u32[]{:S(2)}, u32[]{:S(2)}) collective-permute-start(f32[128,256]{1,0:T(8,128)S(1)} %get-tuple-element.21), channel_id=1, source_target_pairs={{0,0},{1,8},{2,16},{3,24},{4,4},{5,12},{6,20},{7,28},{8,1},{9,9},{... | collective-permute-start | bytes 393224 | tf_op jit(solution)/shard_map/ppermute | solution.py:54
  27.3 30.7 %copy-start.1 = (f32[4,1,256,256]{3,2,1,0:T(8,128)S(1)}, f32[4,1,256,256]{3,2,1,0:T(8,128)}, u32[]{:S(2)}) copy-start(f32[4,1,256,256]{3,2,1,0:T(8,128)} %param.4) | copy-start | bytes 3145732
  27.3 9.5 %collective-permute-start.4 = (f32[128,256]{1,0:T(8,128)S(1)}, f32[128,256]{1,0:T(8,128)S(1)}, u32[]{:S(2)}, u32[]{:S(2)}) collective-permute-start(f32[128,256]{1,0:T(8,128)S(1)} %get-tuple-element.22), channel_id=1, source_target_pairs={{0,2},{1,10},{2,18},{3,26},{4,6},{5,14},{6,22},{7,30},{8,3},{9,11}... | collective-permute-start | bytes 393224 | tf_op jit(solution)/shard_map/ppermute | solution.py:54
  31.9 26.7 %copy-start = (f32[4,1,256,2,1,256]{5,4,3,2,1,0:T(1,128)S(1)}, f32[4,1,256,2,1,256]{5,4,3,2,1,0:T(1,128)}, u32[]{:S(2)}) copy-start(f32[4,1,256,2,1,256]{5,4,3,2,1,0:T(1,128)} %param.3) | copy-start | bytes 6291460
  32.4 7.2 %collective-permute-start.14 = (f32[64,256]{1,0:T(8,128)S(1)}, f32[64,256]{1,0:T(8,128)S(1)}, u32[]{:S(2)}, u32[]{:S(2)}) collective-permute-start(f32[64,256]{1,0:T(8,128)S(1)} %shard_map.43), channel_id=1, source_target_pairs={{0,6},{1,7},{2,4},{3,5},{4,2},{5,3},{6,0},{7,1},{8,14},{9,15},{10,... | collective-permute-start | bytes 196616 | tf_op jit(solution)/shard_map/ppermute | solution.py:54
  34.5 7.8 %collective-permute-start.13 = (f32[64,256]{1,0:T(8,128)S(1)}, f32[64,256]{1,0:T(8,128)S(1)}, u32[]{:S(2)}, u32[]{:S(2)}) collective-permute-start(f32[64,256]{1,0:T(8,128)S(1)} %shard_map.43), channel_id=1, source_target_pairs={{0,4},{1,5},{2,6},{3,7},{4,0},{5,1},{6,2},{7,3},{8,12},{9,13},{10,... | collective-permute-start | bytes 196616 | tf_op jit(solution)/shard_map/ppermute | solution.py:54
  35.1 7.2 %collective-permute-start.12 = (f32[64,256]{1,0:T(8,128)S(1)}, f32[64,256]{1,0:T(8,128)S(1)}, u32[]{:S(2)}, u32[]{:S(2)}) collective-permute-start(f32[64,256]{1,0:T(8,128)S(1)} %shard_map.43), channel_id=1, source_target_pairs={{0,2},{1,3},{2,0},{3,1},{4,6},{5,7},{6,4},{7,5},{8,10},{9,11},{10,... | collective-permute-start | bytes 196616 | tf_op jit(solution)/shard_map/ppermute | solution.py:54
  36.9 9.3 %collective-permute-start.7 = (f32[128,256]{1,0:T(8,128)S(1)}, f32[128,256]{1,0:T(8,128)S(1)}, u32[]{:S(2)}, u32[]{:S(2)}) collective-permute-start(f32[128,256]{1,0:T(8,128)S(1)} %add.23.refs_0_), channel_id=1, source_target_pairs={{0,6},{1,7},{2,4},{3,5},{4,2},{5,3},{6,0},{7,1},{8,14},{9,15},{10,... | collective-permute-start | bytes 393224 | tf_op jit(solution)/shard_map/ppermute | solution.py:54
  39.6 13.8 %collective-permute-start.6 = (f32[128,256]{1,0:T(8,128)S(1)}, f32[128,256]{1,0:T(8,128)S(1)}, u32[]{:S(2)}, u32[]{:S(2)}) collective-permute-start(f32[128,256]{1,0:T(8,128)S(1)} %add.23.refs_0_), channel_id=1, source_target_pairs={{0,4},{1,5},{2,6},{3,7},{4,0},{5,1},{6,2},{7,3},{8,12},{9,13},{10,... | collective-permute-start | bytes 393224 | tf_op jit(solution)/shard_map/ppermute | solution.py:54
  39.6 16.0 %collective-permute-start.5 = (f32[128,256]{1,0:T(8,128)S(1)}, f32[128,256]{1,0:T(8,128)S(1)}, u32[]{:S(2)}, u32[]{:S(2)}) collective-permute-start(f32[128,256]{1,0:T(8,128)S(1)} %add.23.refs_0_), channel_id=1, source_target_pairs={{0,2},{1,3},{2,0},{3,1},{4,6},{5,7},{6,4},{7,5},{8,10},{9,11},{10,... | collective-permute-start | bytes 393224 | tf_op jit(solution)/shard_map/ppermute | solution.py:54
  42.4 11.2 %collective-permute-start.15 = (f32[64,256]{1,0:T(8,128)S(1)}, f32[64,256]{1,0:T(8,128)S(1)}, u32[]{:S(2)}, u32[]{:S(2)}) collective-permute-start(f32[64,256]{1,0:T(8,128)S(1)} %add_add_fusion), channel_id=1, source_target_pairs={{0,1},{1,0},{2,3},{3,2},{4,5},{5,4},{6,7},{7,6},{8,9},{9,8},{10,11... | collective-permute-start | bytes 196616 | tf_op jit(solution)/shard_map/ppermute | solution.py:54
  53.4 9.2 %collective-permute-start.9 = (f32[256,256]{1,0:T(8,128)S(1)}, f32[256,256]{1,0:T(8,128)S(1)}, u32[]{:S(2)}, u32[]{:S(2)}) collective-permute-start(f32[256,256]{1,0:T(8,128)S(1)} %pad_maximum_fusion.1), channel_id=1, source_target_pairs={{0,1},{1,0},{2,3},{3,2},{4,5},{5,4},{6,7},{7,6},{8,9},{9,8},{10,11... | collective-permute-start | bytes 786440 | tf_op jit(solution)/shard_map/ppermute | solution.py:54
  53.5 4.4 %collective-permute-start.16 = (f32[64,256]{1,0:T(8,128)S(1)}, f32[64,256]{1,0:T(8,128)S(1)}, u32[]{:S(2)}, u32[]{:S(2)}) collective-permute-start(f32[64,256]{1,0:T(8,128)S(1)} %add.28.refs_0_), channel_id=1, source_target_pairs={{0,16},{1,17},{2,18},{3,19},{4,20},{5,21},{6,22},{7,23},{8,24},{9,... | collective-permute-start | bytes 196616 | tf_op jit(solution)/shard_map/ppermute | solution.py:54
  55.6 11.9 %collective-permute-start.8 = (f32[256,256]{1,0:T(8,128)S(1)}, f32[256,256]{1,0:T(8,128)S(1)}, u32[]{:S(2)}, u32[]{:S(2)}) collective-permute-start(f32[256,256]{1,0:T(8,128)S(1)} %pad_maximum_fusion), channel_id=1, source_target_pairs={{0,1},{1,0},{2,3},{3,2},{4,5},{5,4},{6,7},{7,6},{8,9},{9,8},{10,11... | collective-permute-start | bytes 786440 | tf_op jit(solution)/shard_map/ppermute | solution.py:54
  57.9 10.2 %collective-permute-start.17 = (f32[128,256]{1,0:T(8,128)S(1)}, f32[128,256]{1,0:T(8,128)S(1)}, u32[]{:S(2)}, u32[]{:S(2)}) collective-permute-start(f32[128,256]{1,0:T(8,128)S(1)} %pad_maximum_fusion.2), channel_id=1, source_target_pairs={{0,8},{1,9},{2,10},{3,11},{4,12},{5,13},{6,14},{7,15},{8,0},{9,1},... | collective-permute-start | bytes 393224 | tf_op jit(solution)/shard_map/ppermute | solution.py:54

commit v2 on v1

v2 whole, which is shorter than its diff:
```python
import functools

import jax
import jax.numpy as jnp
from jax import lax
from jax.experimental import pallas as pl
from jax.experimental.pallas import tpu as pltpu
from jax.sharding import PartitionSpec as P

AXES = ("row", "col")
F32, BF16 = jnp.float32, jnp.bfloat16
NN, NT, TN = ((1,), (0,)), ((1,), (1,)), ((0,), (0,))
LANES = 128
VMEM = pl.BlockSpec(memory_space=pltpu.VMEM)
HBM = pl.BlockSpec(memory_space=pltpu.HBM)
ANY = pl.BlockSpec(memory_space=pl.ANY)


def split(value):
    high = value.astype(BF16)
    return high, (value - high.astype(F32)).astype(BF16)


def product(left, right, dims):
    def one(a, b):
        return lax.dot_general(a, b, (dims, ((), ())), preferred_element_type=F32)

    (lh, ll), (rh, rl) = left, right
    return one(lh, rh) + (one(lh, rl) + one(ll, rh))


def sds(*shape, dtype=F32):
    return jax.ShapeDtypeStruct(shape, dtype)


def call(kernel, outs, *args, specs=None, scratch=(), limit=32):
    return pl.pallas_call(
        kernel,
        out_shape=outs,
        in_specs=specs or [VMEM] * len(args),
        out_specs=jax.tree.map(lambda _: VMEM, outs),
        scratch_shapes=list(scratch),
        compiler_params=pltpu.CompilerParams(vmem_limit_bytes=limit << 20),
    )(*args)


def send(value, rows, cols, target):
    pairs = []
    for row in range(rows):
        for col in range(cols):
            to = target(row, col)
            if to is not None:
                pairs.append((row * cols + col, to[0] * cols + to[1]))
    return lax.ppermute(value, AXES, pairs)


def with_unit_top(block):
    size = block.shape[0]
    i = lax.broadcasted_iota(jnp.int32, (size, size), 0)
    j = lax.broadcasted_iota(jnp.int32, (size, size), 1)
    unit = jnp.where(i > j, block, jnp.where(i == j, 1.0, 0.0))
    return jnp.where(lax.axis_index("row") == 0, unit, block)


def tile_rows(ref, start, count, width, first, lanes):
    step = width // LANES
    return jnp.concatenate(
        [ref[pl.ds(start * step + first + k, count, stride=step), :] for k in range(lanes // LANES)], axis=1
    )


def sums_kernel(width, a_hbm, v_hbm, keep, give, a_buf, v_buf, a_sem, v_sem):
    nb = v_buf.shape[1]
    count, step = v_buf.shape[0], width // LANES
    core = lax.axis_index("row") % 2
    copies = []
    for b in range(count):
        v_copy = pltpu.make_async_copy(v_hbm.at[pl.ds(b * nb, nb)], v_buf.at[b], v_sem.at[b])
        a_copy = pltpu.make_async_copy(a_hbm.at[pl.ds(b * nb * step, nb * step)], a_buf.at[b], a_sem.at[b])
        v_copy.start()
        a_copy.start()
        copies.append((v_copy, a_copy))
    for b in range(count):
        copies[b][0].wait()
        block = v_buf[b]
        if b == 0:
            block = with_unit_top(block)
        right = split(block)
        copies[b][1].wait()
        for out, half in ((give, 1 - core), (keep, core)):
            left = split(tile_rows(a_buf.at[b], 0, nb, width, half * (nb // LANES), nb))
            value = product(left, right, TN)
            out[...] = value if b == 0 else out[...] + value


def add_kernel(*refs):
    *terms, out = refs
    total = terms[0][...]
    for term in terms[1:]:
        total = total + term[...]
    out[...] = total


def late_add_kernel(count, *refs):
    add_kernel(*refs[count:])


def own_kernel(rows, v_ref, out):
    nb = v_ref.shape[1]
    group, ratio = lax.axis_index("col") // rows, lax.axis_size("col") // rows
    for k in range(out.shape[0] // nb):
        block = v_ref[pl.ds((k * ratio + group) * nb, nb), :]
        if k == 0:
            block = jnp.where(group == 0, with_unit_top(block), block)
        out[pl.ds(k * nb, nb), :] = block


def near_kernel(blocks, own, *refs):
    vecs, outs = refs[:-blocks], refs[-blocks:]
    nb = outs[0].shape[0]
    home = lax.axis_index("row") == lax.axis_index("col") % lax.axis_size("row")
    for k, out in enumerate(outs):
        at = pl.ds(k * nb, nb)

        @pl.when(home)
        def _():
            out[...] = own[at, :]

        @pl.when(jnp.logical_not(home))
        def _():
            came = vecs[0][at, :]
            for ref in vecs[1:]:
                came = came + ref[at, :]
            out[...] = came


def cols_kernel(t_ref, *refs):
    *vecs, high, low = refs
    blocks = len(vecs) // 2
    nb = vecs[0].shape[0]
    same = lax.axis_index("row") % 2 == lax.axis_index("col") % 2
    right = split(t_ref[...])
    for k in range(blocks):
        at = pl.ds(k * nb, nb)
        block = jnp.where(same, vecs[k][...], vecs[blocks + k][...])
        high[at, :], low[at, :] = split(product(split(block), right, NT))


def part_kernel(t, rows, v_ref, p_one, p_two, *refs):
    *before, out = refs
    nb, ratio = out.shape[0], v_ref.shape[0] // out.shape[0] // 2
    col = lax.axis_index("col")
    group, x = col // rows, col % 2
    value = 0.0
    for k, array in enumerate((p_one, p_two)):
        at = (x ^ k) * ratio + (group ^ t)
        block = v_ref[pl.ds(at * nb, nb), :]
        block = jnp.where(at == 0, with_unit_top(block), block)
        value = value + product(split(block), split(array[...]), TN)
    for ref in before:
        value = value + ref[...]
    out[...] = value


def cut_kernel(t, rows, v_ref, p_one, p_two, before, keep, give, whole):
    part_kernel(t, rows, v_ref, p_one, p_two, before, whole)
    count = keep.shape[0]
    core = lax.axis_index("row") % 2
    keep[...] = whole[pl.ds(core * count, count), :]
    give[...] = whole[pl.ds((1 - core) * count, count), :]


def rows_kernel(v_ref, t_ref, high, low):
    nb = t_ref.shape[0]
    right = split(t_ref[...])
    for b in range(v_ref.shape[0] // nb):
        at = pl.ds(b * nb, nb)
        block = v_ref[at, :]
        if b == 0:
            block = with_unit_top(block)
        high[at, :], low[at, :] = split(product(split(block), right, NT))


def first_kernel(flip, rows, a_ref, u_high, u_low, *refs):
    *arrays, out = refs
    col = lax.axis_index("col")
    group, h = col // rows, (col % 2) ^ flip
    nb, width = arrays[0].shape[0], out.shape[1]
    right = u_high[...], u_low[...]
    for t, array in enumerate(arrays):
        at = group ^ t
        value = product(split(array[...]), right, NT)
        out[pl.ds(at * nb, nb), :] = tile_rows(a_ref, (h * len(arrays) + at) * nb, nb, width, 0, width) - value


def last_kernel(nb, one, two, v_high, v_low, u_high, u_low, p_mine, p_other, s_mine, s_other, out, *scratch):
    inner, mixed, buf, sem = scratch
    row, x = lax.axis_index("row"), lax.axis_index("col") % 2
    core = row % 2
    count = s_mine.shape[0]
    inner[pl.ds(core * count, count), :] = s_mine[...]
    inner[pl.ds((1 - core) * count, count), :] = s_other[...]
    mixed[...] = product((u_high[...], u_low[...]), split(inner[...]), NT)
    half = p_mine.shape[0]
    for ref, c in ((p_mine, core), (p_other, 1 - core)):
        at = pl.ds(c * half, half)
        mixed[at, :] = mixed[at, :] - ref[...]
    right = split(mixed[...])
    width = one.shape[1]
    step = width // LANES
    blocks = one.shape[0] // nb
    copies = []
    for u, base in enumerate((one, two)):
        for b in range(blocks):
            at = (x ^ u) * blocks + b
            rows = pl.ds(at * nb, nb)
            value = base[pl.ds(b * nb, nb), :] + product((v_high[rows, :], v_low[rows, :]), right, NT)
            slot = u * blocks + b
            for k in range(step):
                buf[slot, pl.ds(k, nb, stride=step), :] = value[:, k * LANES : (k + 1) * LANES]
            copy = pltpu.make_async_copy(buf.at[slot], out.at[pl.ds(at * nb * step, nb * step)], sem.at[slot])
            copy.start()
            copies.append(copy)
    for copy in copies:
        copy.wait()


def per_device(matrix, vectors, t_factor):
    block_rows, _, nb, _ = vectors.shape
    width = matrix.shape[3] * nb
    rows, cols = lax.axis_size("row"), lax.axis_size("col")
    ratio, ys, zs = cols // rows, rows // 2, cols // 2
    row, col = lax.axis_index("row"), lax.axis_index("col")
    height, half, piece, share = block_rows * nb, width // 2, width // rows, nb // rows
    assert half == nb and block_rows == 2 * ratio
    step = width // LANES
    linear = matrix.reshape(height * step, LANES)
    vecs = vectors.reshape(height, nb)

    def move(value, target):
        return send(value, rows, cols, target)

    def other_core(r, c):
        return r ^ 1, c

    keep, give = call(
        functools.partial(sums_kernel, width),
        (sds(half, nb), sds(half, nb)),
        pltpu.with_memory_space_constraint(linear, pltpu.HBM),
        pltpu.with_memory_space_constraint(vecs, pltpu.HBM),
        specs=[HBM, HBM],
        scratch=[
            pltpu.VMEM((block_rows, nb * step, LANES), F32),
            pltpu.VMEM((block_rows, nb, nb), F32),
            pltpu.SemaphoreType.DMA((block_rows,)),
            pltpu.SemaphoreType.DMA((block_rows,)),
        ],
        limit=16,
    )
    chip = call(add_kernel, sds(half, nb), keep, move(give, other_core))

    sums = [move(chip, lambda r, c, s=s: (r ^ (2 * s), c)) for s in range(1, ys)]
    total = call(add_kernel, sds(half, nb), chip, *sums)

    def target(r, c, t):
        group, twin = c // rows, c % rows // 2
        return twin * 2 + c % 2, (group ^ t) * rows + (r ^ (2 * t))

    straight = [move(total, lambda r, c, t=t: target(r, c, t)) for t in range(ratio)]
    across = [move(value, lambda r, c: (r, c ^ 1)) for value in straight]

    own = call(functools.partial(own_kernel, rows), sds(width, nb), vecs)
    came = [move(own, lambda r, c, s=s: (r ^ (2 * s), c) if r == c % rows else None) for s in range(1, ys)]
    near = call(functools.partial(near_kernel, width // nb), [sds(nb, nb)] * (width // nb), own, *came)
    over = [move(part, lambda r, c: other_core(r, c) if r % 2 == c % 2 else None) for part in near]
    u_high, u_low = call(
        cols_kernel, (sds(width, nb, dtype=BF16), sds(width, nb, dtype=BF16)), t_factor, *near, *over
    )
    other = move(total, other_core)

    def first(flip, arrays):
        return call(
            functools.partial(first_kernel, flip, rows), sds(height // 2, width), linear, u_high, u_low, *arrays
        )

    one, two = first(0, straight), first(1, across)
    v_high, v_low = call(
        rows_kernel, (sds(height, nb, dtype=BF16), sds(height, nb, dtype=BF16)), vecs, t_factor
    )

    parts = []
    for t in range(ratio - 1):
        parts = [
            call(
                functools.partial(part_kernel, t, rows),
                sds(nb, nb),
                vecs,
                straight[t],
                across[t],
                *parts,
            )
        ]
    keep, give = call(
        functools.partial(cut_kernel, ratio - 1, rows),
        (sds(nb // 2, nb), sds(nb // 2, nb)),
        vecs,
        straight[-1],
        across[-1],
        *parts,
        scratch=[pltpu.VMEM((nb, nb), F32)],
    )
    share = call(add_kernel, sds(nb // 2, nb), keep, move(give, other_core))
    others = [move(share, lambda r, c, s=s: (r ^ (2 * s), c)) for s in range(1, ys)]
    ready = (one, two, v_high)
    share = call(
        functools.partial(late_add_kernel, len(ready)),
        sds(nb // 2, nb),
        *ready,
        share,
        *others,
        specs=[ANY] * len(ready) + [VMEM] * ys,
    )
    rest = move(share, other_core)

    result = pl.pallas_call(
        functools.partial(last_kernel, nb),
        out_shape=sds(height * step, LANES),
        in_specs=[VMEM] * 10,
        out_specs=HBM,
        scratch_shapes=[
            pltpu.VMEM((nb, nb), F32),
            pltpu.VMEM((width, nb), F32),
            pltpu.VMEM((block_rows, nb * step, LANES), F32),
            pltpu.SemaphoreType.DMA((block_rows,)),
        ],
        compiler_params=pltpu.CompilerParams(vmem_limit_bytes=32 << 20),
    )(one, two, v_high, v_low, u_high, u_low, total, other, share, rest)
    return result.reshape(matrix.shape)


def solution(mesh):
    in_specs = (P(None, "row", None, None, "col", None), P(None, "row", None, None), P())
    out_specs = P(None, "row", None, None, "col", None)
    return jax.shard_map(
        per_device, mesh=mesh, in_specs=in_specs, out_specs=out_specs, check_vma=False
    )
```

time: 71.3 us -> 54.2 us (0.76)
  waiting for transfers between devices: 29.7 us -> 22.1 us
  starting transfers between devices: 29.5 us -> 22.6 us
  other arithmetic: 1.23 us -> 0 us
  local copies, waits for them, and re-layouts: 0.97 us -> 0.02 us
    ppermute x18 -> x13, waiting for transfers between devices: 29.7 us -> 22.1 us  [send(): return lax.ppermute(value, AXES, pairs)]
    ppermute x18 -> x13, starting transfers between devices: 29.5 us -> 22.6 us  [send(): return lax.ppermute(value, AXES, pairs)]
    select_n x1 -> x0, other arithmetic: 1.11 us -> none  [per_device(): near = jnp.where(row == col % rows, own, came)]
    unnamed x8 -> x6, local copies, waits for them, and re-layouts: 0.97 us -> 0.02 us
    pallas_call x7 -> x13, Pallas kernels: 6.51 us -> 6.21 us  [call(): pl.pallas_call(kernel, out_shape=outs, in_specs=specs or [VMEM] * len(arg...]
  transfers between devices with their start and end apart: 18 -> 13, of which waited for: 8 -> 7; matrix products, arithmetic and copies ran while one was open for 0% -> 0% of each run, Pallas kernels for 4% -> 6%
where the time goes in v2:
time: 54.2 us; the launch traced here: 54 us
  starting transfers between devices  22.6 us (42%)
  waiting for transfers between devices  22.1 us (41%)
  Pallas kernels  9.09 us (17%)
    ppermute x13, starting transfers between devices, send(): return lax.ppermute(value, AXES, pairs)  22.6 us
    ppermute x13, waiting for transfers between devices, send(): return lax.ppermute(value, AXES, pairs)  22.1 us
    pallas_call x13, Pallas kernels, call(): pl.pallas_call(kernel, out_shape=outs, in_specs=specs or [VMEM] * len(arg...  6.21 us
    pallas_call x1, Pallas kernels, per_device(): pl.pallas_call(functools.partial(last_kernel, nb), out_shape=sds(height *...  2.89 us
  transfers between devices with their start and end apart: 13, of which 7 were waited for; matrix products, arithmetic and copies ran while one was open for 0% of the time, Pallas kernels for 6%

profile of v2, /device:TPU:0, one launch (start us, length us, event | category | flops | bytes accessed | tf_op | source)
XLA Modules:
  0.0 54.0 jit_solution(12405817216056833561)
XLA Ops:
  0.0 0.0 copy-start
  0.0 2.8 %shard_map.40 = (f32[256,256]{1,0:T(8,128)S(1)}, f32[256,256]{1,0:T(8,128)S(1)}) custom-call(f32[4096,128]{1,0:T(8,128)} %bitcast.8, f32[1024,256]{1,0:T(8,128)} %bitcast.3), custom_call_target="tpu_custom_call" | custom-call | tf_op jit(solution)/shard_map/pallas_call | solution.py:37
  2.8 0.5 collective-permute-start.3
  3.3 1.2 %collective-permute-done.3.refs_1_ = f32[256,256]{1,0:T(8,128)S(1)} collective-permute-done((f32[256,256]{1,0:T(8,128)S(1)}, f32[256,256]{1,0:T(8,128)S(1)}, u32[]{:S(2)}, u32[]{:S(2)}) %collective-permute-start.3) | collective-permute-done | bytes 262176 | tf_op jit(solution)/shard_map/ppermute | solution.py:54
  4.5 2.9 %collective-permute-start.4 = (f32[256,256]{1,0:T(8,128)S(1)}, f32[256,256]{1,0:T(8,128)S(1)}, u32[]{:S(2)}, u32[]{:S(2)}) collective-permute-start(f32[256,256]{1,0:T(8,128)S(1)} %shard_map.41.refs_0_), channel_id=1, source_target_pairs={{0,16},{1,17},{2,18},{3,19},{4,20},{5,21},{6,22},{7,23},{8,24},{9,... | collective-permute-start | bytes 786440 | tf_op jit(solution)/shard_map/ppermute | solution.py:54
  7.4 0.0 copy-done
  7.5 0.1 shard_map.37.own
  7.5 2.0 %collective-permute-start = (f32[512,256]{1,0:T(8,128)S(1)}, f32[512,256]{1,0:T(8,128)S(1)}, u32[]{:S(2)}, u32[]{:S(2)}) collective-permute-start(f32[512,256]{1,0:T(8,128)S(1)} %shard_map.37.own), channel_id=1, source_target_pairs={{0,16},{4,20},{9,25},{13,29},{18,2},{22,6},{27,11},{31,15}} | collective-permute-start | bytes 1572872 | tf_op jit(solution)/shard_map/ppermute | solution.py:54
  9.5 4.6 %collective-permute-done.4.refs_1_ = f32[256,256]{1,0:T(8,128)S(1)} collective-permute-done((f32[256,256]{1,0:T(8,128)S(1)}, f32[256,256]{1,0:T(8,128)S(1)}, u32[]{:S(2)}, u32[]{:S(2)}) %collective-permute-start.4) | collective-permute-done | bytes 262176 | tf_op jit(solution)/shard_map/ppermute | solution.py:54
  14.1 0.7 %collective-permute-start.5 = (f32[256,256]{1,0:T(8,128)S(1)}, f32[256,256]{1,0:T(8,128)S(1)}, u32[]{:S(2)}, u32[]{:S(2)}) collective-permute-start(f32[256,256]{1,0:T(8,128)S(1)} %shard_map.42.p_mine), channel_id=1, source_target_pairs={{0,0},{1,8},{2,16},{3,24},{4,4},{5,12},{6,20},{7,28},{8,1},{9,9},{... | collective-permute-start | bytes 786440 | tf_op jit(solution)/shard_map/ppermute | solution.py:54
  14.8 6.5 %collective-permute-start.6 = (f32[256,256]{1,0:T(8,128)S(1)}, f32[256,256]{1,0:T(8,128)S(1)}, u32[]{:S(2)}, u32[]{:S(2)}) collective-permute-start(f32[256,256]{1,0:T(8,128)S(1)} %shard_map.42.p_mine), channel_id=1, source_target_pairs={{0,6},{1,14},{2,22},{3,30},{4,2},{5,10},{6,18},{7,26},{8,7},{9,15}... | collective-permute-start | bytes 786440 | tf_op jit(solution)/shard_map/ppermute | solution.py:54
  21.3 0.0 collective-permute-done.5.refs_0_.p_one
  21.3 2.9 %collective-permute-start.7 = (f32[256,256]{1,0:T(8,128)S(1)}, f32[256,256]{1,0:T(8,128)S(1)}, u32[]{:S(2)}, u32[]{:S(2)}) collective-permute-start(f32[256,256]{1,0:T(8,128)S(1)} %collective-permute-done.5.refs_0_.p_one), channel_id=1, source_target_pairs={{0,1},{1,0},{2,3},{3,2},{4,5},{5,4},{6,7},{7,6},{8,9},{9,8},{10,11... | collective-permute-start | bytes 786440 | tf_op jit(solution)/shard_map/ppermute | solution.py:54
  24.2 9.3 %collective-permute-done.6.refs_1_.p_one = f32[256,256]{1,0:T(8,128)S(1)} collective-permute-done((f32[256,256]{1,0:T(8,128)S(1)}, f32[256,256]{1,0:T(8,128)S(1)}, u32[]{:S(2)}, u32[]{:S(2)}) %collective-permute-start.6) | collective-permute-done | bytes 262176 | tf_op jit(solution)/shard_map/ppermute | solution.py:54
  33.5 2.2 %collective-permute-start.8 = (f32[256,256]{1,0:T(8,128)S(1)}, f32[256,256]{1,0:T(8,128)S(1)}, u32[]{:S(2)}, u32[]{:S(2)}) collective-permute-start(f32[256,256]{1,0:T(8,128)S(1)} %collective-permute-done.6.refs_1_.p_one), channel_id=1, source_target_pairs={{0,1},{1,0},{2,3},{3,2},{4,5},{5,4},{6,7},{7,6},{8,9},{9,8},{10,11... | collective-permute-start | bytes 786440 | tf_op jit(solution)/shard_map/ppermute | solution.py:54
  35.7 0.0 collective-permute-done.refs_0_
  35.7 0.0 copy-start.2
  35.8 1.4 %collective-permute-start.1 = (f32[256,256]{1,0:T(8,128)S(1)}, f32[256,256]{1,0:T(8,128)S(1)}, u32[]{:S(2)}, u32[]{:S(2)}) collective-permute-start(f32[256,256]{1,0:T(8,128)S(1)} %get-tuple-element.15.refs_0_), channel_id=1, source_target_pairs={{0,8},{2,10},{4,12},{6,14},{9,1},{11,3},{13,5},{15,7},{16,24},{18,... | collective-permute-start | bytes 786440 | tf_op jit(solution)/shard_map/ppermute | solution.py:54
  37.2 1.3 %collective-permute-start.2 = (f32[256,256]{1,0:T(8,128)S(1)}, f32[256,256]{1,0:T(8,128)S(1)}, u32[]{:S(2)}, u32[]{:S(2)}) collective-permute-start(f32[256,256]{1,0:T(8,128)S(1)} %get-tuple-element.16.refs_1_), channel_id=1, source_target_pairs={{0,8},{2,10},{4,12},{6,14},{9,1},{11,3},{13,5},{15,7},{16,24},{18,... | collective-permute-start | bytes 786440 | tf_op jit(solution)/shard_map/ppermute | solution.py:54
  38.5 0.0 collective-permute-done.7.refs_0_.p_two
  38.5 0.5 shard_map.46.before
  39.0 0.0 copy-start.1
  39.0 2.9 %collective-permute-done.8.refs_1_.p_two = f32[256,256]{1,0:T(8,128)S(1)} collective-permute-done((f32[256,256]{1,0:T(8,128)S(1)}, f32[256,256]{1,0:T(8,128)S(1)}, u32[]{:S(2)}, u32[]{:S(2)}) %collective-permute-start.8) | collective-permute-done | bytes 262176 | tf_op jit(solution)/shard_map/ppermute | solution.py:54
  41.9 0.5 shard_map.47
  42.4 0.1 collective-permute-start.10
  42.5 1.3 %collective-permute-done.10.refs_1_ = f32[128,256]{1,0:T(8,128)S(1)} collective-permute-done((f32[128,256]{1,0:T(8,128)S(1)}, f32[128,256]{1,0:T(8,128)S(1)}, u32[]{:S(2)}, u32[]{:S(2)}) %collective-permute-start.10) | collective-permute-done | bytes 131104 | tf_op jit(solution)/shard_map/ppermute | solution.py:54
  43.8 2.1 %collective-permute-start.11 = (f32[128,256]{1,0:T(8,128)S(1)}, f32[128,256]{1,0:T(8,128)S(1)}, u32[]{:S(2)}, u32[]{:S(2)}) collective-permute-start(f32[128,256]{1,0:T(8,128)S(1)} %shard_map.48.refs_3_), channel_id=1, source_target_pairs={{0,16},{1,17},{2,18},{3,19},{4,20},{5,21},{6,22},{7,23},{8,24},{9,... | collective-permute-start | bytes 393224 | tf_op jit(solution)/shard_map/ppermute | solution.py:54
  45.9 0.0 collective-permute-start.9
  45.9 0.0 copy-done.2
  45.9 0.6 %shard_map.45 = (bf16[1024,256]{1,0:T(8,128)(2,1)S(1)}, bf16[1024,256]{1,0:T(8,128)(2,1)S(1)}) custom-call(f32[1024,256]{1,0:T(8,128)S(1)} %bitcast.7, f32[256,256]{1,0:T(8,128)S(1)} %copy-done.2), custom_call_target="tpu_custom_call" | custom-call | tf_op jit(solution)/shard_map/pallas_call | solution.py:37
  46.5 0.0 collective-permute-done.1.refs_2_
  46.5 0.0 collective-permute-done.2.refs_3_
  46.6 0.4 shard_map.39
  47.0 0.0 copy-done.1
  47.0 0.6 %shard_map.43.refs_0_.one = f32[512,512]{1,0:T(8,128)S(1)} custom-call(f32[4096,128]{1,0:T(8,128)S(1)} %bitcast.9, bf16[512,256]{1,0:T(8,128)(2,1)S(1)} %get-tuple-element.17.u_high, bf16[512,256]{1,0:T(8,128)(2,1)S(1)} %get-tuple-element.18.u_low, f32[256,256]{1,0:T(8,128)S(1)} %collective-permute-done.5.refs_0_.p_one, ...), custom_call_target="tpu_custom_call" | custom-call | tf_op jit(solution)/shard_map/pallas_call | solution.py:37
  47.6 0.6 %shard_map.44.refs_1_.two = f32[512,512]{1,0:T(8,128)S(1)} custom-call(f32[4096,128]{1,0:T(8,128)S(1)} %bitcast.10, bf16[512,256]{1,0:T(8,128)(2,1)S(1)} %get-tuple-element.17.u_high, bf16[512,256]{1,0:T(8,128)(2,1)S(1)} %get-tuple-element.18.u_low, f32[256,256]{1,0:T(8,128)S(1)} %collective-permute-done.7.refs_0_.p_two, ...), custom_call_target="tpu_custom_call" | custom-call | tf_op jit(solution)/shard_map/pallas_call | solution.py:37
  48.2 1.5 %collective-permute-done.11.refs_4_ = f32[128,256]{1,0:T(8,128)S(1)} collective-permute-done((f32[128,256]{1,0:T(8,128)S(1)}, f32[128,256]{1,0:T(8,128)S(1)}, u32[]{:S(2)}, u32[]{:S(2)}) %collective-permute-start.11) | collective-permute-done | bytes 131104 | tf_op jit(solution)/shard_map/ppermute | solution.py:54
  49.7 0.1 collective-permute-start.12
  49.8 0.0 collective-permute-done.9.p_other
  49.8 1.3 %collective-permute-done.12.s_other = f32[128,256]{1,0:T(8,128)S(1)} collective-permute-done((f32[128,256]{1,0:T(8,128)S(1)}, f32[128,256]{1,0:T(8,128)S(1)}, u32[]{:S(2)}, u32[]{:S(2)}) %collective-permute-start.12) | collective-permute-done | bytes 131104 | tf_op jit(solution)/shard_map/ppermute | solution.py:54
  51.1 2.9 %shard_map.50 = f32[4096,128]{1,0:T(8,128)} custom-call(f32[512,512]{1,0:T(8,128)S(1)} %shard_map.43.refs_0_.one, f32[512,512]{1,0:T(8,128)S(1)} %shard_map.44.refs_1_.two, bf16[1024,256]{1,0:T(8,128)(2,1)S(1)} %get-tuple-element.21.refs_2_.v_high, bf16[1024,256]{1,0:T(8,128)(2,1)S(1)} %get-tuple-element.22.v_low, ...), custom_call_target="tpu_custom_call" | custom-call | tf_op jit(solution)/shard_map/pallas_call | solution.py:325
  (5 shorter events, 0.1 us)
Async XLA Ops:
  0.0 7.5 %copy-start = (f32[4,1,256,256]{3,2,1,0:T(8,128)S(1)}, f32[4,1,256,256]{3,2,1,0:T(8,128)}, u32[]{:S(2)}) copy-start(f32[4,1,256,256]{3,2,1,0:T(8,128)} %param.4) | copy-start | bytes 3145732
  2.8 1.7 %collective-permute-start.3 = (f32[256,256]{1,0:T(8,128)S(1)}, f32[256,256]{1,0:T(8,128)S(1)}, u32[]{:S(2)}, u32[]{:S(2)}) collective-permute-start(f32[256,256]{1,0:T(8,128)S(1)} %get-tuple-element.20), channel_id=1, source_target_pairs={{0,8},{1,9},{2,10},{3,11},{4,12},{5,13},{6,14},{7,15},{8,0},{9,1},... | collective-permute-start | bytes 786440 | tf_op jit(solution)/shard_map/ppermute | solution.py:54
  4.5 9.5 %collective-permute-start.4 = (f32[256,256]{1,0:T(8,128)S(1)}, f32[256,256]{1,0:T(8,128)S(1)}, u32[]{:S(2)}, u32[]{:S(2)}) collective-permute-start(f32[256,256]{1,0:T(8,128)S(1)} %shard_map.41.refs_0_), channel_id=1, source_target_pairs={{0,16},{1,17},{2,18},{3,19},{4,20},{5,21},{6,22},{7,23},{8,24},{9,... | collective-permute-start | bytes 786440 | tf_op jit(solution)/shard_map/ppermute | solution.py:54
  7.5 28.2 %collective-permute-start = (f32[512,256]{1,0:T(8,128)S(1)}, f32[512,256]{1,0:T(8,128)S(1)}, u32[]{:S(2)}, u32[]{:S(2)}) collective-permute-start(f32[512,256]{1,0:T(8,128)S(1)} %shard_map.37.own), channel_id=1, source_target_pairs={{0,16},{4,20},{9,25},{13,29},{18,2},{22,6},{27,11},{31,15}} | collective-permute-start | bytes 1572872 | tf_op jit(solution)/shard_map/ppermute | solution.py:54
  14.1 7.2 %collective-permute-start.5 = (f32[256,256]{1,0:T(8,128)S(1)}, f32[256,256]{1,0:T(8,128)S(1)}, u32[]{:S(2)}, u32[]{:S(2)}) collective-permute-start(f32[256,256]{1,0:T(8,128)S(1)} %shard_map.42.p_mine), channel_id=1, source_target_pairs={{0,0},{1,8},{2,16},{3,24},{4,4},{5,12},{6,20},{7,28},{8,1},{9,9},{... | collective-permute-start | bytes 786440 | tf_op jit(solution)/shard_map/ppermute | solution.py:54
  14.8 18.8 %collective-permute-start.6 = (f32[256,256]{1,0:T(8,128)S(1)}, f32[256,256]{1,0:T(8,128)S(1)}, u32[]{:S(2)}, u32[]{:S(2)}) collective-permute-start(f32[256,256]{1,0:T(8,128)S(1)} %shard_map.42.p_mine), channel_id=1, source_target_pairs={{0,6},{1,14},{2,22},{3,30},{4,2},{5,10},{6,18},{7,26},{8,7},{9,15}... | collective-permute-start | bytes 786440 | tf_op jit(solution)/shard_map/ppermute | solution.py:54
  21.3 17.2 %collective-permute-start.7 = (f32[256,256]{1,0:T(8,128)S(1)}, f32[256,256]{1,0:T(8,128)S(1)}, u32[]{:S(2)}, u32[]{:S(2)}) collective-permute-start(f32[256,256]{1,0:T(8,128)S(1)} %collective-permute-done.5.refs_0_.p_one), channel_id=1, source_target_pairs={{0,1},{1,0},{2,3},{3,2},{4,5},{5,4},{6,7},{7,6},{8,9},{9,8},{10,11... | collective-permute-start | bytes 786440 | tf_op jit(solution)/shard_map/ppermute | solution.py:54
  33.5 8.3 %collective-permute-start.8 = (f32[256,256]{1,0:T(8,128)S(1)}, f32[256,256]{1,0:T(8,128)S(1)}, u32[]{:S(2)}, u32[]{:S(2)}) collective-permute-start(f32[256,256]{1,0:T(8,128)S(1)} %collective-permute-done.6.refs_1_.p_one), channel_id=1, source_target_pairs={{0,1},{1,0},{2,3},{3,2},{4,5},{5,4},{6,7},{7,6},{8,9},{9,8},{10,11... | collective-permute-start | bytes 786440 | tf_op jit(solution)/shard_map/ppermute | solution.py:54
  35.7 10.2 %copy-start.2 = (f32[256,256]{1,0:T(8,128)S(1)}, f32[256,256]{1,0:T(8,128)}, u32[]{:S(2)}) copy-start(f32[256,256]{1,0:T(8,128)} %t_ref.3) | copy-start | bytes 786436
  35.8 10.8 %collective-permute-start.1 = (f32[256,256]{1,0:T(8,128)S(1)}, f32[256,256]{1,0:T(8,128)S(1)}, u32[]{:S(2)}, u32[]{:S(2)}) collective-permute-start(f32[256,256]{1,0:T(8,128)S(1)} %get-tuple-element.15.refs_0_), channel_id=1, source_target_pairs={{0,8},{2,10},{4,12},{6,14},{9,1},{11,3},{13,5},{15,7},{16,24},{18,... | collective-permute-start | bytes 786440 | tf_op jit(solution)/shard_map/ppermute | solution.py:54
  37.2 9.3 %collective-permute-start.2 = (f32[256,256]{1,0:T(8,128)S(1)}, f32[256,256]{1,0:T(8,128)S(1)}, u32[]{:S(2)}, u32[]{:S(2)}) collective-permute-start(f32[256,256]{1,0:T(8,128)S(1)} %get-tuple-element.16.refs_1_), channel_id=1, source_target_pairs={{0,8},{2,10},{4,12},{6,14},{9,1},{11,3},{13,5},{15,7},{16,24},{18,... | collective-permute-start | bytes 786440 | tf_op jit(solution)/shard_map/ppermute | solution.py:54
  39.0 8.0 %copy-start.1 = (f32[4,1,256,2,1,256]{5,4,3,2,1,0:T(1,128)S(1)}, f32[4,1,256,2,1,256]{5,4,3,2,1,0:T(1,128)}, u32[]{:S(2)}) copy-start(f32[4,1,256,2,1,256]{5,4,3,2,1,0:T(1,128)} %param.3) | copy-start | bytes 6291460
  42.4 1.4 %collective-permute-start.10 = (f32[128,256]{1,0:T(8,128)S(1)}, f32[128,256]{1,0:T(8,128)S(1)}, u32[]{:S(2)}, u32[]{:S(2)}) collective-permute-start(f32[128,256]{1,0:T(8,128)S(1)} %get-tuple-element.24), channel_id=1, source_target_pairs={{0,8},{1,9},{2,10},{3,11},{4,12},{5,13},{6,14},{7,15},{8,0},{9,1},... | collective-permute-start | bytes 393224 | tf_op jit(solution)/shard_map/ppermute | solution.py:54
  43.8 5.9 %collective-permute-start.11 = (f32[128,256]{1,0:T(8,128)S(1)}, f32[128,256]{1,0:T(8,128)S(1)}, u32[]{:S(2)}, u32[]{:S(2)}) collective-permute-start(f32[128,256]{1,0:T(8,128)S(1)} %shard_map.48.refs_3_), channel_id=1, source_target_pairs={{0,16},{1,17},{2,18},{3,19},{4,20},{5,21},{6,22},{7,23},{8,24},{9,... | collective-permute-start | bytes 393224 | tf_op jit(solution)/shard_map/ppermute | solution.py:54
  45.9 3.9 %collective-permute-start.9 = (f32[256,256]{1,0:T(8,128)S(1)}, f32[256,256]{1,0:T(8,128)S(1)}, u32[]{:S(2)}, u32[]{:S(2)}) collective-permute-start(f32[256,256]{1,0:T(8,128)S(1)} %shard_map.42.p_mine), channel_id=1, source_target_pairs={{0,8},{1,9},{2,10},{3,11},{4,12},{5,13},{6,14},{7,15},{8,0},{9,1},... | collective-permute-start | bytes 786440 | tf_op jit(solution)/shard_map/ppermute | solution.py:54
  49.7 1.4 %collective-permute-start.12 = (f32[128,256]{1,0:T(8,128)S(1)}, f32[128,256]{1,0:T(8,128)S(1)}, u32[]{:S(2)}, u32[]{:S(2)}) collective-permute-start(f32[128,256]{1,0:T(8,128)S(1)} %shard_map.49.s_mine), channel_id=1, source_target_pairs={{0,8},{1,9},{2,10},{3,11},{4,12},{5,13},{6,14},{7,15},{8,0},{9,1},... | collective-permute-start | bytes 393224 | tf_op jit(solution)/shard_map/ppermute | solution.py:54

commit v3 on v2

--- a/solution.py
+++ b/solution.py
@@ -105,69 +105,65 @@
     add_kernel(*refs[count:])
 
 
-def own_kernel(rows, v_ref, out):
+def late_add(ready, *terms):
+    return call(
+        functools.partial(late_add_kernel, len(ready)),
+        sds(*terms[0].shape),
+        *ready,
+        *terms,
+        specs=[ANY] * len(ready) + [VMEM] * len(terms),
+    )
+
+
+def own_kernel(rows, _, v_ref, *outs):
     nb = v_ref.shape[1]
     group, ratio = lax.axis_index("col") // rows, lax.axis_size("col") // rows
-    for k in range(out.shape[0] // nb):
-        block = v_ref[pl.ds((k * ratio + group) * nb, nb), :]
-        if k == 0:
-            block = jnp.where(group == 0, with_unit_top(block), block)
-        out[pl.ds(k * nb, nb), :] = block
-
-
-def near_kernel(blocks, own, *refs):
-    vecs, outs = refs[:-blocks], refs[-blocks:]
-    nb = outs[0].shape[0]
-    home = lax.axis_index("row") == lax.axis_index("col") % lax.axis_size("row")
-    for k, out in enumerate(outs):
+    core = lax.axis_index("row") % 2
+    for k, out in zip((core, 1 - core), outs):
+        at = k * ratio + group
+        block = v_ref[pl.ds(at * nb, nb), :]
+        out[...] = jnp.where(at == 0, with_unit_top(block), block)
+
+
+def pick_core_kernel(mine, came, out):
+    same = lax.axis_index("row") % 2 == lax.axis_index("col") % 2
+    out[...] = jnp.where(same, mine[...], came[...])
+
+
+def pick_plane_kernel(mine, *refs):
+    *vecs, out = refs
+    rows = lax.axis_size("row")
+    same = lax.axis_index("row") // 2 == lax.axis_index("col") % rows // 2
+    came = vecs[0][...]
+    for ref in vecs[1:]:
+        came = came + ref[...]
+    out[...] = jnp.where(same, mine[...], came)
+
+
+def cols_kernel(mine, other, t_ref, high, low):
+    nb = mine.shape[0]
+    core = lax.axis_index("row") % 2
+    right = split(t_ref[...])
+    for k, ref in zip((core, 1 - core), (mine, other)):
         at = pl.ds(k * nb, nb)
-
-        @pl.when(home)
-        def _():
-            out[...] = own[at, :]
-
-        @pl.when(jnp.logical_not(home))
-        def _():
-            came = vecs[0][at, :]
-            for ref in vecs[1:]:
-                came = came + ref[at, :]
-            out[...] = came
-
-
-def cols_kernel(t_ref, *refs):
-    *vecs, high, low = refs
-    blocks = len(vecs) // 2
-    nb = vecs[0].shape[0]
-    same = lax.axis_index("row") % 2 == lax.axis_index("col") % 2
-    right = split(t_ref[...])
-    for k in range(blocks):
-        at = pl.ds(k * nb, nb)
-        block = jnp.where(same, vecs[k][...], vecs[blocks + k][...])
-        high[at, :], low[at, :] = split(product(split(block), right, NT))
-
-
-def part_kernel(t, rows, v_ref, p_one, p_two, *refs):
-    *before, out = refs
-    nb, ratio = out.shape[0], v_ref.shape[0] // out.shape[0] // 2
-    col = lax.axis_index("col")
+        high[at, :], low[at, :] = split(product(split(ref[...]), right, NT))
+
+
+def part_kernel(rows, v_ref, *refs):
+    *arrays, keep, give, whole = refs
+    nb, half = whole.shape[0], whole.shape[0] // 2
+    col, core = lax.axis_index("col"), lax.axis_index("row") % 2
     group, x = col // rows, col % 2
     value = 0.0
-    for k, array in enumerate((p_one, p_two)):
-        at = (x ^ k) * ratio + (group ^ t)
+    for t, array in enumerate(arrays):
+        at = x * len(arrays) + (group ^ t)
         block = v_ref[pl.ds(at * nb, nb), :]
         block = jnp.where(at == 0, with_unit_top(block), block)
         value = value + product(split(block), split(array[...]), TN)
-    for ref in before:
-        value = value + ref[...]
-    out[...] = value
-
-
-def cut_kernel(t, rows, v_ref, p_one, p_two, before, keep, give, whole):
-    part_kernel(t, rows, v_ref, p_one, p_two, before, whole)
-    count = keep.shape[0]
-    core = lax.axis_index("row") % 2
-    keep[...] = whole[pl.ds(core * count, count), :]
-    give[...] = whole[pl.ds((1 - core) * count, count), :]
+    whole[...] = value
+    for out, first in ((keep, core == 0), (give, core == 1)):
+        out[pl.ds(0, half), :] = jnp.where(first, whole[:half, :half], whole[half:, half:])
+        out[pl.ds(half, half // 2), :] = jnp.where(first, whole[: half // 2, half:], whole[half // 2 : half, half:])
 
 
 def rows_kernel(v_ref, t_ref, high, low):
@@ -181,46 +177,46 @@
         high[at, :], low[at, :] = split(product(split(block), right, NT))
 
 
-def first_kernel(flip, rows, a_ref, u_high, u_low, *refs):
-    *arrays, out = refs
+def first_kernel(flip, t, rows, a_ref, u_high, u_low, prods, *refs):
+    out = refs[-1]
     col = lax.axis_index("col")
     group, h = col // rows, (col % 2) ^ flip
-    nb, width = arrays[0].shape[0], out.shape[1]
-    right = u_high[...], u_low[...]
-    for t, array in enumerate(arrays):
-        at = group ^ t
-        value = product(split(array[...]), right, NT)
-        out[pl.ds(at * nb, nb), :] = tile_rows(a_ref, (h * len(arrays) + at) * nb, nb, width, 0, width) - value
-
-
-def last_kernel(nb, one, two, v_high, v_low, u_high, u_low, p_mine, p_other, s_mine, s_other, out, *scratch):
-    inner, mixed, buf, sem = scratch
-    row, x = lax.axis_index("row"), lax.axis_index("col") % 2
+    nb, width = out.shape
+    at = h * (lax.axis_size("col") // rows) + (group ^ t)
+    value = product(split(prods[...]), (u_high[...], u_low[...]), NT)
+    out[...] = tile_rows(a_ref, at * nb, nb, width, 0, width) - value
+
+
+def last_kernel(places, rows, v_high, v_low, u_high, u_low, p_mine, p_other, s_mine, s_other, *refs):
+    *bases, out, inner, mixed, buf, sem = refs
+    row, col = lax.axis_index("row"), lax.axis_index("col")
     core = row % 2
-    count = s_mine.shape[0]
-    inner[pl.ds(core * count, count), :] = s_mine[...]
-    inner[pl.ds((1 - core) * count, count), :] = s_other[...]
+    half = inner.shape[0] // 2
+    first = jnp.where(core == 0, s_mine[...], s_other[...])
+    second = jnp.where(core == 0, s_other[...], s_mine[...])
+    corner = jnp.concatenate([first[half:], second[half:]], axis=0)
+    inner[:half, :half] = first[:half]
+    inner[:half, half:] = corner
+    inner[half:, :half] = corner.T
+    inner[half:, half:] = second[:half]
     mixed[...] = product((u_high[...], u_low[...]), split(inner[...]), NT)
     half = p_mine.shape[0]
     for ref, c in ((p_mine, core), (p_other, 1 - core)):
         at = pl.ds(c * half, half)
         mixed[at, :] = mixed[at, :] - ref[...]
     right = split(mixed[...])
-    width = one.shape[1]
+    nb, width = bases[0].shape
     step = width // LANES
-    blocks = one.shape[0] // nb
     copies = []
-    for u, base in enumerate((one, two)):
-        for b in range(blocks):
-            at = (x ^ u) * blocks + b
-            rows = pl.ds(at * nb, nb)
-            value = base[pl.ds(b * nb, nb), :] + product((v_high[rows, :], v_low[rows, :]), right, NT)
-            slot = u * blocks + b
-            for k in range(step):
-                buf[slot, pl.ds(k, nb, stride=step), :] = value[:, k * LANES : (k + 1) * LANES]
-            copy = pltpu.make_async_copy(buf.at[slot], out.at[pl.ds(at * nb * step, nb * step)], sem.at[slot])
-            copy.start()
-            copies.append(copy)
+    for k, (base, (flip, t)) in enumerate(zip(bases, places)):
+        at = (col % 2 ^ flip) * (lax.axis_size("col") // rows) + (col // rows ^ t)
+        rows_at = pl.ds(at * nb, nb)
+        value = base[...] + product((v_high[rows_at, :], v_low[rows_at, :]), right, NT)
+        for j in range(step):
+            buf[k, pl.ds(j, nb, stride=step), :] = value[:, j * LANES : (j + 1) * LANES]
+        copy = pltpu.make_async_copy(buf.at[k], out.at[pl.ds(at * nb * step, nb * step)], sem.at[k])
+        copy.start()
+        copies.append(copy)
     for copy in copies:
         copy.wait()
 
@@ -269,63 +265,57 @@
     straight = [move(total, lambda r, c, t=t: target(r, c, t)) for t in range(ratio)]
     across = [move(value, lambda r, c: (r, c ^ 1)) for value in straight]
 
-    own = call(functools.partial(own_kernel, rows), sds(width, nb), vecs)
-    came = [move(own, lambda r, c, s=s: (r ^ (2 * s), c) if r == c % rows else None) for s in range(1, ys)]
-    near = call(functools.partial(near_kernel, width // nb), [sds(nb, nb)] * (width // nb), own, *came)
-    over = [move(part, lambda r, c: other_core(r, c) if r % 2 == c % 2 else None) for part in near]
+    own = call(functools.partial(own_kernel, rows), [sds(nb, nb)] * 2, keep, vecs, specs=[ANY, VMEM])
+    came = move(own[1], lambda r, c: other_core(r, c) if r == c % rows else None)
+    block = call(pick_core_kernel, sds(nb, nb), own[0], came)
+    came = [
+        move(block, lambda r, c, s=s: (r ^ (2 * s), c) if r // 2 == c % rows // 2 else None) for s in range(1, ys)
+    ]
+    near = call(pick_plane_kernel, sds(nb, nb), block, *came)
     u_high, u_low = call(
-        cols_kernel, (sds(width, nb, dtype=BF16), sds(width, nb, dtype=BF16)), t_factor, *near, *over
+        cols_kernel,
+        (sds(width, nb, dtype=BF16), sds(width, nb, dtype=BF16)),
+        near,
+        move(near, other_core),
+        t_factor,
     )
     other = move(total, other_core)
 
-    def first(flip, arrays):
-        return call(
-            functools.partial(first_kernel, flip, rows), sds(height // 2, width), linear, u_high, u_low, *arrays
+    places = [(1, 0)] + [(0, t) for t in range(ratio)] + [(1, t) for t in range(1, ratio)]
+    bases = []
+    for flip, t in places:
+        bases.append(
+            call(
+                functools.partial(first_kernel, flip, t, rows),
+                sds(nb, width),
+                linear,
+                u_high,
+                u_low,
+                (straight, across)[flip][t],
+                *bases[-1:],
+                specs=[VMEM] * 4 + [ANY] * len(bases[-1:]),
+            )
         )
-
-    one, two = first(0, straight), first(1, across)
     v_high, v_low = call(
         rows_kernel, (sds(height, nb, dtype=BF16), sds(height, nb, dtype=BF16)), vecs, t_factor
     )
 
-    parts = []
-    for t in range(ratio - 1):
-        parts = [
-            call(
-                functools.partial(part_kernel, t, rows),
-                sds(nb, nb),
-                vecs,
-                straight[t],
-                across[t],
-                *parts,
-            )
-        ]
     keep, give = call(
-        functools.partial(cut_kernel, ratio - 1, rows),
-        (sds(nb // 2, nb), sds(nb // 2, nb)),
+        functools.partial(part_kernel, rows),
+        (sds(3 * nb // 4, nb // 2), sds(3 * nb // 4, nb // 2)),
         vecs,
-        straight[-1],
-        across[-1],
-        *parts,
+        *straight,
         scratch=[pltpu.VMEM((nb, nb), F32)],
     )
-    share = call(add_kernel, sds(nb // 2, nb), keep, move(give, other_core))
-    others = [move(share, lambda r, c, s=s: (r ^ (2 * s), c)) for s in range(1, ys)]
-    ready = (one, two, v_high)
-    share = call(
-        functools.partial(late_add_kernel, len(ready)),
-        sds(nb // 2, nb),
-        *ready,
-        share,
-        *others,
-        specs=[ANY] * len(ready) + [VMEM] * ys,
-    )
+    share = late_add((), keep, move(give, other_core))
+    share = late_add(bases[ratio : ratio + 1], share, *[move(share, lambda r, c, s=s: (r ^ (2 * s), c)) for s in range(1, ys)])
+    share = late_add((bases[-1], v_high), share, move(share, lambda r, c: (r, c ^ 1)))
     rest = move(share, other_core)
 
     result = pl.pallas_call(
-        functools.partial(last_kernel, nb),
+        functools.partial(last_kernel, places, rows),
         out_shape=sds(height * step, LANES),
-        in_specs=[VMEM] * 10,
+        in_specs=[VMEM] * (8 + len(bases)),
         out_specs=HBM,
         scratch_shapes=[
             pltpu.VMEM((nb, nb), F32),
@@ -334,7 +324,7 @@
             pltpu.SemaphoreType.DMA((block_rows,)),
         ],
         compiler_params=pltpu.CompilerParams(vmem_limit_bytes=32 << 20),
-    )(one, two, v_high, v_low, u_high, u_low, total, other, share, rest)
+    )(v_high, v_low, u_high, u_low, total, other, share, rest, *bases)
     return result.reshape(matrix.shape)
 
 

time: 54.2 us -> 51.5 us (0.950)
  starting transfers between devices: 22.6 us -> 20.4 us
    ppermute x13 -> x14, starting transfers between devices: 22.6 us -> 20.4 us  [send(): return lax.ppermute(value, AXES, pairs)]
    ppermute x13 -> x14, waiting for transfers between devices: 22.1 us -> 21.7 us  [send(): return lax.ppermute(value, AXES, pairs)]
    pallas_call x13 -> x16, Pallas kernels: 6.21 us -> 6.13 us  [call(): pl.pallas_call(kernel, out_shape=outs, in_specs=specs or [VMEM] * len(arg...]
  transfers between devices with their start and end apart: 13 -> 14, of which waited for: 7 -> 7; matrix products, arithmetic and copies ran while one was open for 0% -> 0% of each run, Pallas kernels for 6% -> 7%
where the time goes in v3:
time: 51.5 us; the launch traced here: 51.4 us
  waiting for transfers between devices  21.7 us (42%)
  starting transfers between devices  20.4 us (40%)
  Pallas kernels  9.03 us (18%)
    ppermute x14, waiting for transfers between devices, send(): return lax.ppermute(value, AXES, pairs)  21.7 us
    ppermute x14, starting transfers between devices, send(): return lax.ppermute(value, AXES, pairs)  20.4 us
    pallas_call x16, Pallas kernels, call(): pl.pallas_call(kernel, out_shape=outs, in_specs=specs or [VMEM] * len(arg...  6.13 us
    pallas_call x1, Pallas kernels, per_device(): pl.pallas_call(functools.partial(last_kernel, places, rows), out_shape=sd...  2.9 us
  transfers between devices with their start and end apart: 14, of which 7 were waited for; matrix products, arithmetic and copies ran while one was open for 0% of the time, Pallas kernels for 7%

profile of v3, /device:TPU:0, one launch (start us, length us, event | category | flops | bytes accessed | tf_op | source)
XLA Modules:
  0.0 51.4 jit_solution(4081692720502946397)
XLA Ops:
  0.0 0.0 copy-start.1
  0.0 2.8 %shard_map.38 = (f32[256,256]{1,0:T(8,128)S(1)}, f32[256,256]{1,0:T(8,128)S(1)}) custom-call(f32[4096,128]{1,0:T(8,128)} %bitcast.3, f32[1024,256]{1,0:T(8,128)} %bitcast.8), custom_call_target="tpu_custom_call" | custom-call | tf_op jit(solution)/shard_map/pallas_call | solution.py:37
  2.8 0.5 %collective-permute-start.3 = (f32[256,256]{1,0:T(8,128)S(1)}, f32[256,256]{1,0:T(8,128)S(1)}, u32[]{:S(2)}, u32[]{:S(2)}) collective-permute-start(f32[256,256]{1,0:T(8,128)S(1)} %get-tuple-element.22), channel_id=1, source_target_pairs={{0,8},{1,9},{2,10},{3,11},{4,12},{5,13},{6,14},{7,15},{8,0},{9,1},... | collective-permute-start | bytes 786440 | tf_op jit(solution)/shard_map/ppermute | solution.py:54
  3.3 0.0 copy-done.1
  3.3 0.1 shard_map.39
  3.4 2.0 %collective-permute-start = (f32[256,256]{1,0:T(8,128)S(1)}, f32[256,256]{1,0:T(8,128)S(1)}, u32[]{:S(2)}, u32[]{:S(2)}) collective-permute-start(f32[256,256]{1,0:T(8,128)S(1)} %get-tuple-element.19), channel_id=1, source_target_pairs={{0,8},{4,12},{9,1},{13,5},{18,26},{22,30},{27,19},{31,23}} | collective-permute-start | bytes 786440 | tf_op jit(solution)/shard_map/ppermute | solution.py:54
  5.4 0.0 collective-permute-done.3.refs_1_
  5.4 2.0 %collective-permute-start.4 = (f32[256,256]{1,0:T(8,128)S(1)}, f32[256,256]{1,0:T(8,128)S(1)}, u32[]{:S(2)}, u32[]{:S(2)}) collective-permute-start(f32[256,256]{1,0:T(8,128)S(1)} %shard_map.43.refs_0_), channel_id=1, source_target_pairs={{0,16},{1,17},{2,18},{3,19},{4,20},{5,21},{6,22},{7,23},{8,24},{9,... | collective-permute-start | bytes 786440 | tf_op jit(solution)/shard_map/ppermute | solution.py:54
  7.4 0.0 collective-permute-done.came
  7.5 0.0 copy-start.2
  7.5 0.0 copy-start
  7.5 2.1 %collective-permute-start.1 = (f32[256,256]{1,0:T(8,128)S(1)}, f32[256,256]{1,0:T(8,128)S(1)}, u32[]{:S(2)}, u32[]{:S(2)}) collective-permute-start(f32[256,256]{1,0:T(8,128)S(1)} %shard_map.40.mine), channel_id=1, source_target_pairs={{0,16},{1,17},{4,20},{5,21},{8,24},{9,25},{12,28},{13,29},{18,2},{... | collective-permute-start | bytes 786440 | tf_op jit(solution)/shard_map/ppermute | solution.py:54
  9.6 4.5 %collective-permute-done.4.refs_1_ = f32[256,256]{1,0:T(8,128)S(1)} collective-permute-done((f32[256,256]{1,0:T(8,128)S(1)}, f32[256,256]{1,0:T(8,128)S(1)}, u32[]{:S(2)}, u32[]{:S(2)}) %collective-permute-start.4) | collective-permute-done | bytes 262176 | tf_op jit(solution)/shard_map/ppermute | solution.py:54
  14.1 0.7 %collective-permute-start.8 = (f32[256,256]{1,0:T(8,128)S(1)}, f32[256,256]{1,0:T(8,128)S(1)}, u32[]{:S(2)}, u32[]{:S(2)}) collective-permute-start(f32[256,256]{1,0:T(8,128)S(1)} %shard_map.44.p_mine), channel_id=1, source_target_pairs={{0,0},{1,8},{2,16},{3,24},{4,4},{5,12},{6,20},{7,28},{8,1},{9,9},{... | collective-permute-start | bytes 786440 | tf_op jit(solution)/shard_map/ppermute | solution.py:54
  14.8 7.3 %collective-permute-start.6 = (f32[256,256]{1,0:T(8,128)S(1)}, f32[256,256]{1,0:T(8,128)S(1)}, u32[]{:S(2)}, u32[]{:S(2)}) collective-permute-start(f32[256,256]{1,0:T(8,128)S(1)} %shard_map.44.p_mine), channel_id=1, source_target_pairs={{0,6},{1,14},{2,22},{3,30},{4,2},{5,10},{6,18},{7,26},{8,7},{9,15}... | collective-permute-start | bytes 786440 | tf_op jit(solution)/shard_map/ppermute | solution.py:54
  22.1 0.0 collective-permute-done.1.refs_0_
  22.1 0.1 collective-permute-start.2
  22.2 0.0 collective-permute-done.8.prods.refs_0_
  22.2 3.1 %collective-permute-start.9 = (f32[256,256]{1,0:T(8,128)S(1)}, f32[256,256]{1,0:T(8,128)S(1)}, u32[]{:S(2)}, u32[]{:S(2)}) collective-permute-start(f32[256,256]{1,0:T(8,128)S(1)} %collective-permute-done.8.prods.refs_0_), channel_id=1, source_target_pairs={{0,1},{1,0},{2,3},{3,2},{4,5},{5,4},{6,7},{7,6},{8,9},{9,8},{10,11... | collective-permute-start | bytes 786440 | tf_op jit(solution)/shard_map/ppermute | solution.py:54
  25.3 10.3 %collective-permute-done.6.prods.refs_1_ = f32[256,256]{1,0:T(8,128)S(1)} collective-permute-done((f32[256,256]{1,0:T(8,128)S(1)}, f32[256,256]{1,0:T(8,128)S(1)}, u32[]{:S(2)}, u32[]{:S(2)}) %collective-permute-start.6) | collective-permute-done | bytes 262176 | tf_op jit(solution)/shard_map/ppermute | solution.py:54
  35.6 0.5 shard_map.49
  36.1 0.1 collective-permute-start.10
  36.2 1.1 %collective-permute-start.7 = (f32[256,256]{1,0:T(8,128)S(1)}, f32[256,256]{1,0:T(8,128)S(1)}, u32[]{:S(2)}, u32[]{:S(2)}) collective-permute-start(f32[256,256]{1,0:T(8,128)S(1)} %collective-permute-done.6.prods.refs_1_), channel_id=1, source_target_pairs={{0,1},{1,0},{2,3},{3,2},{4,5},{5,4},{6,7},{7,6},{8,9},{9,8},{10,11... | collective-permute-start | bytes 786440 | tf_op jit(solution)/shard_map/ppermute | solution.py:54
  37.3 0.2 collective-permute-done.10.refs_1_
  37.5 0.1 collective-permute-start.11
  37.5 0.2 collective-permute-start.5
  37.8 0.0 collective-permute-done.2.other
  37.8 0.0 copy-done.2
  37.8 0.4 shard_map.42
  38.2 0.0 collective-permute-done.9.prods
  38.2 0.0 copy-done
  38.2 0.4 shard_map.45.refs_0_
  38.6 0.4 shard_map.46.refs_0_.refs_1_
  39.0 0.4 shard_map.47.refs_0_.refs_2_
  39.4 2.9 %collective-permute-done.11.refs_2_ = f32[192,128]{1,0:T(8,128)S(1)} collective-permute-done((f32[192,128]{1,0:T(8,128)S(1)}, f32[192,128]{1,0:T(8,128)S(1)}, u32[]{:S(2)}, u32[]{:S(2)}) %collective-permute-start.11) | collective-permute-done | bytes 98336 | tf_op jit(solution)/shard_map/ppermute | solution.py:54
  42.4 1.1 %collective-permute-start.12 = (f32[192,128]{1,0:T(8,128)S(1)}, f32[192,128]{1,0:T(8,128)S(1)}, u32[]{:S(2)}, u32[]{:S(2)}) collective-permute-start(f32[192,128]{1,0:T(8,128)S(1)} %shard_map.51.refs_2_), channel_id=1, source_target_pairs={{0,1},{1,0},{2,3},{3,2},{4,5},{5,4},{6,7},{7,6},{8,9},{9,8},{10,11... | collective-permute-start | bytes 294920 | tf_op jit(solution)/shard_map/ppermute | solution.py:54
  43.5 0.6 %shard_map.37 = (bf16[1024,256]{1,0:T(8,128)(2,1)S(1)}, bf16[1024,256]{1,0:T(8,128)(2,1)S(1)}) custom-call(f32[1024,256]{1,0:T(8,128)S(1)} %bitcast.11, f32[256,256]{1,0:T(8,128)S(1)} %copy-done.2), custom_call_target="tpu_custom_call" | custom-call | tf_op jit(solution)/shard_map/pallas_call | solution.py:37
  44.2 1.2 %collective-permute-done.7.prods = f32[256,256]{1,0:T(8,128)S(1)} collective-permute-done((f32[256,256]{1,0:T(8,128)S(1)}, f32[256,256]{1,0:T(8,128)S(1)}, u32[]{:S(2)}, u32[]{:S(2)}) %collective-permute-start.7) | collective-permute-done | bytes 262176 | tf_op jit(solution)/shard_map/ppermute | solution.py:54
  45.3 0.4 shard_map.48.refs_0_.refs_3_
  45.8 1.3 %collective-permute-done.12.refs_3_ = f32[192,128]{1,0:T(8,128)S(1)} collective-permute-done((f32[192,128]{1,0:T(8,128)S(1)}, f32[192,128]{1,0:T(8,128)S(1)}, u32[]{:S(2)}, u32[]{:S(2)}) %collective-permute-start.12) | collective-permute-done | bytes 98336 | tf_op jit(solution)/shard_map/ppermute | solution.py:54
  47.1 0.1 collective-permute-start.13
  47.2 0.0 collective-permute-done.5.p_other
  47.2 1.3 %collective-permute-done.13.s_other = f32[192,128]{1,0:T(8,128)S(1)} collective-permute-done((f32[192,128]{1,0:T(8,128)S(1)}, f32[192,128]{1,0:T(8,128)S(1)}, u32[]{:S(2)}, u32[]{:S(2)}) %collective-permute-start.13) | collective-permute-done | bytes 98336 | tf_op jit(solution)/shard_map/ppermute | solution.py:54
  48.5 2.9 %shard_map.53 = f32[4096,128]{1,0:T(8,128)} custom-call(bf16[1024,256]{1,0:T(8,128)(2,1)S(1)} %get-tuple-element.15.refs_1_.v_high, bf16[1024,256]{1,0:T(8,128)(2,1)S(1)} %get-tuple-element.16.v_low, bf16[512,256]{1,0:T(8,128)(2,1)S(1)} %get-tuple-element.20.u_high, bf16[512,256]{1,0:T(8,128)(2,1)S(1)} %get-tuple-element.21.u_low, ...), custom_call_target="tpu_custom_call" | custom-call | tf_op jit(solution)/shard_map/pallas_call | solution.py:315
  (7 shorter events, 0.2 us)
Async XLA Ops:
  0.0 3.3 %copy-start.1 = (f32[4,1,256,256]{3,2,1,0:T(8,128)S(1)}, f32[4,1,256,256]{3,2,1,0:T(8,128)}, u32[]{:S(2)}) copy-start(f32[4,1,256,256]{3,2,1,0:T(8,128)} %param.4) | copy-start | bytes 3145732
  2.8 2.6 %collective-permute-start.3 = (f32[256,256]{1,0:T(8,128)S(1)}, f32[256,256]{1,0:T(8,128)S(1)}, u32[]{:S(2)}, u32[]{:S(2)}) collective-permute-start(f32[256,256]{1,0:T(8,128)S(1)} %get-tuple-element.22), channel_id=1, source_target_pairs={{0,8},{1,9},{2,10},{3,11},{4,12},{5,13},{6,14},{7,15},{8,0},{9,1},... | collective-permute-start | bytes 786440 | tf_op jit(solution)/shard_map/ppermute | solution.py:54
  3.4 4.1 %collective-permute-start = (f32[256,256]{1,0:T(8,128)S(1)}, f32[256,256]{1,0:T(8,128)S(1)}, u32[]{:S(2)}, u32[]{:S(2)}) collective-permute-start(f32[256,256]{1,0:T(8,128)S(1)} %get-tuple-element.19), channel_id=1, source_target_pairs={{0,8},{4,12},{9,1},{13,5},{18,26},{22,30},{27,19},{31,23}} | collective-permute-start | bytes 786440 | tf_op jit(solution)/shard_map/ppermute | solution.py:54
  5.4 8.7 %collective-permute-start.4 = (f32[256,256]{1,0:T(8,128)S(1)}, f32[256,256]{1,0:T(8,128)S(1)}, u32[]{:S(2)}, u32[]{:S(2)}) collective-permute-start(f32[256,256]{1,0:T(8,128)S(1)} %shard_map.43.refs_0_), channel_id=1, source_target_pairs={{0,16},{1,17},{2,18},{3,19},{4,20},{5,21},{6,22},{7,23},{8,24},{9,... | collective-permute-start | bytes 786440 | tf_op jit(solution)/shard_map/ppermute | solution.py:54
  7.5 30.3 %copy-start.2 = (f32[256,256]{1,0:T(8,128)S(1)}, f32[256,256]{1,0:T(8,128)}, u32[]{:S(2)}) copy-start(f32[256,256]{1,0:T(8,128)} %t_ref.3) | copy-start | bytes 786436
  7.5 30.7 %copy-start = (f32[4,1,256,2,1,256]{5,4,3,2,1,0:T(1,128)S(1)}, f32[4,1,256,2,1,256]{5,4,3,2,1,0:T(1,128)}, u32[]{:S(2)}) copy-start(f32[4,1,256,2,1,256]{5,4,3,2,1,0:T(1,128)} %param.3) | copy-start | bytes 6291460
  7.5 14.6 %collective-permute-start.1 = (f32[256,256]{1,0:T(8,128)S(1)}, f32[256,256]{1,0:T(8,128)S(1)}, u32[]{:S(2)}, u32[]{:S(2)}) collective-permute-start(f32[256,256]{1,0:T(8,128)S(1)} %shard_map.40.mine), channel_id=1, source_target_pairs={{0,16},{1,17},{4,20},{5,21},{8,24},{9,25},{12,28},{13,29},{18,2},{... | collective-permute-start | bytes 786440 | tf_op jit(solution)/shard_map/ppermute | solution.py:54
  14.1 8.1 %collective-permute-start.8 = (f32[256,256]{1,0:T(8,128)S(1)}, f32[256,256]{1,0:T(8,128)S(1)}, u32[]{:S(2)}, u32[]{:S(2)}) collective-permute-start(f32[256,256]{1,0:T(8,128)S(1)} %shard_map.44.p_mine), channel_id=1, source_target_pairs={{0,0},{1,8},{2,16},{3,24},{4,4},{5,12},{6,20},{7,28},{8,1},{9,9},{... | collective-permute-start | bytes 786440 | tf_op jit(solution)/shard_map/ppermute | solution.py:54
  14.8 20.8 %collective-permute-start.6 = (f32[256,256]{1,0:T(8,128)S(1)}, f32[256,256]{1,0:T(8,128)S(1)}, u32[]{:S(2)}, u32[]{:S(2)}) collective-permute-start(f32[256,256]{1,0:T(8,128)S(1)} %shard_map.44.p_mine), channel_id=1, source_target_pairs={{0,6},{1,14},{2,22},{3,30},{4,2},{5,10},{6,18},{7,26},{8,7},{9,15}... | collective-permute-start | bytes 786440 | tf_op jit(solution)/shard_map/ppermute | solution.py:54
  22.1 15.6 %collective-permute-start.2 = (f32[256,256]{1,0:T(8,128)S(1)}, f32[256,256]{1,0:T(8,128)S(1)}, u32[]{:S(2)}, u32[]{:S(2)}) collective-permute-start(f32[256,256]{1,0:T(8,128)S(1)} %shard_map.41.mine), channel_id=1, source_target_pairs={{0,8},{1,9},{2,10},{3,11},{4,12},{5,13},{6,14},{7,15},{8,0},{9,1},... | collective-permute-start | bytes 786440 | tf_op jit(solution)/shard_map/ppermute | solution.py:54
  22.2 16.0 %collective-permute-start.9 = (f32[256,256]{1,0:T(8,128)S(1)}, f32[256,256]{1,0:T(8,128)S(1)}, u32[]{:S(2)}, u32[]{:S(2)}) collective-permute-start(f32[256,256]{1,0:T(8,128)S(1)} %collective-permute-done.8.prods.refs_0_), channel_id=1, source_target_pairs={{0,1},{1,0},{2,3},{3,2},{4,5},{5,4},{6,7},{7,6},{8,9},{9,8},{10,11... | collective-permute-start | bytes 786440 | tf_op jit(solution)/shard_map/ppermute | solution.py:54
  36.1 1.4 %collective-permute-start.10 = (f32[192,128]{1,0:T(8,128)S(1)}, f32[192,128]{1,0:T(8,128)S(1)}, u32[]{:S(2)}, u32[]{:S(2)}) collective-permute-start(f32[192,128]{1,0:T(8,128)S(1)} %get-tuple-element.24), channel_id=1, source_target_pairs={{0,8},{1,9},{2,10},{3,11},{4,12},{5,13},{6,14},{7,15},{8,0},{9,1},... | collective-permute-start | bytes 294920 | tf_op jit(solution)/shard_map/ppermute | solution.py:54
  36.2 9.2 %collective-permute-start.7 = (f32[256,256]{1,0:T(8,128)S(1)}, f32[256,256]{1,0:T(8,128)S(1)}, u32[]{:S(2)}, u32[]{:S(2)}) collective-permute-start(f32[256,256]{1,0:T(8,128)S(1)} %collective-permute-done.6.prods.refs_1_), channel_id=1, source_target_pairs={{0,1},{1,0},{2,3},{3,2},{4,5},{5,4},{6,7},{7,6},{8,9},{9,8},{10,11... | collective-permute-start | bytes 786440 | tf_op jit(solution)/shard_map/ppermute | solution.py:54
  37.5 4.9 %collective-permute-start.11 = (f32[192,128]{1,0:T(8,128)S(1)}, f32[192,128]{1,0:T(8,128)S(1)}, u32[]{:S(2)}, u32[]{:S(2)}) collective-permute-start(f32[192,128]{1,0:T(8,128)S(1)} %shard_map.50.refs_1_), channel_id=1, source_target_pairs={{0,16},{1,17},{2,18},{3,19},{4,20},{5,21},{6,22},{7,23},{8,24},{9,... | collective-permute-start | bytes 294920 | tf_op jit(solution)/shard_map/ppermute | solution.py:54
  37.5 9.6 %collective-permute-start.5 = (f32[256,256]{1,0:T(8,128)S(1)}, f32[256,256]{1,0:T(8,128)S(1)}, u32[]{:S(2)}, u32[]{:S(2)}) collective-permute-start(f32[256,256]{1,0:T(8,128)S(1)} %shard_map.44.p_mine), channel_id=1, source_target_pairs={{0,8},{1,9},{2,10},{3,11},{4,12},{5,13},{6,14},{7,15},{8,0},{9,1},... | collective-permute-start | bytes 786440 | tf_op jit(solution)/shard_map/ppermute | solution.py:54
  42.4 4.7 %collective-permute-start.12 = (f32[192,128]{1,0:T(8,128)S(1)}, f32[192,128]{1,0:T(8,128)S(1)}, u32[]{:S(2)}, u32[]{:S(2)}) collective-permute-start(f32[192,128]{1,0:T(8,128)S(1)} %shard_map.51.refs_2_), channel_id=1, source_target_pairs={{0,1},{1,0},{2,3},{3,2},{4,5},{5,4},{6,7},{7,6},{8,9},{9,8},{10,11... | collective-permute-start | bytes 294920 | tf_op jit(solution)/shard_map/ppermute | solution.py:54
  47.1 1.4 %collective-permute-start.13 = (f32[192,128]{1,0:T(8,128)S(1)}, f32[192,128]{1,0:T(8,128)S(1)}, u32[]{:S(2)}, u32[]{:S(2)}) collective-permute-start(f32[192,128]{1,0:T(8,128)S(1)} %shard_map.52.s_mine), channel_id=1, source_target_pairs={{0,8},{1,9},{2,10},{3,11},{4,12},{5,13},{6,14},{7,15},{8,0},{9,1},... | collective-permute-start | bytes 294920 | tf_op jit(solution)/shard_map/ppermute | solution.py:54

commit v4 on v3

--- a/solution.py
+++ b/solution.py
@@ -99,6 +99,20 @@
     for term in terms[1:]:
         total = total + term[...]
     out[...] = total
+
+
+def total_kernel(*refs):
+    *terms, out, upper, lower = refs
+    add_kernel(*terms, out)
+    half = upper.shape[0]
+    upper[...] = out[:half]
+    lower[...] = out[half:]
+
+
+def join_kernel(upper, lower, out):
+    half = upper.shape[0]
+    out[:half] = upper[...]
+    out[half:] = lower[...]
 
 
 def late_add_kernel(count, *refs):
@@ -256,13 +270,16 @@
     chip = call(add_kernel, sds(half, nb), keep, move(give, other_core))
 
     sums = [move(chip, lambda r, c, s=s: (r ^ (2 * s), c)) for s in range(1, ys)]
-    total = call(add_kernel, sds(half, nb), chip, *sums)
+    total, *halves = call(total_kernel, [sds(half, nb)] + [sds(half // 2, nb)] * 2, chip, *sums)
 
     def target(r, c, t):
         group, twin = c // rows, c % rows // 2
         return twin * 2 + c % 2, (group ^ t) * rows + (r ^ (2 * t))
 
-    straight = [move(total, lambda r, c, t=t: target(r, c, t)) for t in range(ratio)]
+    straight = [move(total, lambda r, c, t=t: target(r, c, t)) for t in range(1, ratio)]
+    straight.insert(
+        0, call(join_kernel, sds(half, nb), *[move(value, lambda r, c: target(r, c, 0)) for value in halves])
+    )
     across = [move(value, lambda r, c: (r, c ^ 1)) for value in straight]
 
     own = call(functools.partial(own_kernel, rows), [sds(nb, nb)] * 2, keep, vecs, specs=[ANY, VMEM])

time: 51.5 us -> 50.6 us (0.983)
  the two profiles are of different devices: /device:TPU:0 before, /device:TPU:9 now
where the time goes in v4:
time: 50.6 us; the launch traced here: 50.4 us
  starting transfers between devices  22.6 us (45%)
  waiting for transfers between devices  18.5 us (37%)
  Pallas kernels  9.06 us (18%)
    ppermute x15, starting transfers between devices, send(): return lax.ppermute(value, AXES, pairs)  22.6 us
    ppermute x15, waiting for transfers between devices, send(): return lax.ppermute(value, AXES, pairs)  18.5 us
    pallas_call x17, Pallas kernels, call(): pl.pallas_call(kernel, out_shape=outs, in_specs=specs or [VMEM] * len(arg...  6.16 us
    pallas_call x1, Pallas kernels, per_device(): pl.pallas_call(functools.partial(last_kernel, places, rows), out_shape=sd...  2.9 us
  transfers between devices with their start and end apart: 15, of which 9 were waited for; matrix products, arithmetic and copies ran while one was open for 0% of the time, Pallas kernels for 7%

profile of v4, /device:TPU:9, one launch (start us, length us, event | category | flops | bytes accessed | tf_op | source)
XLA Modules:
  0.0 50.4 jit_solution(10160460942180919844)
XLA Ops:
  0.0 0.0 copy-start.1
  0.0 2.8 %shard_map.38 = (f32[256,256]{1,0:T(8,128)S(1)}, f32[256,256]{1,0:T(8,128)S(1)}) custom-call(f32[4096,128]{1,0:T(8,128)} %bitcast.3, f32[1024,256]{1,0:T(8,128)} %bitcast.8), custom_call_target="tpu_custom_call" | custom-call | tf_op jit(solution)/shard_map/pallas_call | solution.py:37
  2.8 0.7 %collective-permute-start.3 = (f32[256,256]{1,0:T(8,128)S(1)}, f32[256,256]{1,0:T(8,128)S(1)}, u32[]{:S(2)}, u32[]{:S(2)}) collective-permute-start(f32[256,256]{1,0:T(8,128)S(1)} %get-tuple-element.25), channel_id=1, source_target_pairs={{0,8},{1,9},{2,10},{3,11},{4,12},{5,13},{6,14},{7,15},{8,0},{9,1},... | collective-permute-start | bytes 786440 | tf_op jit(solution)/shard_map/ppermute | solution.py:54
  3.5 0.0 copy-done.1
  3.5 0.1 shard_map.39
  3.6 0.7 %collective-permute-start = (f32[256,256]{1,0:T(8,128)S(1)}, f32[256,256]{1,0:T(8,128)S(1)}, u32[]{:S(2)}, u32[]{:S(2)}) collective-permute-start(f32[256,256]{1,0:T(8,128)S(1)} %get-tuple-element.22), channel_id=1, source_target_pairs={{0,8},{4,12},{9,1},{13,5},{18,26},{22,30},{27,19},{31,23}} | collective-permute-start | bytes 786440 | tf_op jit(solution)/shard_map/ppermute | solution.py:54
  4.3 0.4 collective-permute-done.3.refs_1_
  4.7 1.5 %collective-permute-start.4 = (f32[256,256]{1,0:T(8,128)S(1)}, f32[256,256]{1,0:T(8,128)S(1)}, u32[]{:S(2)}, u32[]{:S(2)}) collective-permute-start(f32[256,256]{1,0:T(8,128)S(1)} %shard_map.43.refs_0_), channel_id=1, source_target_pairs={{0,16},{1,17},{2,18},{3,19},{4,20},{5,21},{6,22},{7,23},{8,24},{9,... | collective-permute-start | bytes 786440 | tf_op jit(solution)/shard_map/ppermute | solution.py:54
  6.3 0.0 collective-permute-done.came
  6.3 0.0 copy-start.2
  6.3 1.4 %collective-permute-start.1 = (f32[256,256]{1,0:T(8,128)S(1)}, f32[256,256]{1,0:T(8,128)S(1)}, u32[]{:S(2)}, u32[]{:S(2)}) collective-permute-start(f32[256,256]{1,0:T(8,128)S(1)} %shard_map.40.mine), channel_id=1, source_target_pairs={{0,16},{1,17},{4,20},{5,21},{8,24},{9,25},{12,28},{13,29},{18,2},{... | collective-permute-start | bytes 786440 | tf_op jit(solution)/shard_map/ppermute | solution.py:54
  7.7 4.0 %collective-permute-done.4.refs_1_ = f32[256,256]{1,0:T(8,128)S(1)} collective-permute-done((f32[256,256]{1,0:T(8,128)S(1)}, f32[256,256]{1,0:T(8,128)S(1)}, u32[]{:S(2)}, u32[]{:S(2)}) %collective-permute-start.4) | collective-permute-done | bytes 262176 | tf_op jit(solution)/shard_map/ppermute | solution.py:54
  11.8 0.0 copy-start
  11.8 6.7 %collective-permute-start.6 = (f32[256,256]{1,0:T(8,128)S(1)}, f32[256,256]{1,0:T(8,128)S(1)}, u32[]{:S(2)}, u32[]{:S(2)}) collective-permute-start(f32[256,256]{1,0:T(8,128)S(1)} %get-tuple-element.26.p_mine), channel_id=1, source_target_pairs={{0,6},{1,14},{2,22},{3,30},{4,2},{5,10},{6,18},{7,26},{8,7},{9,15}... | collective-permute-start | bytes 786440 | tf_op jit(solution)/shard_map/ppermute | solution.py:54
  18.5 1.9 %collective-permute-start.8 = (f32[128,256]{1,0:T(8,128)S(1)}, f32[128,256]{1,0:T(8,128)S(1)}, u32[]{:S(2)}, u32[]{:S(2)}) collective-permute-start(f32[128,256]{1,0:T(8,128)S(1)} %get-tuple-element.27), channel_id=1, source_target_pairs={{0,0},{1,8},{2,16},{3,24},{4,4},{5,12},{6,20},{7,28},{8,1},{9,9},{... | collective-permute-start | bytes 393224 | tf_op jit(solution)/shard_map/ppermute | solution.py:54
  20.4 5.4 %collective-permute-start.9 = (f32[128,256]{1,0:T(8,128)S(1)}, f32[128,256]{1,0:T(8,128)S(1)}, u32[]{:S(2)}, u32[]{:S(2)}) collective-permute-start(f32[128,256]{1,0:T(8,128)S(1)} %get-tuple-element.28), channel_id=1, source_target_pairs={{0,0},{1,8},{2,16},{3,24},{4,4},{5,12},{6,20},{7,28},{8,1},{9,9},{... | collective-permute-start | bytes 393224 | tf_op jit(solution)/shard_map/ppermute | solution.py:54
  25.8 0.0 collective-permute-done.1.refs_0_
  25.9 0.1 collective-permute-start.2
  26.0 1.9 %collective-permute-done.8.upper = f32[128,256]{1,0:T(8,128)S(1)} collective-permute-done((f32[128,256]{1,0:T(8,128)S(1)}, f32[128,256]{1,0:T(8,128)S(1)}, u32[]{:S(2)}, u32[]{:S(2)}) %collective-permute-start.8) | collective-permute-done | bytes 131104 | tf_op jit(solution)/shard_map/ppermute | solution.py:54
  27.9 2.1 %collective-permute-done.9.lower = f32[128,256]{1,0:T(8,128)S(1)} collective-permute-done((f32[128,256]{1,0:T(8,128)S(1)}, f32[128,256]{1,0:T(8,128)S(1)}, u32[]{:S(2)}, u32[]{:S(2)}) %collective-permute-start.9) | collective-permute-done | bytes 131104 | tf_op jit(solution)/shard_map/ppermute | solution.py:54
  30.0 0.1 collective-permute-start.10
  30.0 0.0 collective-permute-done.6.prods.refs_1_
  30.1 0.5 shard_map.50
  30.5 2.3 %collective-permute-start.11 = (f32[192,128]{1,0:T(8,128)S(1)}, f32[192,128]{1,0:T(8,128)S(1)}, u32[]{:S(2)}, u32[]{:S(2)}) collective-permute-start(f32[192,128]{1,0:T(8,128)S(1)} %get-tuple-element.30), channel_id=1, source_target_pairs={{0,8},{1,9},{2,10},{3,11},{4,12},{5,13},{6,14},{7,15},{8,0},{9,1},... | collective-permute-start | bytes 294920 | tf_op jit(solution)/shard_map/ppermute | solution.py:54
  32.8 0.0 collective-permute-start.7
  32.8 0.9 %collective-permute-done.11.refs_1_ = f32[192,128]{1,0:T(8,128)S(1)} collective-permute-done((f32[192,128]{1,0:T(8,128)S(1)}, f32[192,128]{1,0:T(8,128)S(1)}, u32[]{:S(2)}, u32[]{:S(2)}) %collective-permute-start.11) | collective-permute-done | bytes 98336 | tf_op jit(solution)/shard_map/ppermute | solution.py:54
  33.8 0.1 collective-permute-start.12
  33.9 0.4 collective-permute-start.5
  34.3 0.0 collective-permute-done.2.other
  34.3 0.0 copy-done.2
  34.3 0.4 shard_map.42
  34.7 2.9 %collective-permute-done.10.prods = f32[256,256]{1,0:T(8,128)S(1)} collective-permute-done((f32[256,256]{1,0:T(8,128)S(1)}, f32[256,256]{1,0:T(8,128)S(1)}, u32[]{:S(2)}, u32[]{:S(2)}) %collective-permute-start.10) | collective-permute-done | bytes 262176 | tf_op jit(solution)/shard_map/ppermute | solution.py:54
  37.6 0.0 copy-done
  37.6 0.4 shard_map.46.refs_0_
  38.0 0.4 shard_map.47.refs_0_.refs_1_
  38.4 0.4 shard_map.48.refs_0_.refs_2_
  38.8 0.0 collective-permute-done.12.refs_2_
  38.8 0.1 collective-permute-start.13
  38.9 0.6 %shard_map.37 = (bf16[1024,256]{1,0:T(8,128)(2,1)S(1)}, bf16[1024,256]{1,0:T(8,128)(2,1)S(1)}) custom-call(f32[1024,256]{1,0:T(8,128)S(1)} %bitcast.11, f32[256,256]{1,0:T(8,128)S(1)} %copy-done.2), custom_call_target="tpu_custom_call" | custom-call | tf_op jit(solution)/shard_map/pallas_call | solution.py:37
  39.5 3.7 %collective-permute-done.7.prods = f32[256,256]{1,0:T(8,128)S(1)} collective-permute-done((f32[256,256]{1,0:T(8,128)S(1)}, f32[256,256]{1,0:T(8,128)S(1)}, u32[]{:S(2)}, u32[]{:S(2)}) %collective-permute-start.7) | collective-permute-done | bytes 262176 | tf_op jit(solution)/shard_map/ppermute | solution.py:54
  43.2 0.4 shard_map.49.refs_0_.refs_3_
  43.6 1.7 %collective-permute-done.13.refs_3_ = f32[192,128]{1,0:T(8,128)S(1)} collective-permute-done((f32[192,128]{1,0:T(8,128)S(1)}, f32[192,128]{1,0:T(8,128)S(1)}, u32[]{:S(2)}, u32[]{:S(2)}) %collective-permute-start.13) | collective-permute-done | bytes 98336 | tf_op jit(solution)/shard_map/ppermute | solution.py:54
  45.3 1.3 %collective-permute-start.14 = (f32[192,128]{1,0:T(8,128)S(1)}, f32[192,128]{1,0:T(8,128)S(1)}, u32[]{:S(2)}, u32[]{:S(2)}) collective-permute-start(f32[192,128]{1,0:T(8,128)S(1)} %shard_map.53.s_mine), channel_id=1, source_target_pairs={{0,8},{1,9},{2,10},{3,11},{4,12},{5,13},{6,14},{7,15},{8,0},{9,1},... | collective-permute-start | bytes 294920 | tf_op jit(solution)/shard_map/ppermute | solution.py:54
  46.6 0.0 collective-permute-done.5.p_other
  46.6 0.9 %collective-permute-done.14.s_other = f32[192,128]{1,0:T(8,128)S(1)} collective-permute-done((f32[192,128]{1,0:T(8,128)S(1)}, f32[192,128]{1,0:T(8,128)S(1)}, u32[]{:S(2)}, u32[]{:S(2)}) %collective-permute-start.14) | collective-permute-done | bytes 98336 | tf_op jit(solution)/shard_map/ppermute | solution.py:54
  47.5 2.9 %shard_map.54 = f32[4096,128]{1,0:T(8,128)} custom-call(bf16[1024,256]{1,0:T(8,128)(2,1)S(1)} %get-tuple-element.18.refs_1_.v_high, bf16[1024,256]{1,0:T(8,128)(2,1)S(1)} %get-tuple-element.19.v_low, bf16[512,256]{1,0:T(8,128)(2,1)S(1)} %get-tuple-element.23.u_high, bf16[512,256]{1,0:T(8,128)(2,1)S(1)} %get-tuple-element.24.u_low, ...), custom_call_target="tpu_custom_call" | custom-call | tf_op jit(solution)/shard_map/pallas_call | solution.py:332
  (8 shorter events, 0.2 us)
Async XLA Ops:
  0.0 3.5 %copy-start.1 = (f32[4,1,256,256]{3,2,1,0:T(8,128)S(1)}, f32[4,1,256,256]{3,2,1,0:T(8,128)}, u32[]{:S(2)}) copy-start(f32[4,1,256,256]{3,2,1,0:T(8,128)} %param.4) | copy-start | bytes 3145732
  2.8 1.9 %collective-permute-start.3 = (f32[256,256]{1,0:T(8,128)S(1)}, f32[256,256]{1,0:T(8,128)S(1)}, u32[]{:S(2)}, u32[]{:S(2)}) collective-permute-start(f32[256,256]{1,0:T(8,128)S(1)} %get-tuple-element.25), channel_id=1, source_target_pairs={{0,8},{1,9},{2,10},{3,11},{4,12},{5,13},{6,14},{7,15},{8,0},{9,1},... | collective-permute-start | bytes 786440 | tf_op jit(solution)/shard_map/ppermute | solution.py:54
  3.6 2.7 %collective-permute-start = (f32[256,256]{1,0:T(8,128)S(1)}, f32[256,256]{1,0:T(8,128)S(1)}, u32[]{:S(2)}, u32[]{:S(2)}) collective-permute-start(f32[256,256]{1,0:T(8,128)S(1)} %get-tuple-element.22), channel_id=1, source_target_pairs={{0,8},{4,12},{9,1},{13,5},{18,26},{22,30},{27,19},{31,23}} | collective-permute-start | bytes 786440 | tf_op jit(solution)/shard_map/ppermute | solution.py:54
  4.7 7.0 %collective-permute-start.4 = (f32[256,256]{1,0:T(8,128)S(1)}, f32[256,256]{1,0:T(8,128)S(1)}, u32[]{:S(2)}, u32[]{:S(2)}) collective-permute-start(f32[256,256]{1,0:T(8,128)S(1)} %shard_map.43.refs_0_), channel_id=1, source_target_pairs={{0,16},{1,17},{2,18},{3,19},{4,20},{5,21},{6,22},{7,23},{8,24},{9,... | collective-permute-start | bytes 786440 | tf_op jit(solution)/shard_map/ppermute | solution.py:54
  6.3 28.0 %copy-start.2 = (f32[256,256]{1,0:T(8,128)S(1)}, f32[256,256]{1,0:T(8,128)}, u32[]{:S(2)}) copy-start(f32[256,256]{1,0:T(8,128)} %t_ref.3) | copy-start | bytes 786436
  6.3 19.5 %collective-permute-start.1 = (f32[256,256]{1,0:T(8,128)S(1)}, f32[256,256]{1,0:T(8,128)S(1)}, u32[]{:S(2)}, u32[]{:S(2)}) collective-permute-start(f32[256,256]{1,0:T(8,128)S(1)} %shard_map.40.mine), channel_id=1, source_target_pairs={{0,16},{1,17},{4,20},{5,21},{8,24},{9,25},{12,28},{13,29},{18,2},{... | collective-permute-start | bytes 786440 | tf_op jit(solution)/shard_map/ppermute | solution.py:54
  11.8 25.8 %copy-start = (f32[4,1,256,2,1,256]{5,4,3,2,1,0:T(1,128)S(1)}, f32[4,1,256,2,1,256]{5,4,3,2,1,0:T(1,128)}, u32[]{:S(2)}) copy-start(f32[4,1,256,2,1,256]{5,4,3,2,1,0:T(1,128)} %param.3) | copy-start | bytes 6291460
  11.8 18.2 %collective-permute-start.6 = (f32[256,256]{1,0:T(8,128)S(1)}, f32[256,256]{1,0:T(8,128)S(1)}, u32[]{:S(2)}, u32[]{:S(2)}) collective-permute-start(f32[256,256]{1,0:T(8,128)S(1)} %get-tuple-element.26.p_mine), channel_id=1, source_target_pairs={{0,6},{1,14},{2,22},{3,30},{4,2},{5,10},{6,18},{7,26},{8,7},{9,15}... | collective-permute-start | bytes 786440 | tf_op jit(solution)/shard_map/ppermute | solution.py:54
  18.5 9.4 %collective-permute-start.8 = (f32[128,256]{1,0:T(8,128)S(1)}, f32[128,256]{1,0:T(8,128)S(1)}, u32[]{:S(2)}, u32[]{:S(2)}) collective-permute-start(f32[128,256]{1,0:T(8,128)S(1)} %get-tuple-element.27), channel_id=1, source_target_pairs={{0,0},{1,8},{2,16},{3,24},{4,4},{5,12},{6,20},{7,28},{8,1},{9,9},{... | collective-permute-start | bytes 393224 | tf_op jit(solution)/shard_map/ppermute | solution.py:54
  20.4 9.6 %collective-permute-start.9 = (f32[128,256]{1,0:T(8,128)S(1)}, f32[128,256]{1,0:T(8,128)S(1)}, u32[]{:S(2)}, u32[]{:S(2)}) collective-permute-start(f32[128,256]{1,0:T(8,128)S(1)} %get-tuple-element.28), channel_id=1, source_target_pairs={{0,0},{1,8},{2,16},{3,24},{4,4},{5,12},{6,20},{7,28},{8,1},{9,9},{... | collective-permute-start | bytes 393224 | tf_op jit(solution)/shard_map/ppermute | solution.py:54
  25.9 8.4 %collective-permute-start.2 = (f32[256,256]{1,0:T(8,128)S(1)}, f32[256,256]{1,0:T(8,128)S(1)}, u32[]{:S(2)}, u32[]{:S(2)}) collective-permute-start(f32[256,256]{1,0:T(8,128)S(1)} %shard_map.41.mine), channel_id=1, source_target_pairs={{0,8},{1,9},{2,10},{3,11},{4,12},{5,13},{6,14},{7,15},{8,0},{9,1},... | collective-permute-start | bytes 786440 | tf_op jit(solution)/shard_map/ppermute | solution.py:54
  30.0 7.6 %collective-permute-start.10 = (f32[256,256]{1,0:T(8,128)S(1)}, f32[256,256]{1,0:T(8,128)S(1)}, u32[]{:S(2)}, u32[]{:S(2)}) collective-permute-start(f32[256,256]{1,0:T(8,128)S(1)} %shard_map.45.prods.refs_0_), channel_id=1, source_target_pairs={{0,1},{1,0},{2,3},{3,2},{4,5},{5,4},{6,7},{7,6},{8,9},{9,8},{10,11... | collective-permute-start | bytes 786440 | tf_op jit(solution)/shard_map/ppermute | solution.py:54
  30.5 3.2 %collective-permute-start.11 = (f32[192,128]{1,0:T(8,128)S(1)}, f32[192,128]{1,0:T(8,128)S(1)}, u32[]{:S(2)}, u32[]{:S(2)}) collective-permute-start(f32[192,128]{1,0:T(8,128)S(1)} %get-tuple-element.30), channel_id=1, source_target_pairs={{0,8},{1,9},{2,10},{3,11},{4,12},{5,13},{6,14},{7,15},{8,0},{9,1},... | collective-permute-start | bytes 294920 | tf_op jit(solution)/shard_map/ppermute | solution.py:54
  32.8 10.4 %collective-permute-start.7 = (f32[256,256]{1,0:T(8,128)S(1)}, f32[256,256]{1,0:T(8,128)S(1)}, u32[]{:S(2)}, u32[]{:S(2)}) collective-permute-start(f32[256,256]{1,0:T(8,128)S(1)} %collective-permute-done.6.prods.refs_1_), channel_id=1, source_target_pairs={{0,1},{1,0},{2,3},{3,2},{4,5},{5,4},{6,7},{7,6},{8,9},{9,8},{10,11... | collective-permute-start | bytes 786440 | tf_op jit(solution)/shard_map/ppermute | solution.py:54
  33.8 5.0 %collective-permute-start.12 = (f32[192,128]{1,0:T(8,128)S(1)}, f32[192,128]{1,0:T(8,128)S(1)}, u32[]{:S(2)}, u32[]{:S(2)}) collective-permute-start(f32[192,128]{1,0:T(8,128)S(1)} %shard_map.51.refs_1_), channel_id=1, source_target_pairs={{0,16},{1,17},{2,18},{3,19},{4,20},{5,21},{6,22},{7,23},{8,24},{9,... | collective-permute-start | bytes 294920 | tf_op jit(solution)/shard_map/ppermute | solution.py:54
  33.9 12.7 %collective-permute-start.5 = (f32[256,256]{1,0:T(8,128)S(1)}, f32[256,256]{1,0:T(8,128)S(1)}, u32[]{:S(2)}, u32[]{:S(2)}) collective-permute-start(f32[256,256]{1,0:T(8,128)S(1)} %get-tuple-element.26.p_mine), channel_id=1, source_target_pairs={{0,8},{1,9},{2,10},{3,11},{4,12},{5,13},{6,14},{7,15},{8,0},{9,1},... | collective-permute-start | bytes 786440 | tf_op jit(solution)/shard_map/ppermute | solution.py:54
  38.8 6.5 %collective-permute-start.13 = (f32[192,128]{1,0:T(8,128)S(1)}, f32[192,128]{1,0:T(8,128)S(1)}, u32[]{:S(2)}, u32[]{:S(2)}) collective-permute-start(f32[192,128]{1,0:T(8,128)S(1)} %shard_map.52.refs_2_), channel_id=1, source_target_pairs={{0,1},{1,0},{2,3},{3,2},{4,5},{5,4},{6,7},{7,6},{8,9},{9,8},{10,11... | collective-permute-start | bytes 294920 | tf_op jit(solution)/shard_map/ppermute | solution.py:54
  45.3 2.2 %collective-permute-start.14 = (f32[192,128]{1,0:T(8,128)S(1)}, f32[192,128]{1,0:T(8,128)S(1)}, u32[]{:S(2)}, u32[]{:S(2)}) collective-permute-start(f32[192,128]{1,0:T(8,128)S(1)} %shard_map.53.s_mine), channel_id=1, source_target_pairs={{0,8},{1,9},{2,10},{3,11},{4,12},{5,13},{6,14},{7,15},{8,0},{9,1},... | collective-permute-start | bytes 294920 | tf_op jit(solution)/shard_map/ppermute | solution.py:54

commit v5 on v3

--- a/solution.py
+++ b/solution.py
@@ -101,6 +101,21 @@
     out[...] = total
 
 
+def cut_kernel(keep, came, *parts):
+    y, count = lax.axis_index("row") // 2, parts[0].shape[0]
+    for s, part in enumerate(parts):
+        at = pl.ds((y ^ s) * count, count)
+        part[...] = keep[at, :] + came[at, :]
+
+
+def join_kernel(*refs):
+    *pieces, out = refs
+    count = pieces[0].shape[0]
+    y = lax.axis_index("col") % lax.axis_size("row") // 2
+    for s, piece in enumerate(pieces):
+        out[pl.ds((y ^ s) * count, count), :] = piece[...]
+
+
 def late_add_kernel(count, *refs):
     add_kernel(*refs[count:])
 
@@ -187,8 +202,9 @@
     out[...] = tile_rows(a_ref, at * nb, nb, width, 0, width) - value
 
 
-def last_kernel(places, rows, v_high, v_low, u_high, u_low, p_mine, p_other, s_mine, s_other, *refs):
-    *bases, out, inner, mixed, buf, sem = refs
+def last_kernel(places, rows, v_high, v_low, u_high, u_low, s_mine, s_other, *refs):
+    *refs, out, inner, mixed, buf, sem = refs
+    bases, prods = refs[: len(places)], refs[len(places) :]
     row, col = lax.axis_index("row"), lax.axis_index("col")
     core = row % 2
     half = inner.shape[0] // 2
@@ -200,9 +216,9 @@
     inner[half:, :half] = corner.T
     inner[half:, half:] = second[:half]
     mixed[...] = product((u_high[...], u_low[...]), split(inner[...]), NT)
-    half = p_mine.shape[0]
-    for ref, c in ((p_mine, core), (p_other, 1 - core)):
-        at = pl.ds(c * half, half)
+    count, ys = prods[0].shape[0], len(prods) // 2
+    for k, ref in enumerate(prods):
+        at = pl.ds(((core ^ k // ys) * ys + (row // 2 ^ k % ys)) * count, count)
         mixed[at, :] = mixed[at, :] - ref[...]
     right = split(mixed[...])
     nb, width = bases[0].shape
@@ -253,16 +269,32 @@
         ],
         limit=16,
     )
-    chip = call(add_kernel, sds(half, nb), keep, move(give, other_core))
-
-    sums = [move(chip, lambda r, c, s=s: (r ^ (2 * s), c)) for s in range(1, ys)]
-    total = call(add_kernel, sds(half, nb), chip, *sums)
-
-    def target(r, c, t):
+    piece = half // ys
+    cuts = call(cut_kernel, [sds(piece, nb)] * ys, keep, move(give, other_core))
+
+    def along_y(value):
+        return [move(value, lambda r, c, s=s: (r ^ (2 * s), c)) for s in range(1, ys)]
+
+    total = call(
+        add_kernel,
+        sds(piece, nb),
+        cuts[0],
+        *[move(cut, lambda r, c, s=s: (r ^ (2 * s), c)) for s, cut in enumerate(cuts) if s],
+    )
+    mine = [total, *along_y(total)]
+
+    def target(r, c, t, s):
         group, twin = c // rows, c % rows // 2
-        return twin * 2 + c % 2, (group ^ t) * rows + (r ^ (2 * t))
-
-    straight = [move(total, lambda r, c, t=t: target(r, c, t)) for t in range(ratio)]
+        return twin * 2 + c % 2, (group ^ t) * rows + (r ^ (2 * s))
+
+    straight = [
+        call(
+            join_kernel,
+            sds(half, nb),
+            *[move(total, lambda r, c, t=t, s=s: target(r, c, t, s)) for s in range(ys)],
+        )
+        for t in range(ratio)
+    ]
     across = [move(value, lambda r, c: (r, c ^ 1)) for value in straight]
 
     own = call(functools.partial(own_kernel, rows), [sds(nb, nb)] * 2, keep, vecs, specs=[ANY, VMEM])
@@ -279,9 +311,9 @@
         move(near, other_core),
         t_factor,
     )
-    other = move(total, other_core)
-
-    places = [(1, 0)] + [(0, t) for t in range(ratio)] + [(1, t) for t in range(1, ratio)]
+    other = [move(value, other_core) for value in mine]
+
+    places = [(1, 1)] + [(0, t) for t in range(ratio)] + [(1, t) for t in range(ratio) if t != 1]
     bases = []
     for flip, t in places:
         bases.append(
@@ -308,14 +340,14 @@
         scratch=[pltpu.VMEM((nb, nb), F32)],
     )
     share = late_add((), keep, move(give, other_core))
-    share = late_add(bases[ratio : ratio + 1], share, *[move(share, lambda r, c, s=s: (r ^ (2 * s), c)) for s in range(1, ys)])
+    share = late_add(bases[ratio : ratio + 1], share, *along_y(share))
     share = late_add((bases[-1], v_high), share, move(share, lambda r, c: (r, c ^ 1)))
     rest = move(share, other_core)
 
     result = pl.pallas_call(
         functools.partial(last_kernel, places, rows),
         out_shape=sds(height * step, LANES),
-        in_specs=[VMEM] * (8 + len(bases)),
+        in_specs=[VMEM] * (6 + len(bases) + 2 * ys),
         out_specs=HBM,
         scratch_shapes=[
             pltpu.VMEM((nb, nb), F32),
@@ -324,7 +356,7 @@
             pltpu.SemaphoreType.DMA((block_rows,)),
         ],
         compiler_params=pltpu.CompilerParams(vmem_limit_bytes=32 << 20),
-    )(v_high, v_low, u_high, u_low, total, other, share, rest, *bases)
+    )(v_high, v_low, u_high, u_low, share, rest, *bases, *mine, *other)
     return result.reshape(matrix.shape)
 
 

time: 51.5 us -> 48.3 us (0.938)
  waiting for transfers between devices: 21.7 us -> 13.9 us
  starting transfers between devices: 20.4 us -> 25.1 us
    ppermute x14 -> x18, waiting for transfers between devices: 21.7 us -> 13.9 us  [send(): return lax.ppermute(value, AXES, pairs)]
    ppermute x14 -> x18, starting transfers between devices: 20.4 us -> 25.1 us  [send(): return lax.ppermute(value, AXES, pairs)]
    pallas_call x16 -> x18, Pallas kernels: 6.13 us -> 6.22 us  [call(): pl.pallas_call(kernel, out_shape=outs, in_specs=specs or [VMEM] * len(arg...]
  transfers between devices with their start and end apart: 14 -> 18, of which waited for: 7 -> 8; matrix products, arithmetic and copies ran while one was open for 0% -> 0% of each run, Pallas kernels for 7% -> 7%
where the time goes in v5:
time: 48.3 us; the launch traced here: 48.2 us
  starting transfers between devices  25.1 us (52%)
  waiting for transfers between devices  13.9 us (29%)
  Pallas kernels  9 us (19%)
    ppermute x18, starting transfers between devices, send(): return lax.ppermute(value, AXES, pairs)  25.1 us
    ppermute x18, waiting for transfers between devices, send(): return lax.ppermute(value, AXES, pairs)  13.9 us
    pallas_call x18, Pallas kernels, call(): pl.pallas_call(kernel, out_shape=outs, in_specs=specs or [VMEM] * len(arg...  6.22 us
    pallas_call x1, Pallas kernels, per_device(): pl.pallas_call(functools.partial(last_kernel, places, rows), out_shape=sd...  2.78 us
  transfers between devices with their start and end apart: 18, of which 8 were waited for; matrix products, arithmetic and copies ran while one was open for 0% of the time, Pallas kernels for 7%

profile of v5, /device:TPU:0, one launch (start us, length us, event | category | flops | bytes accessed | tf_op | source)
XLA Modules:
  0.0 48.2 jit_solution(14709023125419822170)
XLA Ops:
  0.0 2.8 %shard_map.38 = (f32[256,256]{1,0:T(8,128)S(1)}, f32[256,256]{1,0:T(8,128)S(1)}) custom-call(f32[4096,128]{1,0:T(8,128)} %bitcast.3, f32[1024,256]{1,0:T(8,128)} %bitcast.8), custom_call_target="tpu_custom_call" | custom-call | tf_op jit(solution)/shard_map/pallas_call | solution.py:37
  2.8 0.5 %collective-permute-start.3 = (f32[256,256]{1,0:T(8,128)S(1)}, f32[256,256]{1,0:T(8,128)S(1)}, u32[]{:S(2)}, u32[]{:S(2)}) collective-permute-start(f32[256,256]{1,0:T(8,128)S(1)} %get-tuple-element.24), channel_id=1, source_target_pairs={{0,8},{1,9},{2,10},{3,11},{4,12},{5,13},{6,14},{7,15},{8,0},{9,1},... | collective-permute-start | bytes 786440 | tf_op jit(solution)/shard_map/ppermute | solution.py:54
  3.3 0.1 shard_map.39
  3.4 2.0 %collective-permute-start = (f32[256,256]{1,0:T(8,128)S(1)}, f32[256,256]{1,0:T(8,128)S(1)}, u32[]{:S(2)}, u32[]{:S(2)}) collective-permute-start(f32[256,256]{1,0:T(8,128)S(1)} %get-tuple-element.21), channel_id=1, source_target_pairs={{0,8},{4,12},{9,1},{13,5},{18,26},{22,30},{27,19},{31,23}} | collective-permute-start | bytes 786440 | tf_op jit(solution)/shard_map/ppermute | solution.py:54
  5.4 0.0 collective-permute-done.3.came
  5.4 2.0 %collective-permute-start.4 = (f32[128,256]{1,0:T(8,128)S(1)}, f32[128,256]{1,0:T(8,128)S(1)}, u32[]{:S(2)}, u32[]{:S(2)}) collective-permute-start(f32[128,256]{1,0:T(8,128)S(1)} %get-tuple-element.26), channel_id=1, source_target_pairs={{0,16},{1,17},{2,18},{3,19},{4,20},{5,21},{6,22},{7,23},{8,24},{9,... | collective-permute-start | bytes 393224 | tf_op jit(solution)/shard_map/ppermute | solution.py:54
  7.4 0.0 collective-permute-done.came
  7.5 0.0 copy-start.2
  7.5 2.1 %collective-permute-start.1 = (f32[256,256]{1,0:T(8,128)S(1)}, f32[256,256]{1,0:T(8,128)S(1)}, u32[]{:S(2)}, u32[]{:S(2)}) collective-permute-start(f32[256,256]{1,0:T(8,128)S(1)} %shard_map.40.mine), channel_id=1, source_target_pairs={{0,16},{1,17},{4,20},{5,21},{8,24},{9,25},{12,28},{13,29},{18,2},{... | collective-permute-start | bytes 786440 | tf_op jit(solution)/shard_map/ppermute | solution.py:54
  9.6 1.6 %collective-permute-done.4.refs_1_ = f32[128,256]{1,0:T(8,128)S(1)} collective-permute-done((f32[128,256]{1,0:T(8,128)S(1)}, f32[128,256]{1,0:T(8,128)S(1)}, u32[]{:S(2)}, u32[]{:S(2)}) %collective-permute-start.4) | collective-permute-done | bytes 131104 | tf_op jit(solution)/shard_map/ppermute | solution.py:54
  11.3 0.0 copy-start
  11.3 3.9 %collective-permute-start.9 = (f32[128,256]{1,0:T(8,128)S(1)}, f32[128,256]{1,0:T(8,128)S(1)}, u32[]{:S(2)}, u32[]{:S(2)}) collective-permute-start(f32[128,256]{1,0:T(8,128)S(1)} %shard_map.44.refs_4_), channel_id=1, source_target_pairs={{0,6},{1,14},{2,22},{3,30},{4,2},{5,10},{6,18},{7,26},{8,7},{9,15}... | collective-permute-start | bytes 393224 | tf_op jit(solution)/shard_map/ppermute | solution.py:54
  15.2 0.0 collective-permute-start.8
  15.2 1.9 %collective-permute-start.6 = (f32[128,256]{1,0:T(8,128)S(1)}, f32[128,256]{1,0:T(8,128)S(1)}, u32[]{:S(2)}, u32[]{:S(2)}) collective-permute-start(f32[128,256]{1,0:T(8,128)S(1)} %shard_map.44.refs_4_), channel_id=1, source_target_pairs={{0,2},{1,10},{2,18},{3,26},{4,6},{5,14},{6,22},{7,30},{8,3},{9,11}... | collective-permute-start | bytes 393224 | tf_op jit(solution)/shard_map/ppermute | solution.py:54
  17.1 0.7 %collective-permute-start.5 = (f32[128,256]{1,0:T(8,128)S(1)}, f32[128,256]{1,0:T(8,128)S(1)}, u32[]{:S(2)}, u32[]{:S(2)}) collective-permute-start(f32[128,256]{1,0:T(8,128)S(1)} %shard_map.44.refs_4_), channel_id=1, source_target_pairs={{0,0},{1,8},{2,16},{3,24},{4,4},{5,12},{6,20},{7,28},{8,1},{9,9},{... | collective-permute-start | bytes 393224 | tf_op jit(solution)/shard_map/ppermute | solution.py:54
  17.8 0.0 collective-permute-done.1.refs_0_
  17.9 3.8 %collective-permute-start.2 = (f32[256,256]{1,0:T(8,128)S(1)}, f32[256,256]{1,0:T(8,128)S(1)}, u32[]{:S(2)}, u32[]{:S(2)}) collective-permute-start(f32[256,256]{1,0:T(8,128)S(1)} %shard_map.41.mine), channel_id=1, source_target_pairs={{0,8},{1,9},{2,10},{3,11},{4,12},{5,13},{6,14},{7,15},{8,0},{9,1},... | collective-permute-start | bytes 786440 | tf_op jit(solution)/shard_map/ppermute | solution.py:54
  21.7 2.4 %collective-permute-done.9.refs_1_ = f32[128,256]{1,0:T(8,128)S(1)} collective-permute-done((f32[128,256]{1,0:T(8,128)S(1)}, f32[128,256]{1,0:T(8,128)S(1)}, u32[]{:S(2)}, u32[]{:S(2)}) %collective-permute-start.9) | collective-permute-done | bytes 131104 | tf_op jit(solution)/shard_map/ppermute | solution.py:54
  24.1 2.9 %collective-permute-done.8.refs_0_ = f32[128,256]{1,0:T(8,128)S(1)} collective-permute-done((f32[128,256]{1,0:T(8,128)S(1)}, f32[128,256]{1,0:T(8,128)S(1)}, u32[]{:S(2)}, u32[]{:S(2)}) %collective-permute-start.8) | collective-permute-done | bytes 131104 | tf_op jit(solution)/shard_map/ppermute | solution.py:54
  27.1 1.9 %collective-permute-start.10 = (f32[256,256]{1,0:T(8,128)S(1)}, f32[256,256]{1,0:T(8,128)S(1)}, u32[]{:S(2)}, u32[]{:S(2)}) collective-permute-start(f32[256,256]{1,0:T(8,128)S(1)} %shard_map.46.prods.refs_1_), channel_id=1, source_target_pairs={{0,1},{1,0},{2,3},{3,2},{4,5},{5,4},{6,7},{7,6},{8,9},{9,8},{10,11... | collective-permute-start | bytes 786440 | tf_op jit(solution)/shard_map/ppermute | solution.py:54
  29.0 0.0 collective-permute-done.6.refs_1_
  29.0 0.0 collective-permute-done.5.refs_0_
  29.0 0.5 shard_map.51
  29.5 0.1 collective-permute-start.11
  29.6 0.8 %collective-permute-start.7 = (f32[256,256]{1,0:T(8,128)S(1)}, f32[256,256]{1,0:T(8,128)S(1)}, u32[]{:S(2)}, u32[]{:S(2)}) collective-permute-start(f32[256,256]{1,0:T(8,128)S(1)} %shard_map.45.prods.refs_0_), channel_id=1, source_target_pairs={{0,1},{1,0},{2,3},{3,2},{4,5},{5,4},{6,7},{7,6},{8,9},{9,8},{10,11... | collective-permute-start | bytes 786440 | tf_op jit(solution)/shard_map/ppermute | solution.py:54
  30.4 0.5 collective-permute-done.11.refs_1_
  30.9 2.6 %collective-permute-start.12 = (f32[192,128]{1,0:T(8,128)S(1)}, f32[192,128]{1,0:T(8,128)S(1)}, u32[]{:S(2)}, u32[]{:S(2)}) collective-permute-start(f32[192,128]{1,0:T(8,128)S(1)} %shard_map.52.refs_1_), channel_id=1, source_target_pairs={{0,16},{1,17},{2,18},{3,19},{4,20},{5,21},{6,22},{7,23},{8,24},{9,... | collective-permute-start | bytes 294920 | tf_op jit(solution)/shard_map/ppermute | solution.py:54
  33.5 0.1 collective-permute-start.15
  33.5 0.0 collective-permute-done.2.other
  33.6 0.4 shard_map.42
  34.0 2.3 %collective-permute-done.10.prods = f32[256,256]{1,0:T(8,128)S(1)} collective-permute-done((f32[256,256]{1,0:T(8,128)S(1)}, f32[256,256]{1,0:T(8,128)S(1)}, u32[]{:S(2)}, u32[]{:S(2)}) %collective-permute-start.10) | collective-permute-done | bytes 262176 | tf_op jit(solution)/shard_map/ppermute | solution.py:54
  36.3 0.4 shard_map.47.refs_0_
  36.7 0.4 shard_map.48.refs_0_.refs_1_
  37.1 0.4 shard_map.49.refs_0_.refs_2_
  37.5 0.0 collective-permute-done.12.refs_2_
  37.6 2.0 %collective-permute-start.13 = (f32[192,128]{1,0:T(8,128)S(1)}, f32[192,128]{1,0:T(8,128)S(1)}, u32[]{:S(2)}, u32[]{:S(2)}) collective-permute-start(f32[192,128]{1,0:T(8,128)S(1)} %shard_map.53.refs_2_), channel_id=1, source_target_pairs={{0,1},{1,0},{2,3},{3,2},{4,5},{5,4},{6,7},{7,6},{8,9},{9,8},{10,11... | collective-permute-start | bytes 294920 | tf_op jit(solution)/shard_map/ppermute | solution.py:54
  39.5 0.0 collective-permute-start.16
  39.5 0.0 collective-permute-done.15.refs_5_
  39.5 0.5 %collective-permute-start.17 = (f32[128,256]{1,0:T(8,128)S(1)}, f32[128,256]{1,0:T(8,128)S(1)}, u32[]{:S(2)}, u32[]{:S(2)}) collective-permute-start(f32[128,256]{1,0:T(8,128)S(1)} %collective-permute-done.15.refs_5_), channel_id=1, source_target_pairs={{0,8},{1,9},{2,10},{3,11},{4,12},{5,13},{6,14},{7,15},{8,0},{9,1},... | collective-permute-start | bytes 393224 | tf_op jit(solution)/shard_map/ppermute | solution.py:54
  40.0 0.6 %shard_map.37 = (bf16[1024,256]{1,0:T(8,128)(2,1)S(1)}, bf16[1024,256]{1,0:T(8,128)(2,1)S(1)}) custom-call(f32[1024,256]{1,0:T(8,128)S(1)} %bitcast.11, f32[256,256]{1,0:T(8,128)S(1)} %copy-done.2), custom_call_target="tpu_custom_call" | custom-call | tf_op jit(solution)/shard_map/pallas_call | solution.py:37
  40.7 1.2 %collective-permute-done.7.prods = f32[256,256]{1,0:T(8,128)S(1)} collective-permute-done((f32[256,256]{1,0:T(8,128)S(1)}, f32[256,256]{1,0:T(8,128)S(1)}, u32[]{:S(2)}, u32[]{:S(2)}) %collective-permute-start.7) | collective-permute-done | bytes 262176 | tf_op jit(solution)/shard_map/ppermute | solution.py:54
  41.9 0.4 shard_map.50.refs_0_.refs_3_
  42.3 1.7 %collective-permute-done.13.refs_3_ = f32[192,128]{1,0:T(8,128)S(1)} collective-permute-done((f32[192,128]{1,0:T(8,128)S(1)}, f32[192,128]{1,0:T(8,128)S(1)}, u32[]{:S(2)}, u32[]{:S(2)}) %collective-permute-start.13) | collective-permute-done | bytes 98336 | tf_op jit(solution)/shard_map/ppermute | solution.py:54
  44.0 0.1 collective-permute-start.14
  44.2 0.0 collective-permute-done.16.refs_6_
  44.2 0.0 collective-permute-done.17.refs_7_
  44.2 1.2 %collective-permute-done.14.s_other = f32[192,128]{1,0:T(8,128)S(1)} collective-permute-done((f32[192,128]{1,0:T(8,128)S(1)}, f32[192,128]{1,0:T(8,128)S(1)}, u32[]{:S(2)}, u32[]{:S(2)}) %collective-permute-start.14) | collective-permute-done | bytes 98336 | tf_op jit(solution)/shard_map/ppermute | solution.py:54
  45.4 2.8 %shard_map.55 = f32[4096,128]{1,0:T(8,128)} custom-call(bf16[1024,256]{1,0:T(8,128)(2,1)S(1)} %get-tuple-element.17.refs_1_.v_high, bf16[1024,256]{1,0:T(8,128)(2,1)S(1)} %get-tuple-element.18.v_low, bf16[512,256]{1,0:T(8,128)(2,1)S(1)} %get-tuple-element.22.u_high, bf16[512,256]{1,0:T(8,128)(2,1)S(1)} %get-tuple-element.23.u_low, ...), custom_call_target="tpu_custom_call" | custom-call | tf_op jit(solution)/shard_map/pallas_call | solution.py:347
  (13 shorter events, 0.3 us)
Async XLA Ops:
  0.0 3.3 %copy-start.1 = (f32[4,1,256,256]{3,2,1,0:T(8,128)S(1)}, f32[4,1,256,256]{3,2,1,0:T(8,128)}, u32[]{:S(2)}) copy-start(f32[4,1,256,256]{3,2,1,0:T(8,128)} %param.4) | copy-start | bytes 3145732
  2.8 2.6 %collective-permute-start.3 = (f32[256,256]{1,0:T(8,128)S(1)}, f32[256,256]{1,0:T(8,128)S(1)}, u32[]{:S(2)}, u32[]{:S(2)}) collective-permute-start(f32[256,256]{1,0:T(8,128)S(1)} %get-tuple-element.24), channel_id=1, source_target_pairs={{0,8},{1,9},{2,10},{3,11},{4,12},{5,13},{6,14},{7,15},{8,0},{9,1},... | collective-permute-start | bytes 786440 | tf_op jit(solution)/shard_map/ppermute | solution.py:54
  3.4 4.1 %collective-permute-start = (f32[256,256]{1,0:T(8,128)S(1)}, f32[256,256]{1,0:T(8,128)S(1)}, u32[]{:S(2)}, u32[]{:S(2)}) collective-permute-start(f32[256,256]{1,0:T(8,128)S(1)} %get-tuple-element.21), channel_id=1, source_target_pairs={{0,8},{4,12},{9,1},{13,5},{18,26},{22,30},{27,19},{31,23}} | collective-permute-start | bytes 786440 | tf_op jit(solution)/shard_map/ppermute | solution.py:54
  5.4 5.8 %collective-permute-start.4 = (f32[128,256]{1,0:T(8,128)S(1)}, f32[128,256]{1,0:T(8,128)S(1)}, u32[]{:S(2)}, u32[]{:S(2)}) collective-permute-start(f32[128,256]{1,0:T(8,128)S(1)} %get-tuple-element.26), channel_id=1, source_target_pairs={{0,16},{1,17},{2,18},{3,19},{4,20},{5,21},{6,22},{7,23},{8,24},{9,... | collective-permute-start | bytes 393224 | tf_op jit(solution)/shard_map/ppermute | solution.py:54
  7.5 26.1 %copy-start.2 = (f32[256,256]{1,0:T(8,128)S(1)}, f32[256,256]{1,0:T(8,128)}, u32[]{:S(2)}) copy-start(f32[256,256]{1,0:T(8,128)} %t_ref.3) | copy-start | bytes 786436
  7.5 10.3 %collective-permute-start.1 = (f32[256,256]{1,0:T(8,128)S(1)}, f32[256,256]{1,0:T(8,128)S(1)}, u32[]{:S(2)}, u32[]{:S(2)}) collective-permute-start(f32[256,256]{1,0:T(8,128)S(1)} %shard_map.40.mine), channel_id=1, source_target_pairs={{0,16},{1,17},{4,20},{5,21},{8,24},{9,25},{12,28},{13,29},{18,2},{... | collective-permute-start | bytes 786440 | tf_op jit(solution)/shard_map/ppermute | solution.py:54
  11.3 25.0 %copy-start = (f32[4,1,256,2,1,256]{5,4,3,2,1,0:T(1,128)S(1)}, f32[4,1,256,2,1,256]{5,4,3,2,1,0:T(1,128)}, u32[]{:S(2)}) copy-start(f32[4,1,256,2,1,256]{5,4,3,2,1,0:T(1,128)} %param.3) | copy-start | bytes 6291460
  11.3 12.8 %collective-permute-start.9 = (f32[128,256]{1,0:T(8,128)S(1)}, f32[128,256]{1,0:T(8,128)S(1)}, u32[]{:S(2)}, u32[]{:S(2)}) collective-permute-start(f32[128,256]{1,0:T(8,128)S(1)} %shard_map.44.refs_4_), channel_id=1, source_target_pairs={{0,6},{1,14},{2,22},{3,30},{4,2},{5,10},{6,18},{7,26},{8,7},{9,15}... | collective-permute-start | bytes 393224 | tf_op jit(solution)/shard_map/ppermute | solution.py:54
  15.2 11.8 %collective-permute-start.8 = (f32[128,256]{1,0:T(8,128)S(1)}, f32[128,256]{1,0:T(8,128)S(1)}, u32[]{:S(2)}, u32[]{:S(2)}) collective-permute-start(f32[128,256]{1,0:T(8,128)S(1)} %shard_map.44.refs_4_), channel_id=1, source_target_pairs={{0,4},{1,12},{2,20},{3,28},{4,0},{5,8},{6,16},{7,24},{8,5},{9,13},... | collective-permute-start | bytes 393224 | tf_op jit(solution)/shard_map/ppermute | solution.py:54
  15.2 13.8 %collective-permute-start.6 = (f32[128,256]{1,0:T(8,128)S(1)}, f32[128,256]{1,0:T(8,128)S(1)}, u32[]{:S(2)}, u32[]{:S(2)}) collective-permute-start(f32[128,256]{1,0:T(8,128)S(1)} %shard_map.44.refs_4_), channel_id=1, source_target_pairs={{0,2},{1,10},{2,18},{3,26},{4,6},{5,14},{6,22},{7,30},{8,3},{9,11}... | collective-permute-start | bytes 393224 | tf_op jit(solution)/shard_map/ppermute | solution.py:54
  17.1 11.8 %collective-permute-start.5 = (f32[128,256]{1,0:T(8,128)S(1)}, f32[128,256]{1,0:T(8,128)S(1)}, u32[]{:S(2)}, u32[]{:S(2)}) collective-permute-start(f32[128,256]{1,0:T(8,128)S(1)} %shard_map.44.refs_4_), channel_id=1, source_target_pairs={{0,0},{1,8},{2,16},{3,24},{4,4},{5,12},{6,20},{7,28},{8,1},{9,9},{... | collective-permute-start | bytes 393224 | tf_op jit(solution)/shard_map/ppermute | solution.py:54
  17.9 15.7 %collective-permute-start.2 = (f32[256,256]{1,0:T(8,128)S(1)}, f32[256,256]{1,0:T(8,128)S(1)}, u32[]{:S(2)}, u32[]{:S(2)}) collective-permute-start(f32[256,256]{1,0:T(8,128)S(1)} %shard_map.41.mine), channel_id=1, source_target_pairs={{0,8},{1,9},{2,10},{3,11},{4,12},{5,13},{6,14},{7,15},{8,0},{9,1},... | collective-permute-start | bytes 786440 | tf_op jit(solution)/shard_map/ppermute | solution.py:54
  27.1 9.2 %collective-permute-start.10 = (f32[256,256]{1,0:T(8,128)S(1)}, f32[256,256]{1,0:T(8,128)S(1)}, u32[]{:S(2)}, u32[]{:S(2)}) collective-permute-start(f32[256,256]{1,0:T(8,128)S(1)} %shard_map.46.prods.refs_1_), channel_id=1, source_target_pairs={{0,1},{1,0},{2,3},{3,2},{4,5},{5,4},{6,7},{7,6},{8,9},{9,8},{10,11... | collective-permute-start | bytes 786440 | tf_op jit(solution)/shard_map/ppermute | solution.py:54
  29.5 1.4 %collective-permute-start.11 = (f32[192,128]{1,0:T(8,128)S(1)}, f32[192,128]{1,0:T(8,128)S(1)}, u32[]{:S(2)}, u32[]{:S(2)}) collective-permute-start(f32[192,128]{1,0:T(8,128)S(1)} %get-tuple-element.28), channel_id=1, source_target_pairs={{0,8},{1,9},{2,10},{3,11},{4,12},{5,13},{6,14},{7,15},{8,0},{9,1},... | collective-permute-start | bytes 294920 | tf_op jit(solution)/shard_map/ppermute | solution.py:54
  29.6 12.3 %collective-permute-start.7 = (f32[256,256]{1,0:T(8,128)S(1)}, f32[256,256]{1,0:T(8,128)S(1)}, u32[]{:S(2)}, u32[]{:S(2)}) collective-permute-start(f32[256,256]{1,0:T(8,128)S(1)} %shard_map.45.prods.refs_0_), channel_id=1, source_target_pairs={{0,1},{1,0},{2,3},{3,2},{4,5},{5,4},{6,7},{7,6},{8,9},{9,8},{10,11... | collective-permute-start | bytes 786440 | tf_op jit(solution)/shard_map/ppermute | solution.py:54
  30.9 6.7 %collective-permute-start.12 = (f32[192,128]{1,0:T(8,128)S(1)}, f32[192,128]{1,0:T(8,128)S(1)}, u32[]{:S(2)}, u32[]{:S(2)}) collective-permute-start(f32[192,128]{1,0:T(8,128)S(1)} %shard_map.52.refs_1_), channel_id=1, source_target_pairs={{0,16},{1,17},{2,18},{3,19},{4,20},{5,21},{6,22},{7,23},{8,24},{9,... | collective-permute-start | bytes 294920 | tf_op jit(solution)/shard_map/ppermute | solution.py:54
  33.5 6.1 %collective-permute-start.15 = (f32[128,256]{1,0:T(8,128)S(1)}, f32[128,256]{1,0:T(8,128)S(1)}, u32[]{:S(2)}, u32[]{:S(2)}) collective-permute-start(f32[128,256]{1,0:T(8,128)S(1)} %shard_map.44.refs_4_), channel_id=1, source_target_pairs={{0,16},{1,17},{2,18},{3,19},{4,20},{5,21},{6,22},{7,23},{8,24},{9,... | collective-permute-start | bytes 393224 | tf_op jit(solution)/shard_map/ppermute | solution.py:54
  37.6 6.4 %collective-permute-start.13 = (f32[192,128]{1,0:T(8,128)S(1)}, f32[192,128]{1,0:T(8,128)S(1)}, u32[]{:S(2)}, u32[]{:S(2)}) collective-permute-start(f32[192,128]{1,0:T(8,128)S(1)} %shard_map.53.refs_2_), channel_id=1, source_target_pairs={{0,1},{1,0},{2,3},{3,2},{4,5},{5,4},{6,7},{7,6},{8,9},{9,8},{10,11... | collective-permute-start | bytes 294920 | tf_op jit(solution)/shard_map/ppermute | solution.py:54
  39.5 4.6 %collective-permute-start.16 = (f32[128,256]{1,0:T(8,128)S(1)}, f32[128,256]{1,0:T(8,128)S(1)}, u32[]{:S(2)}, u32[]{:S(2)}) collective-permute-start(f32[128,256]{1,0:T(8,128)S(1)} %shard_map.44.refs_4_), channel_id=1, source_target_pairs={{0,8},{1,9},{2,10},{3,11},{4,12},{5,13},{6,14},{7,15},{8,0},{9,1},... | collective-permute-start | bytes 393224 | tf_op jit(solution)/shard_map/ppermute | solution.py:54
  39.5 4.6 %collective-permute-start.17 = (f32[128,256]{1,0:T(8,128)S(1)}, f32[128,256]{1,0:T(8,128)S(1)}, u32[]{:S(2)}, u32[]{:S(2)}) collective-permute-start(f32[128,256]{1,0:T(8,128)S(1)} %collective-permute-done.15.refs_5_), channel_id=1, source_target_pairs={{0,8},{1,9},{2,10},{3,11},{4,12},{5,13},{6,14},{7,15},{8,0},{9,1},... | collective-permute-start | bytes 393224 | tf_op jit(solution)/shard_map/ppermute | solution.py:54
  44.0 1.4 %collective-permute-start.14 = (f32[192,128]{1,0:T(8,128)S(1)}, f32[192,128]{1,0:T(8,128)S(1)}, u32[]{:S(2)}, u32[]{:S(2)}) collective-permute-start(f32[192,128]{1,0:T(8,128)S(1)} %shard_map.54.s_mine), channel_id=1, source_target_pairs={{0,8},{1,9},{2,10},{3,11},{4,12},{5,13},{6,14},{7,15},{8,0},{9,1},... | collective-permute-start | bytes 294920 | tf_op jit(solution)/shard_map/ppermute | solution.py:54

commit v6 on v5

--- a/solution.py
+++ b/solution.py
@@ -155,13 +155,19 @@
     out[...] = jnp.where(same, mine[...], came)
 
 
-def cols_kernel(mine, other, t_ref, high, low):
+def scale_kernel(v_ref, mine, other, t_ref, high, low, v_high, v_low):
     nb = mine.shape[0]
     core = lax.axis_index("row") % 2
     right = split(t_ref[...])
     for k, ref in zip((core, 1 - core), (mine, other)):
         at = pl.ds(k * nb, nb)
         high[at, :], low[at, :] = split(product(split(ref[...]), right, NT))
+    for b in range(v_ref.shape[0] // nb):
+        at = pl.ds(b * nb, nb)
+        block = v_ref[at, :]
+        if b == 0:
+            block = with_unit_top(block)
+        v_high[at, :], v_low[at, :] = split(product(split(block), right, NT))
 
 
 def part_kernel(rows, v_ref, *refs):
@@ -179,17 +185,6 @@
     for out, first in ((keep, core == 0), (give, core == 1)):
         out[pl.ds(0, half), :] = jnp.where(first, whole[:half, :half], whole[half:, half:])
         out[pl.ds(half, half // 2), :] = jnp.where(first, whole[: half // 2, half:], whole[half // 2 : half, half:])
-
-
-def rows_kernel(v_ref, t_ref, high, low):
-    nb = t_ref.shape[0]
-    right = split(t_ref[...])
-    for b in range(v_ref.shape[0] // nb):
-        at = pl.ds(b * nb, nb)
-        block = v_ref[at, :]
-        if b == 0:
-            block = with_unit_top(block)
-        high[at, :], low[at, :] = split(product(split(block), right, NT))
 
 
 def first_kernel(flip, t, rows, a_ref, u_high, u_low, prods, *refs):
@@ -291,7 +286,7 @@
         call(
             join_kernel,
             sds(half, nb),
-            *[move(total, lambda r, c, t=t, s=s: target(r, c, t, s)) for s in range(ys)],
+            *[move(total, lambda r, c, t=t, s=s: target(r, c, t, s)) for s in reversed(range(ys))][::-1],
         )
         for t in range(ratio)
     ]
@@ -304,9 +299,10 @@
         move(block, lambda r, c, s=s: (r ^ (2 * s), c) if r // 2 == c % rows // 2 else None) for s in range(1, ys)
     ]
     near = call(pick_plane_kernel, sds(nb, nb), block, *came)
-    u_high, u_low = call(
-        cols_kernel,
-        (sds(width, nb, dtype=BF16), sds(width, nb, dtype=BF16)),
+    u_high, u_low, v_high, v_low = call(
+        scale_kernel,
+        [sds(width, nb, dtype=BF16)] * 2 + [sds(height, nb, dtype=BF16)] * 2,
+        vecs,
         near,
         move(near, other_core),
         t_factor,
@@ -328,10 +324,6 @@
                 specs=[VMEM] * 4 + [ANY] * len(bases[-1:]),
             )
         )
-    v_high, v_low = call(
-        rows_kernel, (sds(height, nb, dtype=BF16), sds(height, nb, dtype=BF16)), vecs, t_factor
-    )
-
     keep, give = call(
         functools.partial(part_kernel, rows),
         (sds(3 * nb // 4, nb // 2), sds(3 * nb // 4, nb // 2)),
@@ -341,7 +333,7 @@
     )
     share = late_add((), keep, move(give, other_core))
     share = late_add(bases[ratio : ratio + 1], share, *along_y(share))
-    share = late_add((bases[-1], v_high), share, move(share, lambda r, c: (r, c ^ 1)))
+    share = late_add(bases[-1:], share, move(share, lambda r, c: (r, c ^ 1)))
     rest = move(share, other_core)
 
     result = pl.pallas_call(

time: 48.3 us -> 48.3 us (level)
    pallas_call x18 -> x17, Pallas kernels: 6.22 us -> 6.01 us  [call(): pl.pallas_call(kernel, out_shape=outs, in_specs=specs or [VMEM] * len(arg...]
where the time goes in v6:
time: 48.3 us; the launch traced here: 48.2 us
  starting transfers between devices  25.1 us (52%)
  waiting for transfers between devices  14.1 us (29%)
  Pallas kernels  8.8 us (18%)
    ppermute x18, starting transfers between devices, send(): return lax.ppermute(value, AXES, pairs)  25.1 us
    ppermute x18, waiting for transfers between devices, send(): return lax.ppermute(value, AXES, pairs)  14.1 us
    pallas_call x17, Pallas kernels, call(): pl.pallas_call(kernel, out_shape=outs, in_specs=specs or [VMEM] * len(arg...  6.01 us
    pallas_call x1, Pallas kernels, per_device(): pl.pallas_call(functools.partial(last_kernel, places, rows), out_shape=sd...  2.78 us
  transfers between devices with their start and end apart: 18, of which 8 were waited for; matrix products, arithmetic and copies ran while one was open for 0% of the time, Pallas kernels for 7%

profile of v6, /device:TPU:0, one launch (start us, length us, event | category | flops | bytes accessed | tf_op | source)
XLA Modules:
  0.0 48.2 jit_solution(6442047666529035436)
XLA Ops:
  0.0 2.8 %shard_map.37 = (f32[256,256]{1,0:T(8,128)S(1)}, f32[256,256]{1,0:T(8,128)S(1)}) custom-call(f32[4096,128]{1,0:T(8,128)} %bitcast.3, f32[1024,256]{1,0:T(8,128)} %bitcast.8), custom_call_target="tpu_custom_call" | custom-call | tf_op jit(solution)/shard_map/pallas_call | solution.py:37
  2.8 0.5 %collective-permute-start.3 = (f32[256,256]{1,0:T(8,128)S(1)}, f32[256,256]{1,0:T(8,128)S(1)}, u32[]{:S(2)}, u32[]{:S(2)}) collective-permute-start(f32[256,256]{1,0:T(8,128)S(1)} %get-tuple-element.24), channel_id=1, source_target_pairs={{0,8},{1,9},{2,10},{3,11},{4,12},{5,13},{6,14},{7,15},{8,0},{9,1},... | collective-permute-start | bytes 786440 | tf_op jit(solution)/shard_map/ppermute | solution.py:54
  3.3 0.0 copy-done.1
  3.3 0.1 shard_map.38
  3.4 2.0 %collective-permute-start = (f32[256,256]{1,0:T(8,128)S(1)}, f32[256,256]{1,0:T(8,128)S(1)}, u32[]{:S(2)}, u32[]{:S(2)}) collective-permute-start(f32[256,256]{1,0:T(8,128)S(1)} %get-tuple-element.19), channel_id=1, source_target_pairs={{0,8},{4,12},{9,1},{13,5},{18,26},{22,30},{27,19},{31,23}} | collective-permute-start | bytes 786440 | tf_op jit(solution)/shard_map/ppermute | solution.py:54
  5.4 0.0 collective-permute-done.3.came
  5.4 2.0 %collective-permute-start.4 = (f32[128,256]{1,0:T(8,128)S(1)}, f32[128,256]{1,0:T(8,128)S(1)}, u32[]{:S(2)}, u32[]{:S(2)}) collective-permute-start(f32[128,256]{1,0:T(8,128)S(1)} %get-tuple-element.26), channel_id=1, source_target_pairs={{0,16},{1,17},{2,18},{3,19},{4,20},{5,21},{6,22},{7,23},{8,24},{9,... | collective-permute-start | bytes 393224 | tf_op jit(solution)/shard_map/ppermute | solution.py:54
  7.4 0.0 collective-permute-done.came
  7.5 0.0 copy-start.2
  7.5 2.1 %collective-permute-start.1 = (f32[256,256]{1,0:T(8,128)S(1)}, f32[256,256]{1,0:T(8,128)S(1)}, u32[]{:S(2)}, u32[]{:S(2)}) collective-permute-start(f32[256,256]{1,0:T(8,128)S(1)} %shard_map.39.mine), channel_id=1, source_target_pairs={{0,16},{1,17},{4,20},{5,21},{8,24},{9,25},{12,28},{13,29},{18,2},{... | collective-permute-start | bytes 786440 | tf_op jit(solution)/shard_map/ppermute | solution.py:54
  9.6 1.6 %collective-permute-done.4.refs_1_ = f32[128,256]{1,0:T(8,128)S(1)} collective-permute-done((f32[128,256]{1,0:T(8,128)S(1)}, f32[128,256]{1,0:T(8,128)S(1)}, u32[]{:S(2)}, u32[]{:S(2)}) %collective-permute-start.4) | collective-permute-done | bytes 131104 | tf_op jit(solution)/shard_map/ppermute | solution.py:54
  11.3 3.9 %collective-permute-start.9 = (f32[128,256]{1,0:T(8,128)S(1)}, f32[128,256]{1,0:T(8,128)S(1)}, u32[]{:S(2)}, u32[]{:S(2)}) collective-permute-start(f32[128,256]{1,0:T(8,128)S(1)} %shard_map.43.refs_4_), channel_id=1, source_target_pairs={{0,6},{1,14},{2,22},{3,30},{4,2},{5,10},{6,18},{7,26},{8,7},{9,15}... | collective-permute-start | bytes 393224 | tf_op jit(solution)/shard_map/ppermute | solution.py:54
  15.2 0.0 collective-permute-start.8
  15.2 1.9 %collective-permute-start.6 = (f32[128,256]{1,0:T(8,128)S(1)}, f32[128,256]{1,0:T(8,128)S(1)}, u32[]{:S(2)}, u32[]{:S(2)}) collective-permute-start(f32[128,256]{1,0:T(8,128)S(1)} %shard_map.43.refs_4_), channel_id=1, source_target_pairs={{0,2},{1,10},{2,18},{3,26},{4,6},{5,14},{6,22},{7,30},{8,3},{9,11}... | collective-permute-start | bytes 393224 | tf_op jit(solution)/shard_map/ppermute | solution.py:54
  17.1 0.7 %collective-permute-start.5 = (f32[128,256]{1,0:T(8,128)S(1)}, f32[128,256]{1,0:T(8,128)S(1)}, u32[]{:S(2)}, u32[]{:S(2)}) collective-permute-start(f32[128,256]{1,0:T(8,128)S(1)} %shard_map.43.refs_4_), channel_id=1, source_target_pairs={{0,0},{1,8},{2,16},{3,24},{4,4},{5,12},{6,20},{7,28},{8,1},{9,9},{... | collective-permute-start | bytes 393224 | tf_op jit(solution)/shard_map/ppermute | solution.py:54
  17.8 0.0 collective-permute-done.1.refs_0_
  17.8 3.8 %collective-permute-start.2 = (f32[256,256]{1,0:T(8,128)S(1)}, f32[256,256]{1,0:T(8,128)S(1)}, u32[]{:S(2)}, u32[]{:S(2)}) collective-permute-start(f32[256,256]{1,0:T(8,128)S(1)} %shard_map.40.mine), channel_id=1, source_target_pairs={{0,8},{1,9},{2,10},{3,11},{4,12},{5,13},{6,14},{7,15},{8,0},{9,1},... | collective-permute-start | bytes 786440 | tf_op jit(solution)/shard_map/ppermute | solution.py:54
  21.7 2.4 %collective-permute-done.9.refs_1_ = f32[128,256]{1,0:T(8,128)S(1)} collective-permute-done((f32[128,256]{1,0:T(8,128)S(1)}, f32[128,256]{1,0:T(8,128)S(1)}, u32[]{:S(2)}, u32[]{:S(2)}) %collective-permute-start.9) | collective-permute-done | bytes 131104 | tf_op jit(solution)/shard_map/ppermute | solution.py:54
  24.1 2.9 %collective-permute-done.8.refs_0_ = f32[128,256]{1,0:T(8,128)S(1)} collective-permute-done((f32[128,256]{1,0:T(8,128)S(1)}, f32[128,256]{1,0:T(8,128)S(1)}, u32[]{:S(2)}, u32[]{:S(2)}) %collective-permute-start.8) | collective-permute-done | bytes 131104 | tf_op jit(solution)/shard_map/ppermute | solution.py:54
  27.0 0.0 copy-start
  27.1 1.9 %collective-permute-start.10 = (f32[256,256]{1,0:T(8,128)S(1)}, f32[256,256]{1,0:T(8,128)S(1)}, u32[]{:S(2)}, u32[]{:S(2)}) collective-permute-start(f32[256,256]{1,0:T(8,128)S(1)} %shard_map.45.prods.refs_1_), channel_id=1, source_target_pairs={{0,1},{1,0},{2,3},{3,2},{4,5},{5,4},{6,7},{7,6},{8,9},{9,8},{10,11... | collective-permute-start | bytes 786440 | tf_op jit(solution)/shard_map/ppermute | solution.py:54
  29.0 0.0 collective-permute-done.6.refs_1_
  29.0 0.0 collective-permute-done.5.refs_0_
  29.0 0.5 shard_map.50
  29.5 0.1 collective-permute-start.11
  29.6 0.8 %collective-permute-start.7 = (f32[256,256]{1,0:T(8,128)S(1)}, f32[256,256]{1,0:T(8,128)S(1)}, u32[]{:S(2)}, u32[]{:S(2)}) collective-permute-start(f32[256,256]{1,0:T(8,128)S(1)} %shard_map.44.prods.refs_0_), channel_id=1, source_target_pairs={{0,1},{1,0},{2,3},{3,2},{4,5},{5,4},{6,7},{7,6},{8,9},{9,8},{10,11... | collective-permute-start | bytes 786440 | tf_op jit(solution)/shard_map/ppermute | solution.py:54
  30.4 0.5 collective-permute-done.11.refs_1_
  30.9 2.6 %collective-permute-start.12 = (f32[192,128]{1,0:T(8,128)S(1)}, f32[192,128]{1,0:T(8,128)S(1)}, u32[]{:S(2)}, u32[]{:S(2)}) collective-permute-start(f32[192,128]{1,0:T(8,128)S(1)} %shard_map.51.refs_1_), channel_id=1, source_target_pairs={{0,16},{1,17},{2,18},{3,19},{4,20},{5,21},{6,22},{7,23},{8,24},{9,... | collective-permute-start | bytes 294920 | tf_op jit(solution)/shard_map/ppermute | solution.py:54
  33.5 0.1 collective-permute-start.15
  33.5 0.0 collective-permute-done.2.other
  33.5 0.8 %shard_map.41 = (bf16[512,256]{1,0:T(8,128)(2,1)S(1)}, bf16[512,256]{1,0:T(8,128)(2,1)S(1)}, bf16[1024,256]{1,0:T(8,128)(2,1)S(1)}, bf16[1024,256]{1,0:T(8,128)(2,1)S(1)}) custom-call(f32[1024,256]{1,0:T(8,128)S(1)} %bitcast.11, f32[256,256]{1,0:T(8,128)S(1)} %shard_map.40.mine, f32[256,256]{1,0:T(8,128)S(1)} %collective-permute-done.2.other, ...), custom_call_target="tpu_custom_call" | custom-call | tf_op jit(solution)/shard_map/pallas_call | solution.py:37
  34.4 1.9 %collective-permute-done.10.prods = f32[256,256]{1,0:T(8,128)S(1)} collective-permute-done((f32[256,256]{1,0:T(8,128)S(1)}, f32[256,256]{1,0:T(8,128)S(1)}, u32[]{:S(2)}, u32[]{:S(2)}) %collective-permute-start.10) | collective-permute-done | bytes 262176 | tf_op jit(solution)/shard_map/ppermute | solution.py:54
  36.3 0.4 shard_map.46.refs_0_
  36.7 0.4 shard_map.47.refs_0_.refs_1_
  37.1 0.4 shard_map.48.refs_0_.refs_2_
  37.5 0.0 collective-permute-done.12.refs_2_
  37.6 2.0 %collective-permute-start.13 = (f32[192,128]{1,0:T(8,128)S(1)}, f32[192,128]{1,0:T(8,128)S(1)}, u32[]{:S(2)}, u32[]{:S(2)}) collective-permute-start(f32[192,128]{1,0:T(8,128)S(1)} %shard_map.52.refs_1_), channel_id=1, source_target_pairs={{0,1},{1,0},{2,3},{3,2},{4,5},{5,4},{6,7},{7,6},{8,9},{9,8},{10,11... | collective-permute-start | bytes 294920 | tf_op jit(solution)/shard_map/ppermute | solution.py:54
  39.5 0.0 collective-permute-start.16
  39.5 0.0 collective-permute-done.15.refs_5_
  39.5 0.5 %collective-permute-start.17 = (f32[128,256]{1,0:T(8,128)S(1)}, f32[128,256]{1,0:T(8,128)S(1)}, u32[]{:S(2)}, u32[]{:S(2)}) collective-permute-start(f32[128,256]{1,0:T(8,128)S(1)} %collective-permute-done.15.refs_5_), channel_id=1, source_target_pairs={{0,8},{1,9},{2,10},{3,11},{4,12},{5,13},{6,14},{7,15},{8,0},{9,1},... | collective-permute-start | bytes 393224 | tf_op jit(solution)/shard_map/ppermute | solution.py:54
  40.0 1.9 %collective-permute-done.7.prods = f32[256,256]{1,0:T(8,128)S(1)} collective-permute-done((f32[256,256]{1,0:T(8,128)S(1)}, f32[256,256]{1,0:T(8,128)S(1)}, u32[]{:S(2)}, u32[]{:S(2)}) %collective-permute-start.7) | collective-permute-done | bytes 262176 | tf_op jit(solution)/shard_map/ppermute | solution.py:54
  41.9 0.4 shard_map.49.refs_0_.refs_3_
  42.3 1.7 %collective-permute-done.13.refs_2_ = f32[192,128]{1,0:T(8,128)S(1)} collective-permute-done((f32[192,128]{1,0:T(8,128)S(1)}, f32[192,128]{1,0:T(8,128)S(1)}, u32[]{:S(2)}, u32[]{:S(2)}) %collective-permute-start.13) | collective-permute-done | bytes 98336 | tf_op jit(solution)/shard_map/ppermute | solution.py:54
  44.0 0.1 collective-permute-start.14
  44.2 0.0 collective-permute-done.16.refs_6_
  44.2 0.0 collective-permute-done.17.refs_7_
  44.2 1.2 %collective-permute-done.14.s_other = f32[192,128]{1,0:T(8,128)S(1)} collective-permute-done((f32[192,128]{1,0:T(8,128)S(1)}, f32[192,128]{1,0:T(8,128)S(1)}, u32[]{:S(2)}, u32[]{:S(2)}) %collective-permute-start.14) | collective-permute-done | bytes 98336 | tf_op jit(solution)/shard_map/ppermute | solution.py:54
  45.4 2.8 %shard_map.54 = f32[4096,128]{1,0:T(8,128)} custom-call(bf16[1024,256]{1,0:T(8,128)(2,1)S(1)} %get-tuple-element.20.v_high, bf16[1024,256]{1,0:T(8,128)(2,1)S(1)} %get-tuple-element.21.v_low, bf16[512,256]{1,0:T(8,128)(2,1)S(1)} %get-tuple-element.22.u_high, bf16[512,256]{1,0:T(8,128)(2,1)S(1)} %get-tuple-element.23.u_low, f32[192,128]{1,0:T(8,128)S(1)} %shard_map.53.s_mine, ...), custom_call_target="tpu_custom_call" | custom-call | tf_op jit(solution)/shard_map/pallas_call | solution.py:339
  (12 shorter events, 0.2 us)
Async XLA Ops:
  0.0 3.3 %copy-start.1 = (f32[4,1,256,256]{3,2,1,0:T(8,128)S(1)}, f32[4,1,256,256]{3,2,1,0:T(8,128)}, u32[]{:S(2)}) copy-start(f32[4,1,256,256]{3,2,1,0:T(8,128)} %param.4) | copy-start | bytes 3145732
  2.8 2.6 %collective-permute-start.3 = (f32[256,256]{1,0:T(8,128)S(1)}, f32[256,256]{1,0:T(8,128)S(1)}, u32[]{:S(2)}, u32[]{:S(2)}) collective-permute-start(f32[256,256]{1,0:T(8,128)S(1)} %get-tuple-element.24), channel_id=1, source_target_pairs={{0,8},{1,9},{2,10},{3,11},{4,12},{5,13},{6,14},{7,15},{8,0},{9,1},... | collective-permute-start | bytes 786440 | tf_op jit(solution)/shard_map/ppermute | solution.py:54
  3.4 4.1 %collective-permute-start = (f32[256,256]{1,0:T(8,128)S(1)}, f32[256,256]{1,0:T(8,128)S(1)}, u32[]{:S(2)}, u32[]{:S(2)}) collective-permute-start(f32[256,256]{1,0:T(8,128)S(1)} %get-tuple-element.19), channel_id=1, source_target_pairs={{0,8},{4,12},{9,1},{13,5},{18,26},{22,30},{27,19},{31,23}} | collective-permute-start | bytes 786440 | tf_op jit(solution)/shard_map/ppermute | solution.py:54
  5.4 5.8 %collective-permute-start.4 = (f32[128,256]{1,0:T(8,128)S(1)}, f32[128,256]{1,0:T(8,128)S(1)}, u32[]{:S(2)}, u32[]{:S(2)}) collective-permute-start(f32[128,256]{1,0:T(8,128)S(1)} %get-tuple-element.26), channel_id=1, source_target_pairs={{0,16},{1,17},{2,18},{3,19},{4,20},{5,21},{6,22},{7,23},{8,24},{9,... | collective-permute-start | bytes 393224 | tf_op jit(solution)/shard_map/ppermute | solution.py:54
  7.5 26.0 %copy-start.2 = (f32[256,256]{1,0:T(8,128)S(1)}, f32[256,256]{1,0:T(8,128)}, u32[]{:S(2)}) copy-start(f32[256,256]{1,0:T(8,128)} %t_ref.1) | copy-start | bytes 786436
  7.5 10.3 %collective-permute-start.1 = (f32[256,256]{1,0:T(8,128)S(1)}, f32[256,256]{1,0:T(8,128)S(1)}, u32[]{:S(2)}, u32[]{:S(2)}) collective-permute-start(f32[256,256]{1,0:T(8,128)S(1)} %shard_map.39.mine), channel_id=1, source_target_pairs={{0,16},{1,17},{4,20},{5,21},{8,24},{9,25},{12,28},{13,29},{18,2},{... | collective-permute-start | bytes 786440 | tf_op jit(solution)/shard_map/ppermute | solution.py:54
  11.3 12.8 %collective-permute-start.9 = (f32[128,256]{1,0:T(8,128)S(1)}, f32[128,256]{1,0:T(8,128)S(1)}, u32[]{:S(2)}, u32[]{:S(2)}) collective-permute-start(f32[128,256]{1,0:T(8,128)S(1)} %shard_map.43.refs_4_), channel_id=1, source_target_pairs={{0,6},{1,14},{2,22},{3,30},{4,2},{5,10},{6,18},{7,26},{8,7},{9,15}... | collective-permute-start | bytes 393224 | tf_op jit(solution)/shard_map/ppermute | solution.py:54
  15.2 11.8 %collective-permute-start.8 = (f32[128,256]{1,0:T(8,128)S(1)}, f32[128,256]{1,0:T(8,128)S(1)}, u32[]{:S(2)}, u32[]{:S(2)}) collective-permute-start(f32[128,256]{1,0:T(8,128)S(1)} %shard_map.43.refs_4_), channel_id=1, source_target_pairs={{0,4},{1,12},{2,20},{3,28},{4,0},{5,8},{6,16},{7,24},{8,5},{9,13},... | collective-permute-start | bytes 393224 | tf_op jit(solution)/shard_map/ppermute | solution.py:54
  15.2 13.8 %collective-permute-start.6 = (f32[128,256]{1,0:T(8,128)S(1)}, f32[128,256]{1,0:T(8,128)S(1)}, u32[]{:S(2)}, u32[]{:S(2)}) collective-permute-start(f32[128,256]{1,0:T(8,128)S(1)} %shard_map.43.refs_4_), channel_id=1, source_target_pairs={{0,2},{1,10},{2,18},{3,26},{4,6},{5,14},{6,22},{7,30},{8,3},{9,11}... | collective-permute-start | bytes 393224 | tf_op jit(solution)/shard_map/ppermute | solution.py:54
  17.1 11.9 %collective-permute-start.5 = (f32[128,256]{1,0:T(8,128)S(1)}, f32[128,256]{1,0:T(8,128)S(1)}, u32[]{:S(2)}, u32[]{:S(2)}) collective-permute-start(f32[128,256]{1,0:T(8,128)S(1)} %shard_map.43.refs_4_), channel_id=1, source_target_pairs={{0,0},{1,8},{2,16},{3,24},{4,4},{5,12},{6,20},{7,28},{8,1},{9,9},{... | collective-permute-start | bytes 393224 | tf_op jit(solution)/shard_map/ppermute | solution.py:54
  17.8 15.7 %collective-permute-start.2 = (f32[256,256]{1,0:T(8,128)S(1)}, f32[256,256]{1,0:T(8,128)S(1)}, u32[]{:S(2)}, u32[]{:S(2)}) collective-permute-start(f32[256,256]{1,0:T(8,128)S(1)} %shard_map.40.mine), channel_id=1, source_target_pairs={{0,8},{1,9},{2,10},{3,11},{4,12},{5,13},{6,14},{7,15},{8,0},{9,1},... | collective-permute-start | bytes 786440 | tf_op jit(solution)/shard_map/ppermute | solution.py:54
  27.0 9.3 %copy-start = (f32[4,1,256,2,1,256]{5,4,3,2,1,0:T(1,128)S(1)}, f32[4,1,256,2,1,256]{5,4,3,2,1,0:T(1,128)}, u32[]{:S(2)}) copy-start(f32[4,1,256,2,1,256]{5,4,3,2,1,0:T(1,128)} %param.3) | copy-start | bytes 6291460
  27.1 9.2 %collective-permute-start.10 = (f32[256,256]{1,0:T(8,128)S(1)}, f32[256,256]{1,0:T(8,128)S(1)}, u32[]{:S(2)}, u32[]{:S(2)}) collective-permute-start(f32[256,256]{1,0:T(8,128)S(1)} %shard_map.45.prods.refs_1_), channel_id=1, source_target_pairs={{0,1},{1,0},{2,3},{3,2},{4,5},{5,4},{6,7},{7,6},{8,9},{9,8},{10,11... | collective-permute-start | bytes 786440 | tf_op jit(solution)/shard_map/ppermute | solution.py:54
  29.5 1.4 %collective-permute-start.11 = (f32[192,128]{1,0:T(8,128)S(1)}, f32[192,128]{1,0:T(8,128)S(1)}, u32[]{:S(2)}, u32[]{:S(2)}) collective-permute-start(f32[192,128]{1,0:T(8,128)S(1)} %get-tuple-element.28), channel_id=1, source_target_pairs={{0,8},{1,9},{2,10},{3,11},{4,12},{5,13},{6,14},{7,15},{8,0},{9,1},... | collective-permute-start | bytes 294920 | tf_op jit(solution)/shard_map/ppermute | solution.py:54
  29.6 12.3 %collective-permute-start.7 = (f32[256,256]{1,0:T(8,128)S(1)}, f32[256,256]{1,0:T(8,128)S(1)}, u32[]{:S(2)}, u32[]{:S(2)}) collective-permute-start(f32[256,256]{1,0:T(8,128)S(1)} %shard_map.44.prods.refs_0_), channel_id=1, source_target_pairs={{0,1},{1,0},{2,3},{3,2},{4,5},{5,4},{6,7},{7,6},{8,9},{9,8},{10,11... | collective-permute-start | bytes 786440 | tf_op jit(solution)/shard_map/ppermute | solution.py:54
  30.9 6.7 %collective-permute-start.12 = (f32[192,128]{1,0:T(8,128)S(1)}, f32[192,128]{1,0:T(8,128)S(1)}, u32[]{:S(2)}, u32[]{:S(2)}) collective-permute-start(f32[192,128]{1,0:T(8,128)S(1)} %shard_map.51.refs_1_), channel_id=1, source_target_pairs={{0,16},{1,17},{2,18},{3,19},{4,20},{5,21},{6,22},{7,23},{8,24},{9,... | collective-permute-start | bytes 294920 | tf_op jit(solution)/shard_map/ppermute | solution.py:54
  33.5 6.1 %collective-permute-start.15 = (f32[128,256]{1,0:T(8,128)S(1)}, f32[128,256]{1,0:T(8,128)S(1)}, u32[]{:S(2)}, u32[]{:S(2)}) collective-permute-start(f32[128,256]{1,0:T(8,128)S(1)} %shard_map.43.refs_4_), channel_id=1, source_target_pairs={{0,16},{1,17},{2,18},{3,19},{4,20},{5,21},{6,22},{7,23},{8,24},{9,... | collective-permute-start | bytes 393224 | tf_op jit(solution)/shard_map/ppermute | solution.py:54
  37.6 6.4 %collective-permute-start.13 = (f32[192,128]{1,0:T(8,128)S(1)}, f32[192,128]{1,0:T(8,128)S(1)}, u32[]{:S(2)}, u32[]{:S(2)}) collective-permute-start(f32[192,128]{1,0:T(8,128)S(1)} %shard_map.52.refs_1_), channel_id=1, source_target_pairs={{0,1},{1,0},{2,3},{3,2},{4,5},{5,4},{6,7},{7,6},{8,9},{9,8},{10,11... | collective-permute-start | bytes 294920 | tf_op jit(solution)/shard_map/ppermute | solution.py:54
  39.5 4.6 %collective-permute-start.16 = (f32[128,256]{1,0:T(8,128)S(1)}, f32[128,256]{1,0:T(8,128)S(1)}, u32[]{:S(2)}, u32[]{:S(2)}) collective-permute-start(f32[128,256]{1,0:T(8,128)S(1)} %shard_map.43.refs_4_), channel_id=1, source_target_pairs={{0,8},{1,9},{2,10},{3,11},{4,12},{5,13},{6,14},{7,15},{8,0},{9,1},... | collective-permute-start | bytes 393224 | tf_op jit(solution)/shard_map/ppermute | solution.py:54
  39.5 4.6 %collective-permute-start.17 = (f32[128,256]{1,0:T(8,128)S(1)}, f32[128,256]{1,0:T(8,128)S(1)}, u32[]{:S(2)}, u32[]{:S(2)}) collective-permute-start(f32[128,256]{1,0:T(8,128)S(1)} %collective-permute-done.15.refs_5_), channel_id=1, source_target_pairs={{0,8},{1,9},{2,10},{3,11},{4,12},{5,13},{6,14},{7,15},{8,0},{9,1},... | collective-permute-start | bytes 393224 | tf_op jit(solution)/shard_map/ppermute | solution.py:54
  44.0 1.4 %collective-permute-start.14 = (f32[192,128]{1,0:T(8,128)S(1)}, f32[192,128]{1,0:T(8,128)S(1)}, u32[]{:S(2)}, u32[]{:S(2)}) collective-permute-start(f32[192,128]{1,0:T(8,128)S(1)} %shard_map.53.s_mine), channel_id=1, source_target_pairs={{0,8},{1,9},{2,10},{3,11},{4,12},{5,13},{6,14},{7,15},{8,0},{9,1},... | collective-permute-start | bytes 294920 | tf_op jit(solution)/shard_map/ppermute | solution.py:54

commit v7 on v6

--- a/solution.py
+++ b/solution.py
@@ -182,9 +182,13 @@
         block = jnp.where(at == 0, with_unit_top(block), block)
         value = value + product(split(block), split(array[...]), TN)
     whole[...] = value
+    part = half // 2
     for out, first in ((keep, core == 0), (give, core == 1)):
-        out[pl.ds(0, half), :] = jnp.where(first, whole[:half, :half], whole[half:, half:])
-        out[pl.ds(half, half // 2), :] = jnp.where(first, whole[: half // 2, half:], whole[half // 2 : half, half:])
+        diagonal = jnp.where(first, whole[:half, :half], whole[half:, half:])
+        last = diagonal[part:, part:]
+        out[:part] = diagonal[:part]
+        out[part : part + part // 2] = jnp.concatenate([last[: part // 2], last[part // 2 :]], axis=1)
+        out[part + part // 2 :] = jnp.where(first, whole[:part, half:], whole[part:half, half:])
 
 
 def first_kernel(flip, t, rows, a_ref, u_high, u_low, prods, *refs):
@@ -205,11 +209,17 @@
     half = inner.shape[0] // 2
     first = jnp.where(core == 0, s_mine[...], s_other[...])
     second = jnp.where(core == 0, s_other[...], s_mine[...])
-    corner = jnp.concatenate([first[half:], second[half:]], axis=0)
-    inner[:half, :half] = first[:half]
+    part = half // 2
+    split_at = part + part // 2
+    corner = jnp.concatenate([first[split_at:], second[split_at:]], axis=0)
+    for k, share in enumerate((first, second)):
+        last = share[part:split_at]
+        last = jnp.concatenate([last[:, :part], last[:, part:]], axis=0)
+        lower = jnp.concatenate([share[:part, part:].T, last], axis=1)
+        at = pl.ds(k * half, half)
+        inner[at, at] = jnp.concatenate([share[:part], lower], axis=0)
     inner[:half, half:] = corner
     inner[half:, :half] = corner.T
-    inner[half:, half:] = second[:half]
     mixed[...] = product((u_high[...], u_low[...]), split(inner[...]), NT)
     count, ys = prods[0].shape[0], len(prods) // 2
     for k, ref in enumerate(prods):
@@ -326,7 +336,7 @@
         )
     keep, give = call(
         functools.partial(part_kernel, rows),
-        (sds(3 * nb // 4, nb // 2), sds(3 * nb // 4, nb // 2)),
+        (sds(5 * nb // 8, nb // 2), sds(5 * nb // 8, nb // 2)),
         vecs,
         *straight,
         scratch=[pltpu.VMEM((nb, nb), F32)],

time: 48.3 us -> 48.3 us (level)
  no operation moved by 1% of the time
where the time goes in v7:
time: 48.3 us; the launch traced here: 48.1 us
  starting transfers between devices  25.1 us (52%)
  waiting for transfers between devices  13.8 us (29%)
  Pallas kernels  8.98 us (19%)
    ppermute x18, starting transfers between devices, send(): return lax.ppermute(value, AXES, pairs)  25.1 us
    ppermute x18, waiting for transfers between devices, send(): return lax.ppermute(value, AXES, pairs)  13.8 us
    pallas_call x17, Pallas kernels, call(): pl.pallas_call(kernel, out_shape=outs, in_specs=specs or [VMEM] * len(arg...  6.07 us
    pallas_call x1, Pallas kernels, per_device(): pl.pallas_call(functools.partial(last_kernel, places, rows), out_shape=sd...  2.91 us
  transfers between devices with their start and end apart: 18, of which 8 were waited for; matrix products, arithmetic and copies ran while one was open for 0% of the time, Pallas kernels for 7%

profile of v7, /device:TPU:0, one launch (start us, length us, event | category | flops | bytes accessed | tf_op | source)
XLA Modules:
  0.0 48.1 jit_solution(7703529732489243918)
XLA Ops:
  0.0 2.8 %shard_map.37 = (f32[256,256]{1,0:T(8,128)S(1)}, f32[256,256]{1,0:T(8,128)S(1)}) custom-call(f32[4096,128]{1,0:T(8,128)} %bitcast.3, f32[1024,256]{1,0:T(8,128)} %bitcast.8), custom_call_target="tpu_custom_call" | custom-call | tf_op jit(solution)/shard_map/pallas_call | solution.py:37
  2.8 0.5 %collective-permute-start.3 = (f32[256,256]{1,0:T(8,128)S(1)}, f32[256,256]{1,0:T(8,128)S(1)}, u32[]{:S(2)}, u32[]{:S(2)}) collective-permute-start(f32[256,256]{1,0:T(8,128)S(1)} %get-tuple-element.24), channel_id=1, source_target_pairs={{0,8},{1,9},{2,10},{3,11},{4,12},{5,13},{6,14},{7,15},{8,0},{9,1},... | collective-permute-start | bytes 786440 | tf_op jit(solution)/shard_map/ppermute | solution.py:54
  3.3 0.1 shard_map.38
  3.4 2.0 %collective-permute-start = (f32[256,256]{1,0:T(8,128)S(1)}, f32[256,256]{1,0:T(8,128)S(1)}, u32[]{:S(2)}, u32[]{:S(2)}) collective-permute-start(f32[256,256]{1,0:T(8,128)S(1)} %get-tuple-element.19), channel_id=1, source_target_pairs={{0,8},{4,12},{9,1},{13,5},{18,26},{22,30},{27,19},{31,23}} | collective-permute-start | bytes 786440 | tf_op jit(solution)/shard_map/ppermute | solution.py:54
  5.4 0.0 collective-permute-done.3.came
  5.4 2.0 %collective-permute-start.4 = (f32[128,256]{1,0:T(8,128)S(1)}, f32[128,256]{1,0:T(8,128)S(1)}, u32[]{:S(2)}, u32[]{:S(2)}) collective-permute-start(f32[128,256]{1,0:T(8,128)S(1)} %get-tuple-element.26), channel_id=1, source_target_pairs={{0,16},{1,17},{2,18},{3,19},{4,20},{5,21},{6,22},{7,23},{8,24},{9,... | collective-permute-start | bytes 393224 | tf_op jit(solution)/shard_map/ppermute | solution.py:54
  7.4 0.0 collective-permute-done.came
  7.5 0.0 copy-start.2
  7.5 2.1 %collective-permute-start.1 = (f32[256,256]{1,0:T(8,128)S(1)}, f32[256,256]{1,0:T(8,128)S(1)}, u32[]{:S(2)}, u32[]{:S(2)}) collective-permute-start(f32[256,256]{1,0:T(8,128)S(1)} %shard_map.39.mine), channel_id=1, source_target_pairs={{0,16},{1,17},{4,20},{5,21},{8,24},{9,25},{12,28},{13,29},{18,2},{... | collective-permute-start | bytes 786440 | tf_op jit(solution)/shard_map/ppermute | solution.py:54
  9.6 1.6 %collective-permute-done.4.refs_1_ = f32[128,256]{1,0:T(8,128)S(1)} collective-permute-done((f32[128,256]{1,0:T(8,128)S(1)}, f32[128,256]{1,0:T(8,128)S(1)}, u32[]{:S(2)}, u32[]{:S(2)}) %collective-permute-start.4) | collective-permute-done | bytes 131104 | tf_op jit(solution)/shard_map/ppermute | solution.py:54
  11.3 3.9 %collective-permute-start.9 = (f32[128,256]{1,0:T(8,128)S(1)}, f32[128,256]{1,0:T(8,128)S(1)}, u32[]{:S(2)}, u32[]{:S(2)}) collective-permute-start(f32[128,256]{1,0:T(8,128)S(1)} %shard_map.43.refs_4_), channel_id=1, source_target_pairs={{0,6},{1,14},{2,22},{3,30},{4,2},{5,10},{6,18},{7,26},{8,7},{9,15}... | collective-permute-start | bytes 393224 | tf_op jit(solution)/shard_map/ppermute | solution.py:54
  15.2 0.0 collective-permute-start.8
  15.2 1.9 %collective-permute-start.6 = (f32[128,256]{1,0:T(8,128)S(1)}, f32[128,256]{1,0:T(8,128)S(1)}, u32[]{:S(2)}, u32[]{:S(2)}) collective-permute-start(f32[128,256]{1,0:T(8,128)S(1)} %shard_map.43.refs_4_), channel_id=1, source_target_pairs={{0,2},{1,10},{2,18},{3,26},{4,6},{5,14},{6,22},{7,30},{8,3},{9,11}... | collective-permute-start | bytes 393224 | tf_op jit(solution)/shard_map/ppermute | solution.py:54
  17.1 0.7 %collective-permute-start.5 = (f32[128,256]{1,0:T(8,128)S(1)}, f32[128,256]{1,0:T(8,128)S(1)}, u32[]{:S(2)}, u32[]{:S(2)}) collective-permute-start(f32[128,256]{1,0:T(8,128)S(1)} %shard_map.43.refs_4_), channel_id=1, source_target_pairs={{0,0},{1,8},{2,16},{3,24},{4,4},{5,12},{6,20},{7,28},{8,1},{9,9},{... | collective-permute-start | bytes 393224 | tf_op jit(solution)/shard_map/ppermute | solution.py:54
  17.8 0.0 collective-permute-done.1.refs_0_
  17.8 3.8 %collective-permute-start.2 = (f32[256,256]{1,0:T(8,128)S(1)}, f32[256,256]{1,0:T(8,128)S(1)}, u32[]{:S(2)}, u32[]{:S(2)}) collective-permute-start(f32[256,256]{1,0:T(8,128)S(1)} %shard_map.40.mine), channel_id=1, source_target_pairs={{0,8},{1,9},{2,10},{3,11},{4,12},{5,13},{6,14},{7,15},{8,0},{9,1},... | collective-permute-start | bytes 786440 | tf_op jit(solution)/shard_map/ppermute | solution.py:54
  21.7 2.4 %collective-permute-done.9.refs_1_ = f32[128,256]{1,0:T(8,128)S(1)} collective-permute-done((f32[128,256]{1,0:T(8,128)S(1)}, f32[128,256]{1,0:T(8,128)S(1)}, u32[]{:S(2)}, u32[]{:S(2)}) %collective-permute-start.9) | collective-permute-done | bytes 131104 | tf_op jit(solution)/shard_map/ppermute | solution.py:54
  24.1 2.9 %collective-permute-done.8.refs_0_ = f32[128,256]{1,0:T(8,128)S(1)} collective-permute-done((f32[128,256]{1,0:T(8,128)S(1)}, f32[128,256]{1,0:T(8,128)S(1)}, u32[]{:S(2)}, u32[]{:S(2)}) %collective-permute-start.8) | collective-permute-done | bytes 131104 | tf_op jit(solution)/shard_map/ppermute | solution.py:54
  27.0 0.0 copy-start
  27.1 1.9 %collective-permute-start.10 = (f32[256,256]{1,0:T(8,128)S(1)}, f32[256,256]{1,0:T(8,128)S(1)}, u32[]{:S(2)}, u32[]{:S(2)}) collective-permute-start(f32[256,256]{1,0:T(8,128)S(1)} %shard_map.45.prods.refs_1_), channel_id=1, source_target_pairs={{0,1},{1,0},{2,3},{3,2},{4,5},{5,4},{6,7},{7,6},{8,9},{9,8},{10,11... | collective-permute-start | bytes 786440 | tf_op jit(solution)/shard_map/ppermute | solution.py:54
  29.0 0.0 collective-permute-done.6.refs_1_
  29.0 0.0 collective-permute-done.5.refs_0_
  29.0 0.2 collective-permute-start.7
  29.3 0.5 %shard_map.50 = (f32[160,128]{1,0:T(8,128)S(1)}, f32[160,128]{1,0:T(8,128)S(1)}) custom-call(f32[1024,256]{1,0:T(8,128)S(1)} %bitcast.10, f32[256,256]{1,0:T(8,128)S(1)} %shard_map.44.prods.refs_0_, f32[256,256]{1,0:T(8,128)S(1)} %shard_map.45.prods.refs_1_), custom_call_target="tpu_custom_call" | custom-call | tf_op jit(solution)/shard_map/pallas_call | solution.py:37
  29.8 0.4 collective-permute-start.11
  30.3 3.2 %collective-permute-start.15 = (f32[128,256]{1,0:T(8,128)S(1)}, f32[128,256]{1,0:T(8,128)S(1)}, u32[]{:S(2)}, u32[]{:S(2)}) collective-permute-start(f32[128,256]{1,0:T(8,128)S(1)} %shard_map.43.refs_4_), channel_id=1, source_target_pairs={{0,16},{1,17},{2,18},{3,19},{4,20},{5,21},{6,22},{7,23},{8,24},{9,... | collective-permute-start | bytes 393224 | tf_op jit(solution)/shard_map/ppermute | solution.py:54
  33.5 0.0 collective-permute-done.11.refs_1_
  33.5 1.3 %collective-permute-start.12 = (f32[160,128]{1,0:T(8,128)S(1)}, f32[160,128]{1,0:T(8,128)S(1)}, u32[]{:S(2)}, u32[]{:S(2)}) collective-permute-start(f32[160,128]{1,0:T(8,128)S(1)} %shard_map.51.refs_1_), channel_id=1, source_target_pairs={{0,16},{1,17},{2,18},{3,19},{4,20},{5,21},{6,22},{7,23},{8,24},{9,... | collective-permute-start | bytes 245768 | tf_op jit(solution)/shard_map/ppermute | solution.py:54
  34.8 0.0 collective-permute-done.2.other
  34.8 0.0 copy-done.2
  34.8 0.8 %shard_map.41 = (bf16[512,256]{1,0:T(8,128)(2,1)S(1)}, bf16[512,256]{1,0:T(8,128)(2,1)S(1)}, bf16[1024,256]{1,0:T(8,128)(2,1)S(1)}, bf16[1024,256]{1,0:T(8,128)(2,1)S(1)}) custom-call(f32[1024,256]{1,0:T(8,128)S(1)} %bitcast.11, f32[256,256]{1,0:T(8,128)S(1)} %shard_map.40.mine, f32[256,256]{1,0:T(8,128)S(1)} %collective-permute-done.2.other, ...), custom_call_target="tpu_custom_call" | custom-call | tf_op jit(solution)/shard_map/pallas_call | solution.py:37
  35.6 0.7 %collective-permute-done.10.prods = f32[256,256]{1,0:T(8,128)S(1)} collective-permute-done((f32[256,256]{1,0:T(8,128)S(1)}, f32[256,256]{1,0:T(8,128)S(1)}, u32[]{:S(2)}, u32[]{:S(2)}) %collective-permute-start.10) | collective-permute-done | bytes 262176 | tf_op jit(solution)/shard_map/ppermute | solution.py:54
  36.3 0.4 shard_map.46.refs_0_
  36.7 0.4 shard_map.47.refs_0_.refs_1_
  37.1 0.4 shard_map.48.refs_0_.refs_2_
  37.5 1.8 %collective-permute-done.12.refs_2_ = f32[160,128]{1,0:T(8,128)S(1)} collective-permute-done((f32[160,128]{1,0:T(8,128)S(1)}, f32[160,128]{1,0:T(8,128)S(1)}, u32[]{:S(2)}, u32[]{:S(2)}) %collective-permute-start.12) | collective-permute-done | bytes 81952 | tf_op jit(solution)/shard_map/ppermute | solution.py:54
  39.4 0.4 collective-permute-start.13
  39.8 0.0 collective-permute-start.16
  39.8 0.0 collective-permute-done.15.refs_5_
  39.8 0.5 %collective-permute-start.17 = (f32[128,256]{1,0:T(8,128)S(1)}, f32[128,256]{1,0:T(8,128)S(1)}, u32[]{:S(2)}, u32[]{:S(2)}) collective-permute-start(f32[128,256]{1,0:T(8,128)S(1)} %collective-permute-done.15.refs_5_), channel_id=1, source_target_pairs={{0,8},{1,9},{2,10},{3,11},{4,12},{5,13},{6,14},{7,15},{8,0},{9,1},... | collective-permute-start | bytes 393224 | tf_op jit(solution)/shard_map/ppermute | solution.py:54
  40.3 1.6 %collective-permute-done.7.prods = f32[256,256]{1,0:T(8,128)S(1)} collective-permute-done((f32[256,256]{1,0:T(8,128)S(1)}, f32[256,256]{1,0:T(8,128)S(1)}, u32[]{:S(2)}, u32[]{:S(2)}) %collective-permute-start.7) | collective-permute-done | bytes 262176 | tf_op jit(solution)/shard_map/ppermute | solution.py:54
  41.9 0.4 shard_map.49.refs_0_.refs_3_
  42.3 1.6 %collective-permute-done.13.refs_2_ = f32[160,128]{1,0:T(8,128)S(1)} collective-permute-done((f32[160,128]{1,0:T(8,128)S(1)}, f32[160,128]{1,0:T(8,128)S(1)}, u32[]{:S(2)}, u32[]{:S(2)}) %collective-permute-start.13) | collective-permute-done | bytes 81952 | tf_op jit(solution)/shard_map/ppermute | solution.py:54
  43.9 0.1 collective-permute-start.14
  44.0 0.0 collective-permute-done.16.refs_6_
  44.0 0.0 collective-permute-done.17.refs_7_
  44.0 1.2 %collective-permute-done.14.s_other = f32[160,128]{1,0:T(8,128)S(1)} collective-permute-done((f32[160,128]{1,0:T(8,128)S(1)}, f32[160,128]{1,0:T(8,128)S(1)}, u32[]{:S(2)}, u32[]{:S(2)}) %collective-permute-start.14) | collective-permute-done | bytes 81952 | tf_op jit(solution)/shard_map/ppermute | solution.py:54
  45.2 2.9 %shard_map.54 = f32[4096,128]{1,0:T(8,128)} custom-call(bf16[1024,256]{1,0:T(8,128)(2,1)S(1)} %get-tuple-element.20.v_high, bf16[1024,256]{1,0:T(8,128)(2,1)S(1)} %get-tuple-element.21.v_low, bf16[512,256]{1,0:T(8,128)(2,1)S(1)} %get-tuple-element.22.u_high, bf16[512,256]{1,0:T(8,128)(2,1)S(1)} %get-tuple-element.23.u_low, f32[160,128]{1,0:T(8,128)S(1)} %shard_map.53.s_mine, ...), custom_call_target="tpu_custom_call" | custom-call | tf_op jit(solution)/shard_map/pallas_call | solution.py:349
  (12 shorter events, 0.2 us)
Async XLA Ops:
  0.0 3.3 %copy-start.1 = (f32[4,1,256,256]{3,2,1,0:T(8,128)S(1)}, f32[4,1,256,256]{3,2,1,0:T(8,128)}, u32[]{:S(2)}) copy-start(f32[4,1,256,256]{3,2,1,0:T(8,128)} %param.4) | copy-start | bytes 3145732
  2.8 2.6 %collective-permute-start.3 = (f32[256,256]{1,0:T(8,128)S(1)}, f32[256,256]{1,0:T(8,128)S(1)}, u32[]{:S(2)}, u32[]{:S(2)}) collective-permute-start(f32[256,256]{1,0:T(8,128)S(1)} %get-tuple-element.24), channel_id=1, source_target_pairs={{0,8},{1,9},{2,10},{3,11},{4,12},{5,13},{6,14},{7,15},{8,0},{9,1},... | collective-permute-start | bytes 786440 | tf_op jit(solution)/shard_map/ppermute | solution.py:54
  3.4 4.1 %collective-permute-start = (f32[256,256]{1,0:T(8,128)S(1)}, f32[256,256]{1,0:T(8,128)S(1)}, u32[]{:S(2)}, u32[]{:S(2)}) collective-permute-start(f32[256,256]{1,0:T(8,128)S(1)} %get-tuple-element.19), channel_id=1, source_target_pairs={{0,8},{4,12},{9,1},{13,5},{18,26},{22,30},{27,19},{31,23}} | collective-permute-start | bytes 786440 | tf_op jit(solution)/shard_map/ppermute | solution.py:54
  5.4 5.8 %collective-permute-start.4 = (f32[128,256]{1,0:T(8,128)S(1)}, f32[128,256]{1,0:T(8,128)S(1)}, u32[]{:S(2)}, u32[]{:S(2)}) collective-permute-start(f32[128,256]{1,0:T(8,128)S(1)} %get-tuple-element.26), channel_id=1, source_target_pairs={{0,16},{1,17},{2,18},{3,19},{4,20},{5,21},{6,22},{7,23},{8,24},{9,... | collective-permute-start | bytes 393224 | tf_op jit(solution)/shard_map/ppermute | solution.py:54
  7.5 27.3 %copy-start.2 = (f32[256,256]{1,0:T(8,128)S(1)}, f32[256,256]{1,0:T(8,128)}, u32[]{:S(2)}) copy-start(f32[256,256]{1,0:T(8,128)} %t_ref.1) | copy-start | bytes 786436
  7.5 10.3 %collective-permute-start.1 = (f32[256,256]{1,0:T(8,128)S(1)}, f32[256,256]{1,0:T(8,128)S(1)}, u32[]{:S(2)}, u32[]{:S(2)}) collective-permute-start(f32[256,256]{1,0:T(8,128)S(1)} %shard_map.39.mine), channel_id=1, source_target_pairs={{0,16},{1,17},{4,20},{5,21},{8,24},{9,25},{12,28},{13,29},{18,2},{... | collective-permute-start | bytes 786440 | tf_op jit(solution)/shard_map/ppermute | solution.py:54
  11.3 12.8 %collective-permute-start.9 = (f32[128,256]{1,0:T(8,128)S(1)}, f32[128,256]{1,0:T(8,128)S(1)}, u32[]{:S(2)}, u32[]{:S(2)}) collective-permute-start(f32[128,256]{1,0:T(8,128)S(1)} %shard_map.43.refs_4_), channel_id=1, source_target_pairs={{0,6},{1,14},{2,22},{3,30},{4,2},{5,10},{6,18},{7,26},{8,7},{9,15}... | collective-permute-start | bytes 393224 | tf_op jit(solution)/shard_map/ppermute | solution.py:54
  15.2 11.8 %collective-permute-start.8 = (f32[128,256]{1,0:T(8,128)S(1)}, f32[128,256]{1,0:T(8,128)S(1)}, u32[]{:S(2)}, u32[]{:S(2)}) collective-permute-start(f32[128,256]{1,0:T(8,128)S(1)} %shard_map.43.refs_4_), channel_id=1, source_target_pairs={{0,4},{1,12},{2,20},{3,28},{4,0},{5,8},{6,16},{7,24},{8,5},{9,13},... | collective-permute-start | bytes 393224 | tf_op jit(solution)/shard_map/ppermute | solution.py:54
  15.2 13.8 %collective-permute-start.6 = (f32[128,256]{1,0:T(8,128)S(1)}, f32[128,256]{1,0:T(8,128)S(1)}, u32[]{:S(2)}, u32[]{:S(2)}) collective-permute-start(f32[128,256]{1,0:T(8,128)S(1)} %shard_map.43.refs_4_), channel_id=1, source_target_pairs={{0,2},{1,10},{2,18},{3,26},{4,6},{5,14},{6,22},{7,30},{8,3},{9,11}... | collective-permute-start | bytes 393224 | tf_op jit(solution)/shard_map/ppermute | solution.py:54
  17.1 11.9 %collective-permute-start.5 = (f32[128,256]{1,0:T(8,128)S(1)}, f32[128,256]{1,0:T(8,128)S(1)}, u32[]{:S(2)}, u32[]{:S(2)}) collective-permute-start(f32[128,256]{1,0:T(8,128)S(1)} %shard_map.43.refs_4_), channel_id=1, source_target_pairs={{0,0},{1,8},{2,16},{3,24},{4,4},{5,12},{6,20},{7,28},{8,1},{9,9},{... | collective-permute-start | bytes 393224 | tf_op jit(solution)/shard_map/ppermute | solution.py:54
  17.8 16.9 %collective-permute-start.2 = (f32[256,256]{1,0:T(8,128)S(1)}, f32[256,256]{1,0:T(8,128)S(1)}, u32[]{:S(2)}, u32[]{:S(2)}) collective-permute-start(f32[256,256]{1,0:T(8,128)S(1)} %shard_map.40.mine), channel_id=1, source_target_pairs={{0,8},{1,9},{2,10},{3,11},{4,12},{5,13},{6,14},{7,15},{8,0},{9,1},... | collective-permute-start | bytes 786440 | tf_op jit(solution)/shard_map/ppermute | solution.py:54
  27.0 9.3 %copy-start = (f32[4,1,256,2,1,256]{5,4,3,2,1,0:T(1,128)S(1)}, f32[4,1,256,2,1,256]{5,4,3,2,1,0:T(1,128)}, u32[]{:S(2)}) copy-start(f32[4,1,256,2,1,256]{5,4,3,2,1,0:T(1,128)} %param.3) | copy-start | bytes 6291460
  27.1 9.2 %collective-permute-start.10 = (f32[256,256]{1,0:T(8,128)S(1)}, f32[256,256]{1,0:T(8,128)S(1)}, u32[]{:S(2)}, u32[]{:S(2)}) collective-permute-start(f32[256,256]{1,0:T(8,128)S(1)} %shard_map.45.prods.refs_1_), channel_id=1, source_target_pairs={{0,1},{1,0},{2,3},{3,2},{4,5},{5,4},{6,7},{7,6},{8,9},{9,8},{10,11... | collective-permute-start | bytes 786440 | tf_op jit(solution)/shard_map/ppermute | solution.py:54
  29.0 12.9 %collective-permute-start.7 = (f32[256,256]{1,0:T(8,128)S(1)}, f32[256,256]{1,0:T(8,128)S(1)}, u32[]{:S(2)}, u32[]{:S(2)}) collective-permute-start(f32[256,256]{1,0:T(8,128)S(1)} %shard_map.44.prods.refs_0_), channel_id=1, source_target_pairs={{0,1},{1,0},{2,3},{3,2},{4,5},{5,4},{6,7},{7,6},{8,9},{9,8},{10,11... | collective-permute-start | bytes 786440 | tf_op jit(solution)/shard_map/ppermute | solution.py:54
  29.8 3.7 %collective-permute-start.11 = (f32[160,128]{1,0:T(8,128)S(1)}, f32[160,128]{1,0:T(8,128)S(1)}, u32[]{:S(2)}, u32[]{:S(2)}) collective-permute-start(f32[160,128]{1,0:T(8,128)S(1)} %get-tuple-element.28), channel_id=1, source_target_pairs={{0,8},{1,9},{2,10},{3,11},{4,12},{5,13},{6,14},{7,15},{8,0},{9,1},... | collective-permute-start | bytes 245768 | tf_op jit(solution)/shard_map/ppermute | solution.py:54
  30.3 9.5 %collective-permute-start.15 = (f32[128,256]{1,0:T(8,128)S(1)}, f32[128,256]{1,0:T(8,128)S(1)}, u32[]{:S(2)}, u32[]{:S(2)}) collective-permute-start(f32[128,256]{1,0:T(8,128)S(1)} %shard_map.43.refs_4_), channel_id=1, source_target_pairs={{0,16},{1,17},{2,18},{3,19},{4,20},{5,21},{6,22},{7,23},{8,24},{9,... | collective-permute-start | bytes 393224 | tf_op jit(solution)/shard_map/ppermute | solution.py:54
  33.5 5.8 %collective-permute-start.12 = (f32[160,128]{1,0:T(8,128)S(1)}, f32[160,128]{1,0:T(8,128)S(1)}, u32[]{:S(2)}, u32[]{:S(2)}) collective-permute-start(f32[160,128]{1,0:T(8,128)S(1)} %shard_map.51.refs_1_), channel_id=1, source_target_pairs={{0,16},{1,17},{2,18},{3,19},{4,20},{5,21},{6,22},{7,23},{8,24},{9,... | collective-permute-start | bytes 245768 | tf_op jit(solution)/shard_map/ppermute | solution.py:54
  39.4 4.5 %collective-permute-start.13 = (f32[160,128]{1,0:T(8,128)S(1)}, f32[160,128]{1,0:T(8,128)S(1)}, u32[]{:S(2)}, u32[]{:S(2)}) collective-permute-start(f32[160,128]{1,0:T(8,128)S(1)} %shard_map.52.refs_1_), channel_id=1, source_target_pairs={{0,1},{1,0},{2,3},{3,2},{4,5},{5,4},{6,7},{7,6},{8,9},{9,8},{10,11... | collective-permute-start | bytes 245768 | tf_op jit(solution)/shard_map/ppermute | solution.py:54
  39.8 4.2 %collective-permute-start.16 = (f32[128,256]{1,0:T(8,128)S(1)}, f32[128,256]{1,0:T(8,128)S(1)}, u32[]{:S(2)}, u32[]{:S(2)}) collective-permute-start(f32[128,256]{1,0:T(8,128)S(1)} %shard_map.43.refs_4_), channel_id=1, source_target_pairs={{0,8},{1,9},{2,10},{3,11},{4,12},{5,13},{6,14},{7,15},{8,0},{9,1},... | collective-permute-start | bytes 393224 | tf_op jit(solution)/shard_map/ppermute | solution.py:54
  39.8 4.2 %collective-permute-start.17 = (f32[128,256]{1,0:T(8,128)S(1)}, f32[128,256]{1,0:T(8,128)S(1)}, u32[]{:S(2)}, u32[]{:S(2)}) collective-permute-start(f32[128,256]{1,0:T(8,128)S(1)} %collective-permute-done.15.refs_5_), channel_id=1, source_target_pairs={{0,8},{1,9},{2,10},{3,11},{4,12},{5,13},{6,14},{7,15},{8,0},{9,1},... | collective-permute-start | bytes 393224 | tf_op jit(solution)/shard_map/ppermute | solution.py:54
  43.9 1.3 %collective-permute-start.14 = (f32[160,128]{1,0:T(8,128)S(1)}, f32[160,128]{1,0:T(8,128)S(1)}, u32[]{:S(2)}, u32[]{:S(2)}) collective-permute-start(f32[160,128]{1,0:T(8,128)S(1)} %shard_map.53.s_mine), channel_id=1, source_target_pairs={{0,8},{1,9},{2,10},{3,11},{4,12},{5,13},{6,14},{7,15},{8,0},{9,1},... | collective-permute-start | bytes 245768 | tf_op jit(solution)/shard_map/ppermute | solution.py:54

commit v8 on v7

--- a/solution.py
+++ b/solution.py
@@ -342,7 +342,7 @@
         scratch=[pltpu.VMEM((nb, nb), F32)],
     )
     share = late_add((), keep, move(give, other_core))
-    share = late_add(bases[ratio : ratio + 1], share, *along_y(share))
+    share = late_add(bases[:1], share, *along_y(share))
     share = late_add(bases[-1:], share, move(share, lambda r, c: (r, c ^ 1)))
     rest = move(share, other_core)
 

time: 48.3 us -> 48.3 us (level)
  no operation moved by 1% of the time
where the time goes in v8:
time: 48.3 us; the launch traced here: 48.1 us
  starting transfers between devices  25.1 us (52%)
  waiting for transfers between devices  13.9 us (29%)
  Pallas kernels  8.97 us (19%)
    ppermute x18, starting transfers between devices, send(): return lax.ppermute(value, AXES, pairs)  25.1 us
    ppermute x18, waiting for transfers between devices, send(): return lax.ppermute(value, AXES, pairs)  13.9 us
    pallas_call x17, Pallas kernels, call(): pl.pallas_call(kernel, out_shape=outs, in_specs=specs or [VMEM] * len(arg...  6.06 us
    pallas_call x1, Pallas kernels, per_device(): pl.pallas_call(functools.partial(last_kernel, places, rows), out_shape=sd...  2.91 us
  transfers between devices with their start and end apart: 18, of which 8 were waited for; matrix products, arithmetic and copies ran while one was open for 0% of the time, Pallas kernels for 7%

profile of v8, /device:TPU:0, one launch (start us, length us, event | category | flops | bytes accessed | tf_op | source)
XLA Modules:
  0.0 48.1 jit_solution(10940064456321439563)
XLA Ops:
  0.0 2.8 %shard_map.37 = (f32[256,256]{1,0:T(8,128)S(1)}, f32[256,256]{1,0:T(8,128)S(1)}) custom-call(f32[4096,128]{1,0:T(8,128)} %bitcast.3, f32[1024,256]{1,0:T(8,128)} %bitcast.8), custom_call_target="tpu_custom_call" | custom-call | tf_op jit(solution)/shard_map/pallas_call | solution.py:37
  2.8 0.5 %collective-permute-start.3 = (f32[256,256]{1,0:T(8,128)S(1)}, f32[256,256]{1,0:T(8,128)S(1)}, u32[]{:S(2)}, u32[]{:S(2)}) collective-permute-start(f32[256,256]{1,0:T(8,128)S(1)} %get-tuple-element.24), channel_id=1, source_target_pairs={{0,8},{1,9},{2,10},{3,11},{4,12},{5,13},{6,14},{7,15},{8,0},{9,1},... | collective-permute-start | bytes 786440 | tf_op jit(solution)/shard_map/ppermute | solution.py:54
  3.3 0.1 shard_map.38
  3.4 2.0 %collective-permute-start = (f32[256,256]{1,0:T(8,128)S(1)}, f32[256,256]{1,0:T(8,128)S(1)}, u32[]{:S(2)}, u32[]{:S(2)}) collective-permute-start(f32[256,256]{1,0:T(8,128)S(1)} %get-tuple-element.19), channel_id=1, source_target_pairs={{0,8},{4,12},{9,1},{13,5},{18,26},{22,30},{27,19},{31,23}} | collective-permute-start | bytes 786440 | tf_op jit(solution)/shard_map/ppermute | solution.py:54
  5.4 0.0 collective-permute-done.3.came
  5.4 2.0 %collective-permute-start.4 = (f32[128,256]{1,0:T(8,128)S(1)}, f32[128,256]{1,0:T(8,128)S(1)}, u32[]{:S(2)}, u32[]{:S(2)}) collective-permute-start(f32[128,256]{1,0:T(8,128)S(1)} %get-tuple-element.26), channel_id=1, source_target_pairs={{0,16},{1,17},{2,18},{3,19},{4,20},{5,21},{6,22},{7,23},{8,24},{9,... | collective-permute-start | bytes 393224 | tf_op jit(solution)/shard_map/ppermute | solution.py:54
  7.4 0.0 collective-permute-done.came
  7.5 0.0 copy-start.2
  7.5 2.1 %collective-permute-start.1 = (f32[256,256]{1,0:T(8,128)S(1)}, f32[256,256]{1,0:T(8,128)S(1)}, u32[]{:S(2)}, u32[]{:S(2)}) collective-permute-start(f32[256,256]{1,0:T(8,128)S(1)} %shard_map.39.mine), channel_id=1, source_target_pairs={{0,16},{1,17},{4,20},{5,21},{8,24},{9,25},{12,28},{13,29},{18,2},{... | collective-permute-start | bytes 786440 | tf_op jit(solution)/shard_map/ppermute | solution.py:54
  9.6 1.6 %collective-permute-done.4.refs_1_ = f32[128,256]{1,0:T(8,128)S(1)} collective-permute-done((f32[128,256]{1,0:T(8,128)S(1)}, f32[128,256]{1,0:T(8,128)S(1)}, u32[]{:S(2)}, u32[]{:S(2)}) %collective-permute-start.4) | collective-permute-done | bytes 131104 | tf_op jit(solution)/shard_map/ppermute | solution.py:54
  11.3 3.9 %collective-permute-start.9 = (f32[128,256]{1,0:T(8,128)S(1)}, f32[128,256]{1,0:T(8,128)S(1)}, u32[]{:S(2)}, u32[]{:S(2)}) collective-permute-start(f32[128,256]{1,0:T(8,128)S(1)} %shard_map.43.refs_4_), channel_id=1, source_target_pairs={{0,6},{1,14},{2,22},{3,30},{4,2},{5,10},{6,18},{7,26},{8,7},{9,15}... | collective-permute-start | bytes 393224 | tf_op jit(solution)/shard_map/ppermute | solution.py:54
  15.2 0.0 collective-permute-start.8
  15.2 1.9 %collective-permute-start.6 = (f32[128,256]{1,0:T(8,128)S(1)}, f32[128,256]{1,0:T(8,128)S(1)}, u32[]{:S(2)}, u32[]{:S(2)}) collective-permute-start(f32[128,256]{1,0:T(8,128)S(1)} %shard_map.43.refs_4_), channel_id=1, source_target_pairs={{0,2},{1,10},{2,18},{3,26},{4,6},{5,14},{6,22},{7,30},{8,3},{9,11}... | collective-permute-start | bytes 393224 | tf_op jit(solution)/shard_map/ppermute | solution.py:54
  17.1 0.7 %collective-permute-start.5 = (f32[128,256]{1,0:T(8,128)S(1)}, f32[128,256]{1,0:T(8,128)S(1)}, u32[]{:S(2)}, u32[]{:S(2)}) collective-permute-start(f32[128,256]{1,0:T(8,128)S(1)} %shard_map.43.refs_4_), channel_id=1, source_target_pairs={{0,0},{1,8},{2,16},{3,24},{4,4},{5,12},{6,20},{7,28},{8,1},{9,9},{... | collective-permute-start | bytes 393224 | tf_op jit(solution)/shard_map/ppermute | solution.py:54
  17.8 0.0 collective-permute-done.1.refs_0_
  17.8 3.8 %collective-permute-start.2 = (f32[256,256]{1,0:T(8,128)S(1)}, f32[256,256]{1,0:T(8,128)S(1)}, u32[]{:S(2)}, u32[]{:S(2)}) collective-permute-start(f32[256,256]{1,0:T(8,128)S(1)} %shard_map.40.mine), channel_id=1, source_target_pairs={{0,8},{1,9},{2,10},{3,11},{4,12},{5,13},{6,14},{7,15},{8,0},{9,1},... | collective-permute-start | bytes 786440 | tf_op jit(solution)/shard_map/ppermute | solution.py:54
  21.7 2.4 %collective-permute-done.9.refs_1_ = f32[128,256]{1,0:T(8,128)S(1)} collective-permute-done((f32[128,256]{1,0:T(8,128)S(1)}, f32[128,256]{1,0:T(8,128)S(1)}, u32[]{:S(2)}, u32[]{:S(2)}) %collective-permute-start.9) | collective-permute-done | bytes 131104 | tf_op jit(solution)/shard_map/ppermute | solution.py:54
  24.1 2.9 %collective-permute-done.8.refs_0_ = f32[128,256]{1,0:T(8,128)S(1)} collective-permute-done((f32[128,256]{1,0:T(8,128)S(1)}, f32[128,256]{1,0:T(8,128)S(1)}, u32[]{:S(2)}, u32[]{:S(2)}) %collective-permute-start.8) | collective-permute-done | bytes 131104 | tf_op jit(solution)/shard_map/ppermute | solution.py:54
  27.0 0.0 copy-start
  27.1 1.9 %collective-permute-start.10 = (f32[256,256]{1,0:T(8,128)S(1)}, f32[256,256]{1,0:T(8,128)S(1)}, u32[]{:S(2)}, u32[]{:S(2)}) collective-permute-start(f32[256,256]{1,0:T(8,128)S(1)} %shard_map.45.prods.refs_1_), channel_id=1, source_target_pairs={{0,1},{1,0},{2,3},{3,2},{4,5},{5,4},{6,7},{7,6},{8,9},{9,8},{10,11... | collective-permute-start | bytes 786440 | tf_op jit(solution)/shard_map/ppermute | solution.py:54
  29.0 0.0 collective-permute-done.6.refs_1_
  29.0 0.0 collective-permute-done.5.refs_0_
  29.0 0.2 collective-permute-start.7
  29.3 0.5 %shard_map.50 = (f32[160,128]{1,0:T(8,128)S(1)}, f32[160,128]{1,0:T(8,128)S(1)}) custom-call(f32[1024,256]{1,0:T(8,128)S(1)} %bitcast.10, f32[256,256]{1,0:T(8,128)S(1)} %shard_map.44.prods.refs_0_, f32[256,256]{1,0:T(8,128)S(1)} %shard_map.45.prods.refs_1_), custom_call_target="tpu_custom_call" | custom-call | tf_op jit(solution)/shard_map/pallas_call | solution.py:37
  29.8 0.4 collective-permute-start.11
  30.3 3.2 %collective-permute-start.15 = (f32[128,256]{1,0:T(8,128)S(1)}, f32[128,256]{1,0:T(8,128)S(1)}, u32[]{:S(2)}, u32[]{:S(2)}) collective-permute-start(f32[128,256]{1,0:T(8,128)S(1)} %shard_map.43.refs_4_), channel_id=1, source_target_pairs={{0,16},{1,17},{2,18},{3,19},{4,20},{5,21},{6,22},{7,23},{8,24},{9,... | collective-permute-start | bytes 393224 | tf_op jit(solution)/shard_map/ppermute | solution.py:54
  33.5 0.0 collective-permute-done.11.refs_1_
  33.5 1.3 %collective-permute-start.12 = (f32[160,128]{1,0:T(8,128)S(1)}, f32[160,128]{1,0:T(8,128)S(1)}, u32[]{:S(2)}, u32[]{:S(2)}) collective-permute-start(f32[160,128]{1,0:T(8,128)S(1)} %shard_map.51.refs_1_), channel_id=1, source_target_pairs={{0,16},{1,17},{2,18},{3,19},{4,20},{5,21},{6,22},{7,23},{8,24},{9,... | collective-permute-start | bytes 245768 | tf_op jit(solution)/shard_map/ppermute | solution.py:54
  34.8 0.0 collective-permute-done.2.other
  34.8 0.0 copy-done.2
  34.8 0.8 %shard_map.41 = (bf16[512,256]{1,0:T(8,128)(2,1)S(1)}, bf16[512,256]{1,0:T(8,128)(2,1)S(1)}, bf16[1024,256]{1,0:T(8,128)(2,1)S(1)}, bf16[1024,256]{1,0:T(8,128)(2,1)S(1)}) custom-call(f32[1024,256]{1,0:T(8,128)S(1)} %bitcast.11, f32[256,256]{1,0:T(8,128)S(1)} %shard_map.40.mine, f32[256,256]{1,0:T(8,128)S(1)} %collective-permute-done.2.other, ...), custom_call_target="tpu_custom_call" | custom-call | tf_op jit(solution)/shard_map/pallas_call | solution.py:37
  35.6 0.7 %collective-permute-done.10.prods = f32[256,256]{1,0:T(8,128)S(1)} collective-permute-done((f32[256,256]{1,0:T(8,128)S(1)}, f32[256,256]{1,0:T(8,128)S(1)}, u32[]{:S(2)}, u32[]{:S(2)}) %collective-permute-start.10) | collective-permute-done | bytes 262176 | tf_op jit(solution)/shard_map/ppermute | solution.py:54
  36.3 0.4 shard_map.46.refs_0_
  36.7 2.6 %collective-permute-done.12.refs_2_ = f32[160,128]{1,0:T(8,128)S(1)} collective-permute-done((f32[160,128]{1,0:T(8,128)S(1)}, f32[160,128]{1,0:T(8,128)S(1)}, u32[]{:S(2)}, u32[]{:S(2)}) %collective-permute-start.12) | collective-permute-done | bytes 81952 | tf_op jit(solution)/shard_map/ppermute | solution.py:54
  39.4 0.4 collective-permute-start.13
  39.8 0.0 collective-permute-start.16
  39.8 0.0 collective-permute-done.15.refs_5_
  39.8 0.5 %collective-permute-start.17 = (f32[128,256]{1,0:T(8,128)S(1)}, f32[128,256]{1,0:T(8,128)S(1)}, u32[]{:S(2)}, u32[]{:S(2)}) collective-permute-start(f32[128,256]{1,0:T(8,128)S(1)} %collective-permute-done.15.refs_5_), channel_id=1, source_target_pairs={{0,8},{1,9},{2,10},{3,11},{4,12},{5,13},{6,14},{7,15},{8,0},{9,1},... | collective-permute-start | bytes 393224 | tf_op jit(solution)/shard_map/ppermute | solution.py:54
  40.3 0.4 shard_map.47.refs_0_.refs_1_
  40.7 0.4 shard_map.48.refs_0_.refs_2_
  41.1 0.8 %collective-permute-done.7.prods = f32[256,256]{1,0:T(8,128)S(1)} collective-permute-done((f32[256,256]{1,0:T(8,128)S(1)}, f32[256,256]{1,0:T(8,128)S(1)}, u32[]{:S(2)}, u32[]{:S(2)}) %collective-permute-start.7) | collective-permute-done | bytes 262176 | tf_op jit(solution)/shard_map/ppermute | solution.py:54
  41.9 0.4 shard_map.49.refs_0_.refs_3_
  42.3 1.6 %collective-permute-done.13.refs_2_ = f32[160,128]{1,0:T(8,128)S(1)} collective-permute-done((f32[160,128]{1,0:T(8,128)S(1)}, f32[160,128]{1,0:T(8,128)S(1)}, u32[]{:S(2)}, u32[]{:S(2)}) %collective-permute-start.13) | collective-permute-done | bytes 81952 | tf_op jit(solution)/shard_map/ppermute | solution.py:54
  43.9 0.1 collective-permute-start.14
  44.0 0.0 collective-permute-done.16.refs_6_
  44.0 0.0 collective-permute-done.17.refs_7_
  44.0 1.2 %collective-permute-done.14.s_other = f32[160,128]{1,0:T(8,128)S(1)} collective-permute-done((f32[160,128]{1,0:T(8,128)S(1)}, f32[160,128]{1,0:T(8,128)S(1)}, u32[]{:S(2)}, u32[]{:S(2)}) %collective-permute-start.14) | collective-permute-done | bytes 81952 | tf_op jit(solution)/shard_map/ppermute | solution.py:54
  45.2 2.9 %shard_map.54 = f32[4096,128]{1,0:T(8,128)} custom-call(bf16[1024,256]{1,0:T(8,128)(2,1)S(1)} %get-tuple-element.20.v_high, bf16[1024,256]{1,0:T(8,128)(2,1)S(1)} %get-tuple-element.21.v_low, bf16[512,256]{1,0:T(8,128)(2,1)S(1)} %get-tuple-element.22.u_high, bf16[512,256]{1,0:T(8,128)(2,1)S(1)} %get-tuple-element.23.u_low, f32[160,128]{1,0:T(8,128)S(1)} %shard_map.53.s_mine, ...), custom_call_target="tpu_custom_call" | custom-call | tf_op jit(solution)/shard_map/pallas_call | solution.py:349
  (12 shorter events, 0.2 us)
Async XLA Ops:
  0.0 3.3 %copy-start.1 = (f32[4,1,256,256]{3,2,1,0:T(8,128)S(1)}, f32[4,1,256,256]{3,2,1,0:T(8,128)}, u32[]{:S(2)}) copy-start(f32[4,1,256,256]{3,2,1,0:T(8,128)} %param.4) | copy-start | bytes 3145732
  2.8 2.6 %collective-permute-start.3 = (f32[256,256]{1,0:T(8,128)S(1)}, f32[256,256]{1,0:T(8,128)S(1)}, u32[]{:S(2)}, u32[]{:S(2)}) collective-permute-start(f32[256,256]{1,0:T(8,128)S(1)} %get-tuple-element.24), channel_id=1, source_target_pairs={{0,8},{1,9},{2,10},{3,11},{4,12},{5,13},{6,14},{7,15},{8,0},{9,1},... | collective-permute-start | bytes 786440 | tf_op jit(solution)/shard_map/ppermute | solution.py:54
  3.4 4.1 %collective-permute-start = (f32[256,256]{1,0:T(8,128)S(1)}, f32[256,256]{1,0:T(8,128)S(1)}, u32[]{:S(2)}, u32[]{:S(2)}) collective-permute-start(f32[256,256]{1,0:T(8,128)S(1)} %get-tuple-element.19), channel_id=1, source_target_pairs={{0,8},{4,12},{9,1},{13,5},{18,26},{22,30},{27,19},{31,23}} | collective-permute-start | bytes 786440 | tf_op jit(solution)/shard_map/ppermute | solution.py:54
  5.4 5.8 %collective-permute-start.4 = (f32[128,256]{1,0:T(8,128)S(1)}, f32[128,256]{1,0:T(8,128)S(1)}, u32[]{:S(2)}, u32[]{:S(2)}) collective-permute-start(f32[128,256]{1,0:T(8,128)S(1)} %get-tuple-element.26), channel_id=1, source_target_pairs={{0,16},{1,17},{2,18},{3,19},{4,20},{5,21},{6,22},{7,23},{8,24},{9,... | collective-permute-start | bytes 393224 | tf_op jit(solution)/shard_map/ppermute | solution.py:54
  7.5 27.3 %copy-start.2 = (f32[256,256]{1,0:T(8,128)S(1)}, f32[256,256]{1,0:T(8,128)}, u32[]{:S(2)}) copy-start(f32[256,256]{1,0:T(8,128)} %t_ref.1) | copy-start | bytes 786436
  7.5 10.3 %collective-permute-start.1 = (f32[256,256]{1,0:T(8,128)S(1)}, f32[256,256]{1,0:T(8,128)S(1)}, u32[]{:S(2)}, u32[]{:S(2)}) collective-permute-start(f32[256,256]{1,0:T(8,128)S(1)} %shard_map.39.mine), channel_id=1, source_target_pairs={{0,16},{1,17},{4,20},{5,21},{8,24},{9,25},{12,28},{13,29},{18,2},{... | collective-permute-start | bytes 786440 | tf_op jit(solution)/shard_map/ppermute | solution.py:54
  11.3 12.8 %collective-permute-start.9 = (f32[128,256]{1,0:T(8,128)S(1)}, f32[128,256]{1,0:T(8,128)S(1)}, u32[]{:S(2)}, u32[]{:S(2)}) collective-permute-start(f32[128,256]{1,0:T(8,128)S(1)} %shard_map.43.refs_4_), channel_id=1, source_target_pairs={{0,6},{1,14},{2,22},{3,30},{4,2},{5,10},{6,18},{7,26},{8,7},{9,15}... | collective-permute-start | bytes 393224 | tf_op jit(solution)/shard_map/ppermute | solution.py:54
  15.2 11.8 %collective-permute-start.8 = (f32[128,256]{1,0:T(8,128)S(1)}, f32[128,256]{1,0:T(8,128)S(1)}, u32[]{:S(2)}, u32[]{:S(2)}) collective-permute-start(f32[128,256]{1,0:T(8,128)S(1)} %shard_map.43.refs_4_), channel_id=1, source_target_pairs={{0,4},{1,12},{2,20},{3,28},{4,0},{5,8},{6,16},{7,24},{8,5},{9,13},... | collective-permute-start | bytes 393224 | tf_op jit(solution)/shard_map/ppermute | solution.py:54
  15.2 13.8 %collective-permute-start.6 = (f32[128,256]{1,0:T(8,128)S(1)}, f32[128,256]{1,0:T(8,128)S(1)}, u32[]{:S(2)}, u32[]{:S(2)}) collective-permute-start(f32[128,256]{1,0:T(8,128)S(1)} %shard_map.43.refs_4_), channel_id=1, source_target_pairs={{0,2},{1,10},{2,18},{3,26},{4,6},{5,14},{6,22},{7,30},{8,3},{9,11}... | collective-permute-start | bytes 393224 | tf_op jit(solution)/shard_map/ppermute | solution.py:54
  17.1 11.9 %collective-permute-start.5 = (f32[128,256]{1,0:T(8,128)S(1)}, f32[128,256]{1,0:T(8,128)S(1)}, u32[]{:S(2)}, u32[]{:S(2)}) collective-permute-start(f32[128,256]{1,0:T(8,128)S(1)} %shard_map.43.refs_4_), channel_id=1, source_target_pairs={{0,0},{1,8},{2,16},{3,24},{4,4},{5,12},{6,20},{7,28},{8,1},{9,9},{... | collective-permute-start | bytes 393224 | tf_op jit(solution)/shard_map/ppermute | solution.py:54
  17.8 16.9 %collective-permute-start.2 = (f32[256,256]{1,0:T(8,128)S(1)}, f32[256,256]{1,0:T(8,128)S(1)}, u32[]{:S(2)}, u32[]{:S(2)}) collective-permute-start(f32[256,256]{1,0:T(8,128)S(1)} %shard_map.40.mine), channel_id=1, source_target_pairs={{0,8},{1,9},{2,10},{3,11},{4,12},{5,13},{6,14},{7,15},{8,0},{9,1},... | collective-permute-start | bytes 786440 | tf_op jit(solution)/shard_map/ppermute | solution.py:54
  27.0 9.3 %copy-start = (f32[4,1,256,2,1,256]{5,4,3,2,1,0:T(1,128)S(1)}, f32[4,1,256,2,1,256]{5,4,3,2,1,0:T(1,128)}, u32[]{:S(2)}) copy-start(f32[4,1,256,2,1,256]{5,4,3,2,1,0:T(1,128)} %param.3) | copy-start | bytes 6291460
  27.1 9.2 %collective-permute-start.10 = (f32[256,256]{1,0:T(8,128)S(1)}, f32[256,256]{1,0:T(8,128)S(1)}, u32[]{:S(2)}, u32[]{:S(2)}) collective-permute-start(f32[256,256]{1,0:T(8,128)S(1)} %shard_map.45.prods.refs_1_), channel_id=1, source_target_pairs={{0,1},{1,0},{2,3},{3,2},{4,5},{5,4},{6,7},{7,6},{8,9},{9,8},{10,11... | collective-permute-start | bytes 786440 | tf_op jit(solution)/shard_map/ppermute | solution.py:54
  29.0 12.9 %collective-permute-start.7 = (f32[256,256]{1,0:T(8,128)S(1)}, f32[256,256]{1,0:T(8,128)S(1)}, u32[]{:S(2)}, u32[]{:S(2)}) collective-permute-start(f32[256,256]{1,0:T(8,128)S(1)} %shard_map.44.prods.refs_0_), channel_id=1, source_target_pairs={{0,1},{1,0},{2,3},{3,2},{4,5},{5,4},{6,7},{7,6},{8,9},{9,8},{10,11... | collective-permute-start | bytes 786440 | tf_op jit(solution)/shard_map/ppermute | solution.py:54
  29.8 3.7 %collective-permute-start.11 = (f32[160,128]{1,0:T(8,128)S(1)}, f32[160,128]{1,0:T(8,128)S(1)}, u32[]{:S(2)}, u32[]{:S(2)}) collective-permute-start(f32[160,128]{1,0:T(8,128)S(1)} %get-tuple-element.28), channel_id=1, source_target_pairs={{0,8},{1,9},{2,10},{3,11},{4,12},{5,13},{6,14},{7,15},{8,0},{9,1},... | collective-permute-start | bytes 245768 | tf_op jit(solution)/shard_map/ppermute | solution.py:54
  30.3 9.5 %collective-permute-start.15 = (f32[128,256]{1,0:T(8,128)S(1)}, f32[128,256]{1,0:T(8,128)S(1)}, u32[]{:S(2)}, u32[]{:S(2)}) collective-permute-start(f32[128,256]{1,0:T(8,128)S(1)} %shard_map.43.refs_4_), channel_id=1, source_target_pairs={{0,16},{1,17},{2,18},{3,19},{4,20},{5,21},{6,22},{7,23},{8,24},{9,... | collective-permute-start | bytes 393224 | tf_op jit(solution)/shard_map/ppermute | solution.py:54
  33.5 5.8 %collective-permute-start.12 = (f32[160,128]{1,0:T(8,128)S(1)}, f32[160,128]{1,0:T(8,128)S(1)}, u32[]{:S(2)}, u32[]{:S(2)}) collective-permute-start(f32[160,128]{1,0:T(8,128)S(1)} %shard_map.51.refs_1_), channel_id=1, source_target_pairs={{0,16},{1,17},{2,18},{3,19},{4,20},{5,21},{6,22},{7,23},{8,24},{9,... | collective-permute-start | bytes 245768 | tf_op jit(solution)/shard_map/ppermute | solution.py:54
  39.4 4.5 %collective-permute-start.13 = (f32[160,128]{1,0:T(8,128)S(1)}, f32[160,128]{1,0:T(8,128)S(1)}, u32[]{:S(2)}, u32[]{:S(2)}) collective-permute-start(f32[160,128]{1,0:T(8,128)S(1)} %shard_map.52.refs_1_), channel_id=1, source_target_pairs={{0,1},{1,0},{2,3},{3,2},{4,5},{5,4},{6,7},{7,6},{8,9},{9,8},{10,11... | collective-permute-start | bytes 245768 | tf_op jit(solution)/shard_map/ppermute | solution.py:54
  39.8 4.2 %collective-permute-start.16 = (f32[128,256]{1,0:T(8,128)S(1)}, f32[128,256]{1,0:T(8,128)S(1)}, u32[]{:S(2)}, u32[]{:S(2)}) collective-permute-start(f32[128,256]{1,0:T(8,128)S(1)} %shard_map.43.refs_4_), channel_id=1, source_target_pairs={{0,8},{1,9},{2,10},{3,11},{4,12},{5,13},{6,14},{7,15},{8,0},{9,1},... | collective-permute-start | bytes 393224 | tf_op jit(solution)/shard_map/ppermute | solution.py:54
  39.8 4.2 %collective-permute-start.17 = (f32[128,256]{1,0:T(8,128)S(1)}, f32[128,256]{1,0:T(8,128)S(1)}, u32[]{:S(2)}, u32[]{:S(2)}) collective-permute-start(f32[128,256]{1,0:T(8,128)S(1)} %collective-permute-done.15.refs_5_), channel_id=1, source_target_pairs={{0,8},{1,9},{2,10},{3,11},{4,12},{5,13},{6,14},{7,15},{8,0},{9,1},... | collective-permute-start | bytes 393224 | tf_op jit(solution)/shard_map/ppermute | solution.py:54
  43.9 1.3 %collective-permute-start.14 = (f32[160,128]{1,0:T(8,128)S(1)}, f32[160,128]{1,0:T(8,128)S(1)}, u32[]{:S(2)}, u32[]{:S(2)}) collective-permute-start(f32[160,128]{1,0:T(8,128)S(1)} %shard_map.53.s_mine), channel_id=1, source_target_pairs={{0,8},{1,9},{2,10},{3,11},{4,12},{5,13},{6,14},{7,15},{8,0},{9,1},... | collective-permute-start | bytes 245768 | tf_op jit(solution)/shard_map/ppermute | solution.py:54
